TPU v7x, 32 devices: a whole 2x2x4 slice. The times are simulated.
32 devices in a mesh: gy: 4 (over y, x), gz: 4 (over z), col: 2 (over core).
Axes of the slice: x: 2, y: 2, z: 4, core: 2. Of those that a mesh axis runs over, the one named last changes fastest.
Arguments:
- noise: float32 [3, 256, 1024], P(None, 'gz', ('gy', 'col')), may hold values from -6 to 6
- mean_profile: float32 [256], P('gz'), may hold values from 0.4 to 1.2
- lund_diag: float32 [3, 256], P(None, 'gz'), may hold values from 0.05 to 0.3
- lund_off: float32 [3, 256], P(None, 'gz'), may hold values from -0.1 to 0.1
- populations: float32 [19, 4, 256, 1024], P(None, None, 'gz', ('gy', 'col')), may hold values from 0.5 to 1.5
- mask: int32 [4, 256, 1024], P(None, 'gz', ('gy', 'col')), may hold values 0 or 1
Outputs:
- inflow: float32 [3, 256, 1024], P(None, 'gz', ('gy', 'col'))
- populations_next: float32 [19, 4, 256, 1024], P(None, None, 'gz', ('gy', 'col'))
All inputs are finite; a program needn't handle non-finite values. No bound on the sum of `mask` on one device may be relied on, other than what follows from the above.
Results may differ from a plain program's by a relative error of at most 0.0001.
Values sent between devices are 32-bit elements; how exact they have to be, the bound alone decides.
No kernel may reach another device: no remote copies, remote signals or barrier semaphores. Data moves between devices by JAX's collectives and lax.ppermute only.
A program may use at most 128 MiB of HBM per device.

v0:
```python
import math

import jax
import jax.numpy as jnp
import numpy as np
from jax import lax
from jax.experimental import pallas as pl
from jax.experimental.pallas import tpu as pltpu
from jax.sharding import PartitionSpec as P

HW = 64
DIRS = [
    (0, 0, 0),
    (1, 0, 0), (-1, 0, 0), (0, 1, 0), (0, -1, 0), (0, 0, 1), (0, 0, -1),
    (1, 1, 0), (-1, -1, 0), (1, -1, 0), (-1, 1, 0),
    (1, 0, 1), (-1, 0, -1), (1, 0, -1), (-1, 0, 1),
    (0, 1, 1), (0, -1, -1), (0, 1, -1), (0, -1, 1),
]
OPP = [DIRS.index((-a, -b, -c)) for a, b, c in DIRS]
MIRROR_Y = [DIRS.index((a, -b, c)) for a, b, c in DIRS]
MIRROR_Z = [DIRS.index((a, b, -c)) for a, b, c in DIRS]
INLET = 0.05

Z_EDGE = [i for i in range(19) if DIRS[i][2] == 0] + [i for i in range(19) if DIRS[i][2] == 1]
Z_SECOND = [i for i in range(19) if DIRS[i][2] == 1]
Y_EDGE = [i for i in range(19) if DIRS[i][1] == 0] + [i for i in range(19) if DIRS[i][1] == 1]
Y_SECOND = [i for i in range(19) if DIRS[i][1] == 1]

ROW_SOLID = 76
ROW_PARAM = 80
ROW_NOISE = 88
PAD = 8
VMEM_BYTES = 48 * 1024 * 1024


def taps():
    k = np.arange(-HW, HW + 1).astype(np.float64)
    raw = np.exp(-math.pi * k * k / (2.0 * (HW // 2) ** 2))
    return raw / np.sqrt(np.sum(raw * raw))


def band(source, target):
    values = taps()
    offset = np.asarray(source)[:, None] - np.asarray(target)[None, :]
    inside = np.abs(offset) <= HW
    return np.where(inside, values[np.clip(offset + HW, 0, 2 * HW)], 0.0).astype(np.float32)


def moments(g):
    s = {a: g[a] + g[a + 1] for a in range(1, 19, 2)}
    d = {a: g[a] - g[a + 1] for a in range(1, 19, 2)}
    w1, w2 = 1.0 / 18.0, 1.0 / 36.0
    rho = (
        g[0] * (1.0 / 3.0)
        + (s[1] + s[3] + s[5]) * w1
        + ((s[7] + s[9]) + (s[11] + s[13]) + (s[15] + s[17])) * w2
    )
    mx = d[1] * w1 + ((d[7] + d[9]) + (d[11] + d[13])) * w2
    my = d[3] * w1 + ((d[7] - d[9]) + (d[15] + d[17])) * w2
    mz = d[5] * w1 + ((d[11] - d[13]) + (d[15] - d[17])) * w2
    return rho, mx, my, mz


def pair_vector(a, vx, vy, vz):
    total = None
    for c, v in zip(DIRS[a], (vx, vy, vz)):
        if c:
            term = v if c > 0 else -v
            total = term if total is None else (total + v if c > 0 else total - v)
    return total


def collide(g, solid, keep=range(19)):
    rho, mx, my, mz = moments(g)
    inv = 1.0 / rho
    ux, uy, uz = mx * inv, my * inv, mz * inv
    square = mx * ux + my * uy + mz * uz
    base = 1.25 * rho - 1.875 * square
    post = [None] * 19
    if 0 in keep:
        post[0] = jnp.where(solid, g[0], base - 0.25 * g[0])
    for a in range(1, 19, 2):
        if a not in keep and a + 1 not in keep:
            continue
        m = pair_vector(a, mx, my, mz)
        p = pair_vector(a, ux, uy, uz)
        even = base + 5.625 * (m * p)
        odd = 3.75 * m
        if a in keep:
            post[a] = jnp.where(solid, g[a + 1], (even + odd) - 0.25 * g[a])
        if a + 1 in keep:
            post[a + 1] = jnp.where(solid, g[a], (even - odd) - 0.25 * g[a + 1])
    return post


def inlet_state(ux, uy, uz):
    base = 1.0 - 1.5 * (ux * ux + uy * uy + uz * uz)
    out = [base] * 19
    for a in range(1, 19, 2):
        p = pair_vector(a, ux, uy, uz)
        even = base + 4.5 * (p * p)
        odd = 3.0 * p
        out[a] = even + odd
        out[a + 1] = even - odd
    return out


def wall_rows(first_row, height, kz, nz):
    rows = lax.broadcasted_iota(jnp.int32, (8, 128), 0) + first_row
    return ((rows == 0) & (kz == 0)) | ((rows == height - 1) & (kz == nz - 1))


def edge_kernel(nz, pops, mask, noise, mean, diag, off, za, zb, z2, edge):
    height = pops.shape[2]
    kz = lax.axis_index("gz")
    upward = lax.rem(kz, 2) == 0
    for part, row in ((0, 0), (1, height - 8)):
        wall = wall_rows(row, height, kz, nz)
        for x in range(4):
            solid = (mask[x, row : row + 8, :] == 1) | wall
            post = collide([pops[i, x, row : row + 8, :] for i in range(19)], solid)
            for i in range(19):
                edge[i, x, 8 * part : 8 * part + 8, :] = post[i]
            edge[19, x, 8 * part : 8 * part + 8, :] = solid.astype(jnp.float32)

    def put(row, up, down):
        za[row : row + 1, :] = jnp.where(upward, up, down)
        zb[row : row + 1, :] = jnp.where(upward, down, up)

    q = 0
    for i in Z_EDGE:
        for x in range(4):
            put(4 * q + x, edge[i, x, 15:16, :], edge[MIRROR_Z[i], x, 0:1, :])
        q += 1
    for i in Z_SECOND:
        for x in range(4):
            put(4 * q + x, edge[i, x, 14:15, :], edge[MIRROR_Z[i], x, 1:2, :])
        q += 1
    for x in range(4):
        put(4 * q + x, edge[19, x, 15:16, :], edge[19, x, 0:1, :])
    for ref in (za, zb):
        ref[ROW_PARAM : ROW_PARAM + 8, :] = jnp.zeros((8, 128), jnp.float32)
        ref[ROW_PARAM : ROW_PARAM + 1, 0:height] = mean[...]
        ref[ROW_PARAM + 1 : ROW_PARAM + 4, 0:height] = diag[...]
        ref[ROW_PARAM + 4 : ROW_PARAM + 7, 0:height] = off[...]
        for c in range(3):
            ref[ROW_NOISE + height * c : ROW_NOISE + height * (c + 1), :] = noise[c]
    low_half = lax.rem(kz, 4) < 2
    z2[...] = jnp.zeros((16, 128), jnp.float32)
    for c in range(3):
        last = noise[c, height - 1 : height, :]
        first = noise[c, 0:1, :]
        z2[c : c + 1, :] = jnp.where(low_half, last, first)
        z2[8 + c : 9 + c, :] = jnp.where(low_half, first, last)


def column_kernel(
    nz, ny, pops, mask, noise, sent, za, zb, z2c, z2d, bandz,
    post, solidp, ya, yb, linear, meanrow,
    wide, filt,
):
    height = pops.shape[2]
    rows = height + 2 * PAD
    kz = lax.axis_index("gz")
    ky = lax.axis_index("gy") * lax.axis_size("col") + lax.axis_index("col")
    z_even = lax.rem(kz, 2) == 0
    y_even = lax.rem(ky, 2) == 0
    low_half = lax.rem(kz, 4) < 2

    def body(t, carry):
        row = pl.multiple_of(t * 8, 8)
        wall = wall_rows(row, height, kz, nz)
        for x in range(4):
            solid = (mask[x, pl.ds(row, 8), :] == 1) | wall
            p = collide([pops[i, x, pl.ds(row, 8), :] for i in range(19)], solid)
            for i in range(19):
                post[i, x, pl.ds(row + PAD, 8), :] = p[i]
            solidp[x, pl.ds(row + PAD, 8), :] = solid.astype(jnp.float32)
        return carry

    lax.fori_loop(0, height // 8, body, 0)

    def below(row, n=1):
        return jnp.where(z_even, zb[row : row + n, :], za[row : row + n, :])

    def above(row, n=1):
        return jnp.where(z_even, za[row : row + n, :], zb[row : row + n, :])

    top = PAD + height
    q = 0
    for i in Z_EDGE:
        for x in range(4):
            post[i, x, PAD - 1 : PAD, :] = below(4 * q + x)
            post[MIRROR_Z[i], x, top : top + 1, :] = above(4 * q + x)
        q += 1
    for i in Z_SECOND:
        for x in range(4):
            post[i, x, PAD - 2 : PAD - 1, :] = below(4 * q + x)
            post[MIRROR_Z[i], x, top + 1 : top + 2, :] = above(4 * q + x)
        q += 1
    for x in range(4):
        solidp[x, PAD - 1 : PAD, :] = below(4 * q + x)
        solidp[x, top : top + 1, :] = above(4 * q + x)

    lane = lax.broadcasted_iota(jnp.int32, (8, 128), 1)
    own_par = pltpu.roll(sent[ROW_PARAM : ROW_PARAM + 8, :], PAD, 1)
    low_par = pltpu.roll(below(ROW_PARAM, 8), 128 - height + PAD, 1)
    high_par = pltpu.roll(above(ROW_PARAM, 8), height + PAD, 1)
    par = jnp.where(lane < PAD, low_par, jnp.where(lane < top, own_par, high_par))
    par = jnp.where(lane < rows, par, 0.0)
    meanrow[...] = par
    cols = jnp.transpose(jnp.concatenate([par] * 16, axis=0))[0:rows]

    for c in range(3):
        lanes = slice(128 * c, 128 * c + 128)
        wide[0:height, lanes] = below(ROW_NOISE + height * c, height)
        wide[height : 2 * height, lanes] = noise[c]
        wide[2 * height : 3 * height, lanes] = above(ROW_NOISE + height * c, height)
    filt[...] = jnp.dot(
        bandz[...], wide[...], precision=lax.Precision.HIGHEST, preferred_element_type=jnp.float32
    )
    b_end = float(taps()[0])
    far_low = jnp.where(low_half, z2d[8:16, :], z2c[0:8, :])
    far_high = jnp.where(low_half, z2c[0:8, :], z2d[8:16, :])
    for c in range(3):
        lanes = slice(128 * c, 128 * c + 128)
        filt[PAD - 1 : PAD, lanes] += b_end * far_low[c : c + 1, :]
        filt[top : top + 1, lanes] += b_end * far_high[c : c + 1, :]
    f0, f1, f2 = (filt[:, 128 * c : 128 * c + 128] for c in range(3))
    linear[0] = cols[:, 1:2] * f0
    linear[1] = cols[:, 4:5] * f0 + cols[:, 2:3] * f1
    linear[2] = cols[:, 5:6] * f0 + cols[:, 6:7] * f1 + cols[:, 3:4] * f2
    linear[3] = jnp.broadcast_to(cols[:, 0:1], (rows, 128))

    def edges(t, carry):
        row = pl.multiple_of(t * 8, 8)
        right = jnp.zeros((8, 128), jnp.float32)
        left = jnp.zeros((8, 128), jnp.float32)
        k = 0
        for items, depth in ((Y_EDGE, 0), (Y_SECOND, 1)):
            for i in items:
                for x in range(4):
                    vr = post[i, x, pl.ds(row, 8), :]
                    vl = post[MIRROR_Y[i], x, pl.ds(row, 8), :]
                    right = jnp.where(lane == k, pltpu.roll(vr, (k - (127 - depth)) % 128, 1), right)
                    left = jnp.where(lane == k, pltpu.roll(vl, (k - depth) % 128, 1), left)
                    k += 1
        for x in range(4):
            v = solidp[x, pl.ds(row, 8), :]
            right = jnp.where(lane == k, pltpu.roll(v, (k - 127) % 128, 1), right)
            left = jnp.where(lane == k, pltpu.roll(v, k, 1), left)
            k += 1
        for c in range(3):
            v = linear[c, pl.ds(row, 8), :]
            right = jnp.where(lane == k, pltpu.roll(v, (k - 63) % 128, 1), right)
            left = jnp.where(lane == k, pltpu.roll(v, (k - 64) % 128, 1), left)
            k += 1
        ya[pl.ds(row, 8), :] = jnp.where(y_even, right, left)
        yb[pl.ds(row, 8), :] = jnp.where(y_even, left, right)
        return carry

    lax.fori_loop(0, rows // 8, edges, 0)
    half = rows // 2
    lane_h = lax.broadcasted_iota(jnp.int32, (half, 128), 1)
    for c in range(3):
        first, second = linear[c, 0:half, :], linear[c, half:rows, :]
        left = jnp.where(lane_h < 64, first, pltpu.roll(second, 64, 1))
        right = jnp.where(lane_h < 64, pltpu.roll(first, 64, 1), second)
        at = slice(rows + half * c, rows + half * (c + 1))
        ya[at, :] = jnp.where(y_even, right, left)
        yb[at, :] = jnp.where(y_even, left, right)


def final_kernel(
    nz, ny, post, solidp, linear, meanrow, sa, sb, ya, yb, wy, wg,
    inflow, state,
    lhs, flow, post2, strip_l, strip_r, own_l, own_r, sx_l, sx_r, ghosts, ghost_cols, tl, tr,
):
    height = state.shape[2]
    rows = height + 2 * PAD
    half = rows // 2
    top = PAD + height
    kz = lax.axis_index("gz")
    ky = lax.axis_index("gy") * lax.axis_size("col") + lax.axis_index("col")
    y_even = lax.rem(ky, 2) == 0
    lane = lax.broadcasted_iota(jnp.int32, (8, 128), 1)
    sub = lax.broadcasted_iota(jnp.int32, (8, 128), 0)

    tl[0:rows, :] = jnp.where(y_even, yb[0:rows, :], ya[0:rows, :])
    tr[0:rows, :] = jnp.where(y_even, ya[0:rows, :], yb[0:rows, :])
    fill = jnp.zeros((128 - rows, 128), jnp.float32)
    strip_l[...] = jnp.transpose(jnp.concatenate([tl[0:rows, :], fill], axis=0))
    strip_r[...] = jnp.transpose(jnp.concatenate([tr[0:rows, :], fill], axis=0))
    mine_right = jnp.where(y_even, sa[0:rows, :], sb[0:rows, :])
    mine_left = jnp.where(y_even, sb[0:rows, :], sa[0:rows, :])
    own_l[...] = jnp.transpose(jnp.concatenate([mine_left, fill], axis=0))
    own_r[...] = jnp.transpose(jnp.concatenate([mine_right, fill], axis=0))

    lane_h = lax.broadcasted_iota(jnp.int32, (half, 128), 1)
    for c in range(3):
        at = slice(rows + half * c, rows + half * (c + 1))
        a, b = ya[at, :], yb[at, :]
        left, right = jnp.where(y_even, b, a), jnp.where(y_even, a, b)
        lo, hi = slice(rows * c, rows * c + half), slice(rows * c + half, rows * (c + 1))
        lhs[rows * c : rows * (c + 1), 0:128] = linear[c]
        lhs[lo, 128:256] = jnp.where(lane_h < 64, left, 0.0)
        lhs[hi, 128:256] = jnp.where(lane_h < 64, 0.0, left)
        lhs[lo, 256:384] = jnp.where(lane_h < 64, right, 0.0)
        lhs[hi, 256:384] = jnp.where(lane_h < 64, 0.0, right)
    prod = jnp.dot(
        lhs[...], wy[...], precision=lax.Precision.HIGHEST, preferred_element_type=jnp.float32
    )
    flow[...] = prod
    flow[0:rows, :] = prod[0:rows] + linear[3]
    for c in range(3):
        inflow[c] = flow[rows * c + PAD : rows * c + top, :]
    b_end = float(taps()[0])
    ghost_flow = []
    for c in range(3):
        g = lax.dot_general(
            wg[...],
            lhs[rows * c : rows * (c + 1), :],
            (((1,), (1,)), ((), ())),
            precision=lax.Precision.HIGHEST,
            preferred_element_type=jnp.float32,
        )
        g = jnp.concatenate([g, jnp.zeros((8, 128 - rows), jnp.float32)], axis=1)
        at_l = g[0:1, :] + b_end * strip_l[80 + c : 81 + c, :]
        at_r = g[1:2, :] + b_end * strip_r[80 + c : 81 + c, :]
        if c == 0:
            at_l = at_l + meanrow[0:1, :]
            at_r = at_r + meanrow[0:1, :]
        ghost_flow.append((at_l, at_r))

    outside = ((lane < PAD) & (kz == 0)) | ((lane >= top) & (kz == nz - 1))
    ghosts[...] = jnp.zeros((128, 128), jnp.float32)
    for side, (got, own, sx, edge_items) in enumerate(
        ((strip_l, own_l, sx_l, False), (strip_r, own_r, sx_r, True))
    ):
        mirror = (lambda i: MIRROR_Y[i]) if edge_items else (lambda i: i)
        solid = got[76:84, :] > 0.5
        g = [None] * 19
        for i in range(19):
            j = mirror(i)
            cx, cy, cz = DIRS[i]
            if DIRS[j][1] == 0:
                q, src = Y_EDGE.index(j), got
            elif DIRS[j][1] == 1:
                q, src = len(Y_EDGE) + Y_SECOND.index(j), got
            else:
                q, src = Y_EDGE.index(MIRROR_Y[j]), own
            v = src[4 * q : 4 * q + 4, :]
            if cx == 0:
                w = src[4 * q : 4 * q + 8, :]
            else:
                sx[0:1, :] = jnp.zeros((1, 128), jnp.float32)
                sx[1:5, :] = v
                sx[5:6, :] = v[3:4, :]
                w = sx[1 - cx : 9 - cx, :]
            g[i] = w if cz == 0 else pltpu.roll(w, cz % 128, 1)
        us = [INLET * jnp.broadcast_to(ghost_flow[c][side], (8, 128)) for c in range(3)]
        eq = inlet_state(*us)
        put = (sub == 0) & jnp.logical_not(solid)
        g = [jnp.where(put, eq[i], g[i]) for i in range(19)]
        keep = [i for i in range(19) if DIRS[mirror(i)][1] == 1]
        p = collide(g, solid, keep)
        for n, i in enumerate(Y_SECOND):
            value = jnp.where(outside, 0.0, p[mirror(i)])
            at = 32 * side + 4 * n
            ghosts[at : at + 4, :] = value[0:4, :]
    ghost_cols[0:128, :] = jnp.transpose(ghosts[...])

    def gather(src, i, x, row, from_left, from_right):
        cx, cy, cz = DIRS[i]
        sxx = x - cx
        if sxx < 0:
            return jnp.zeros((8, 128), jnp.float32)
        sxx = min(sxx, 3)
        v = src[i, sxx, pl.ds(row - cz, 8), :]
        if cy == 0:
            return v
        v = pltpu.roll(v, cy % 128, 1)
        if cy == 1:
            cols, k = from_left(i, sxx)
            ghost = pltpu.roll(cols[pl.ds(row - cz, 8), :], (-k) % 128, 1)
            return jnp.where(lane == 0, ghost, v)
        cols, k = from_right(i, sxx)
        ghost = pltpu.roll(cols[pl.ds(row - cz, 8), :], (127 - k) % 128, 1)
        return jnp.where(lane == 127, ghost, v)

    def first_left(i, x):
        return tl, 4 * Y_EDGE.index(i) + x

    def first_right(i, x):
        return tr, 4 * Y_EDGE.index(MIRROR_Y[i]) + x

    def second_left(i, x):
        return ghost_cols, 4 * Y_SECOND.index(i) + x

    def second_right(i, x):
        return ghost_cols, 32 + 4 * Y_SECOND.index(MIRROR_Y[i]) + x

    def step_one(row, store_row, outside_rows):
        us = [INLET * flow[pl.ds(rows * c + row, 8), :] for c in range(3)]
        eq = inlet_state(*us)
        for x in range(4):
            solid = solidp[x, pl.ds(row, 8), :] > 0.5
            g = [gather(post, i, x, row, first_left, first_right) for i in range(19)]
            if x == 0:
                g = [jnp.where(solid, g[i], eq[i]) for i in range(19)]
            p = collide(g, solid)
            for i in range(19):
                value = p[i]
                if outside_rows is not None:
                    value = jnp.where(outside_rows, 0.0, value)
                post2[i, x, pl.ds(store_row, 8), :] = value

    step_one(PAD - 1, PAD - 1, (sub == 0) & (kz == 0))
    step_one(top - 7, top - 7, (sub == 7) & (kz == nz - 1))

    def main(t, carry):
        row = pl.multiple_of(t * 8 + PAD, 8)
        step_one(row, row, None)
        return carry

    lax.fori_loop(0, height // 8, main, 0)

    def last(t, carry):
        row = pl.multiple_of(t * 8 + PAD, 8)
        us = [INLET * flow[pl.ds(rows * c + row, 8), :] for c in range(3)]
        eq = inlet_state(*us)
        for x in range(4):
            solid = solidp[x, pl.ds(row, 8), :] > 0.5
            for i in range(19):
                g = gather(post2, i, x, row, second_left, second_right)
                if x == 0:
                    g = jnp.where(solid, g, eq[i])
                state[i, x, pl.ds(row - PAD, 8), :] = g
        return carry

    lax.fori_loop(0, height // 8, last, 0)


def swap_pairs(count, phase, distance=1):
    pairs = []
    for i in range(count):
        block = (i + phase * distance) // distance
        j = i + distance if block % 2 == 0 else i - distance
        if 0 <= j < count:
            pairs.append((i, j))
    return pairs


def ring_pairs(count, phase):
    if phase == 0:
        return [(i, i ^ 1) for i in range(count)]
    return [(i, (((i + 1) % count ^ 1) - 1) % count) for i in range(count)]


def vm(n):
    return [pl.BlockSpec(memory_space=pltpu.VMEM)] * n


def f32(*shape):
    return jax.ShapeDtypeStruct(shape, jnp.float32)


def scratch(*shape):
    return pltpu.VMEM(shape, jnp.float32)


def shards(nz, ny, noise, mean_profile, lund_diag, lund_off, populations, mask):
    height, span = noise.shape[1], noise.shape[2]
    rows = height + 2 * PAD
    params = pltpu.CompilerParams(vmem_limit_bytes=VMEM_BYTES)
    message = ROW_NOISE + 3 * height

    za, zb, z2 = pl.pallas_call(
        lambda *refs: edge_kernel(nz, *refs),
        out_shape=(f32(message, 128), f32(message, 128), f32(16, 128)),
        in_specs=vm(6),
        out_specs=vm(3),
        scratch_shapes=[scratch(20, 4, 16, 128)],
        compiler_params=params,
        name="edge_rows",
    )(populations, mask, noise, mean_profile.reshape(1, height), lund_diag, lund_off)

    ra = lax.ppermute(za, "gz", swap_pairs(nz, 0))
    rb = lax.ppermute(zb, "gz", swap_pairs(nz, 1))
    rc = lax.ppermute(z2, "gz", swap_pairs(nz, 0, 2))
    far = swap_pairs(nz, 1, 2)
    far = [pair for pair in far if abs(pair[0] - pair[1]) == 2]
    rd = lax.ppermute(z2, "gz", far) if far else jnp.zeros_like(z2)

    line = np.arange(rows) - PAD
    used = (line >= -1) & (line <= height)
    bandz = np.where(used[:, None], band(np.arange(-height, 2 * height), line).T, 0.0)
    post, solidp, ya, yb, linear, meanrow = pl.pallas_call(
        lambda *refs: column_kernel(nz, ny, *refs),
        out_shape=(
            f32(19, 4, rows, 128), f32(4, rows, 128), f32(rows + 3 * rows // 2, 128),
            f32(rows + 3 * rows // 2, 128), f32(4, rows, 128), f32(8, 128),
        ),
        in_specs=vm(9),
        out_specs=vm(6),
        scratch_shapes=[scratch(3 * height, 384), scratch(rows, 384)],
        compiler_params=params,
        name="columns",
    )(populations, mask, noise, za, ra, rb, rc, rd, jnp.asarray(bandz, jnp.float32))

    qa = lax.ppermute(ya, ("gy", "col"), ring_pairs(ny, 0))
    qb = lax.ppermute(yb, ("gy", "col"), ring_pairs(ny, 1))

    own = np.arange(span)
    left = np.arange(128) % 64 - 64
    right = np.arange(128) % 64 + span
    source = np.concatenate([own, left, right])
    wy = band(source, own)
    wg = np.zeros((8, 384), np.float32)
    wg[0:2] = band(source, np.array([-1, span])).T
    inflow, state = pl.pallas_call(
        lambda *refs: final_kernel(nz, ny, *refs),
        out_shape=(f32(3, height, span), f32(19, 4, height, span)),
        in_specs=vm(10),
        out_specs=vm(2),
        scratch_shapes=[
            scratch(3 * rows, 384), scratch(3 * rows, 128), scratch(19, 4, rows, 128),
            scratch(128, 128), scratch(128, 128), scratch(128, 128), scratch(128, 128),
            scratch(16, 128), scratch(16, 128), scratch(128, 128), scratch(128, 128),
            scratch(rows, 128), scratch(rows, 128),
        ],
        compiler_params=params,
        name="stream",
    )(post, solidp, linear, meanrow, ya, yb, qa, qb, jnp.asarray(wy), jnp.asarray(wg))
    return inflow, state


def solution(mesh):
    nz = mesh.shape["gz"]
    ny = mesh.shape["gy"] * mesh.shape["col"]
    in_specs = (
        P(None, "gz", ("gy", "col")),
        P("gz"),
        P(None, "gz"),
        P(None, "gz"),
        P(None, None, "gz", ("gy", "col")),
        P(None, "gz", ("gy", "col")),
    )
    out_specs = (P(None, "gz", ("gy", "col")), P(None, None, "gz", ("gy", "col")))

    def body(*args):
        return shards(nz, ny, *args)

    return jax.shard_map(body, mesh=mesh, in_specs=in_specs, out_specs=out_specs, check_vma=False)
```

profile of v0, /device:TPU:0, one launch (start us, length us, event | category | flops | bytes accessed | tf_op | source)
XLA Modules:
  0.0 36.0 jit_solution(15753511766310301498)
XLA Ops:
  0.6 0.0 copy-start
  0.6 1.7 %copy-done = f32[19,4,64,128]{3,2,1,0:T(8,128)S(1)} copy-done((f32[19,4,64,128]{3,2,1,0:T(8,128)S(1)}, f32[19,4,64,128]{3,2,1,0:T(8,128)}, u32[]{:S(2)}) %copy-start) | copy-done | bytes 2490392
  2.3 0.0 copy-start.2
  2.3 0.9 %copy-done.2 = s32[4,64,128]{2,1,0:T(8,128)S(1)} copy-done((s32[4,64,128]{2,1,0:T(8,128)S(1)}, s32[4,64,128]{2,1,0:T(8,128)}, u32[]{:S(2)}) %copy-start.2) | copy-done | bytes 131096
  3.2 0.0 copy-start.3
  3.2 0.9 %copy-done.3 = f32[3,64,128]{2,1,0:T(8,128)S(1)} copy-done((f32[3,64,128]{2,1,0:T(8,128)S(1)}, f32[3,64,128]{2,1,0:T(8,128)}, u32[]{:S(2)}) %copy-start.3) | copy-done | bytes 98328
  4.1 0.0 copy-start.7
  4.1 0.7 %copy-done.7 = f32[3,64]{1,0:T(4,128)S(1)} copy-done((f32[3,64]{1,0:T(4,128)S(1)}, f32[3,64]{1,0:T(4,128)}, u32[]{:S(2)}) %copy-start.7) | copy-done | bytes 792
  4.8 0.0 copy-start.8
  4.8 0.7 %copy-done.8 = f32[3,64]{1,0:T(4,128)S(1)} copy-done((f32[3,64]{1,0:T(4,128)S(1)}, f32[3,64]{1,0:T(4,128)}, u32[]{:S(2)}) %copy-start.8) | copy-done | bytes 792
  5.5 0.0 copy-start.9
  5.5 0.7 %copy-done.9 = f32[64]{0:T(128)S(1)} copy-done((f32[64]{0:T(128)S(1)}, f32[64]{0:T(128)}, u32[]{:S(2)}) %copy-start.9) | copy-done | bytes 280
  6.2 0.0 copy-start.5
  6.2 0.0 copy-start.4
  6.2 0.0 copy-start.6
  6.2 0.3 edge_rows.1
  6.4 0.7 %collective-permute-start.1 = (f32[280,128]{1,0:T(8,128)S(1)}, f32[280,128]{1,0:T(8,128)S(1)}, u32[]{:S(2)}, u32[]{:S(2)}) collective-permute-start(f32[280,128]{1,0:T(8,128)S(1)} %get-tuple-element.12), channel_id=1, source_target_pairs={{2,4},{4,2},{3,5},{5,3},{10,12},{12,10},{11,13},{13,11},{18,20},{2... | collective-permute-start | bytes 430088 | tf_op jit(solution)/shard_map/ppermute | solution.py:489
  7.1 5.9 %collective-permute-start = (f32[280,128]{1,0:T(8,128)S(1)}, f32[280,128]{1,0:T(8,128)S(1)}, u32[]{:S(2)}, u32[]{:S(2)}) collective-permute-start(f32[280,128]{1,0:T(8,128)S(1)} %get-tuple-element.11.refs_3_), channel_id=1, source_target_pairs={{0,2},{2,0},{4,6},{6,4},{1,3},{3,1},{5,7},{7,5},{8,10},{10,8},{12,... | collective-permute-start | bytes 430088 | tf_op jit(solution)/shard_map/ppermute | solution.py:488
  13.0 0.0 collective-permute-start.2
  13.0 4.5 %collective-permute-done.2.refs_6_ = f32[16,128]{1,0:T(8,128)S(1)} collective-permute-done((f32[16,128]{1,0:T(8,128)S(1)}, f32[16,128]{1,0:T(8,128)S(1)}, u32[]{:S(2)}, u32[]{:S(2)}) %collective-permute-start.2) | collective-permute-done | bytes 8224 | tf_op jit(solution)/shard_map/ppermute | solution.py:490
  17.6 0.0 collective-permute-done.1.refs_5_
  17.6 0.0 collective-permute-done.refs_4_
  17.6 0.0 copy-done.5
  17.6 5.5 %columns.1 = (f32[19,4,80,128]{3,2,1,0:T(8,128)}, f32[4,80,128]{2,1,0:T(8,128)S(1)}, f32[200,128]{1,0:T(8,128)S(1)}, f32[200,128]{1,0:T(8,128)S(1)}, f32[4,80,128]{2,1,0:T(8,128)S(1)}, /*index=5*/f32[8,128]{1,0:T(8,128)S(1)}) custom-call(f32[19,4,64,128]{3,2,1,0:T(8,128)S(1)} %copy-done, s32[4,64,128]{2,1,0:T(8,128)S(1)} %copy-done.2, ...), custom_call_target="tpu_custom_call" | custom-call | tf_op jit(solution)/shard_map/columns/pallas_call | solution.py:498
  23.1 0.0 collective-permute-start.3
  23.1 2.6 %collective-permute-start.4 = (f32[200,128]{1,0:T(8,128)S(1)}, f32[200,128]{1,0:T(8,128)S(1)}, u32[]{:S(2)}, u32[]{:S(2)}) collective-permute-start(f32[200,128]{1,0:T(8,128)S(1)} %get-tuple-element.19.refs_5_), channel_id=1, source_target_pairs={{0,25},{1,8},{8,1},{9,16},{16,9},{17,24},{24,17},{25,0},{2,27},{3,... | collective-permute-start | bytes 307208 | tf_op jit(solution)/shard_map/ppermute | solution.py:512
  25.6 0.0 collective-permute-done.3.refs_6_
  25.6 2.8 %collective-permute-done.4.refs_7_ = f32[200,128]{1,0:T(8,128)S(1)} collective-permute-done((f32[200,128]{1,0:T(8,128)S(1)}, f32[200,128]{1,0:T(8,128)S(1)}, u32[]{:S(2)}, u32[]{:S(2)}) %collective-permute-start.4) | collective-permute-done | bytes 102432 | tf_op jit(solution)/shard_map/ppermute | solution.py:512
  28.5 0.0 copy-done.4
  28.5 0.0 copy-done.6
  28.5 0.0 copy-start.1
  28.5 1.9 %copy-done.1 = f32[19,4,80,128]{3,2,1,0:T(8,128)S(1)} copy-done((f32[19,4,80,128]{3,2,1,0:T(8,128)S(1)}, f32[19,4,80,128]{3,2,1,0:T(8,128)}, u32[]{:S(2)}) %copy-start.1) | copy-done | bytes 3112984
  30.3 5.6 %stream.1 = (f32[3,64,128]{2,1,0:T(8,128)}, f32[19,4,64,128]{3,2,1,0:T(8,128)}) custom-call(f32[19,4,80,128]{3,2,1,0:T(8,128)S(1)} %copy-done.1, f32[4,80,128]{2,1,0:T(8,128)S(1)} %get-tuple-element.15.refs_1_, f32[4,80,128]{2,1,0:T(8,128)S(1)} %get-tuple-element.16.refs_2_, f32[8,128]{1,0:T(8,128)S(1)} %get-tuple-element.17.refs_3_, ...), custom_call_target="tpu_custom_call" | custom-call | tf_op jit(solution)/shard_map/stream/pallas_call | solution.py:521
  (1 shorter events, 0.0 us)
Async XLA Ops:
  0.6 1.7 %copy-start = (f32[19,4,64,128]{3,2,1,0:T(8,128)S(1)}, f32[19,4,64,128]{3,2,1,0:T(8,128)}, u32[]{:S(2)}) copy-start(f32[19,4,64,128]{3,2,1,0:T(8,128)} %refs_0_.3) | copy-start | bytes 7471108
  2.3 0.9 %copy-start.2 = (s32[4,64,128]{2,1,0:T(8,128)S(1)}, s32[4,64,128]{2,1,0:T(8,128)}, u32[]{:S(2)}) copy-start(s32[4,64,128]{2,1,0:T(8,128)} %refs_1_.3) | copy-start | bytes 393220
  3.2 0.9 %copy-start.3 = (f32[3,64,128]{2,1,0:T(8,128)S(1)}, f32[3,64,128]{2,1,0:T(8,128)}, u32[]{:S(2)}) copy-start(f32[3,64,128]{2,1,0:T(8,128)} %refs_2_.3) | copy-start | bytes 294916
  4.1 0.7 %copy-start.7 = (f32[3,64]{1,0:T(4,128)S(1)}, f32[3,64]{1,0:T(4,128)}, u32[]{:S(2)}) copy-start(f32[3,64]{1,0:T(4,128)} %refs_4_.1) | copy-start | bytes 2308
  4.8 0.7 %copy-start.8 = (f32[3,64]{1,0:T(4,128)S(1)}, f32[3,64]{1,0:T(4,128)}, u32[]{:S(2)}) copy-start(f32[3,64]{1,0:T(4,128)} %refs_5_.1) | copy-start | bytes 2308
  5.5 0.7 %copy-start.9 = (f32[64]{0:T(128)S(1)}, f32[64]{0:T(128)}, u32[]{:S(2)}) copy-start(f32[64]{0:T(128)} %param.10) | copy-start | bytes 772
  6.2 11.4 %copy-start.5 = (f32[80,192]{1,0:T(8,128)S(1)}, f32[80,192]{1,0:T(8,128)}, u32[]{:S(2)}) copy-start(f32[80,192]{1,0:T(8,128)} %constant.8.clone.refs_8_) | copy-start | bytes 184324
  6.2 22.3 %copy-start.4 = (f32[384,128]{1,0:T(8,128)S(1)}, f32[384,128]{1,0:T(8,128)}, u32[]{:S(2)}) copy-start(f32[384,128]{1,0:T(8,128)} %constant.9.clone.refs_8_) | copy-start | bytes 589828
  6.2 22.3 %copy-start.6 = (f32[8,384]{1,0:T(8,128)S(1)}, f32[8,384]{1,0:T(8,128)}, u32[]{:S(2)}) copy-start(f32[8,384]{1,0:T(8,128)} %constant.10.clone.refs_9_) | copy-start | bytes 36868
  6.4 11.1 %collective-permute-start.1 = (f32[280,128]{1,0:T(8,128)S(1)}, f32[280,128]{1,0:T(8,128)S(1)}, u32[]{:S(2)}, u32[]{:S(2)}) collective-permute-start(f32[280,128]{1,0:T(8,128)S(1)} %get-tuple-element.12), channel_id=1, source_target_pairs={{2,4},{4,2},{3,5},{5,3},{10,12},{12,10},{11,13},{13,11},{18,20},{2... | collective-permute-start | bytes 430088 | tf_op jit(solution)/shard_map/ppermute | solution.py:489
  7.1 10.5 %collective-permute-start = (f32[280,128]{1,0:T(8,128)S(1)}, f32[280,128]{1,0:T(8,128)S(1)}, u32[]{:S(2)}, u32[]{:S(2)}) collective-permute-start(f32[280,128]{1,0:T(8,128)S(1)} %get-tuple-element.11.refs_3_), channel_id=1, source_target_pairs={{0,2},{2,0},{4,6},{6,4},{1,3},{3,1},{5,7},{7,5},{8,10},{10,8},{12,... | collective-permute-start | bytes 430088 | tf_op jit(solution)/shard_map/ppermute | solution.py:488
  13.0 4.5 %collective-permute-start.2 = (f32[16,128]{1,0:T(8,128)S(1)}, f32[16,128]{1,0:T(8,128)S(1)}, u32[]{:S(2)}, u32[]{:S(2)}) collective-permute-start(f32[16,128]{1,0:T(8,128)S(1)} %get-tuple-element.13), channel_id=1, source_target_pairs={{0,4},{2,6},{4,0},{6,2},{1,5},{3,7},{5,1},{7,3},{8,12},{10,14},{12... | collective-permute-start | bytes 24584 | tf_op jit(solution)/shard_map/ppermute | solution.py:490
  23.1 2.6 %collective-permute-start.3 = (f32[200,128]{1,0:T(8,128)S(1)}, f32[200,128]{1,0:T(8,128)S(1)}, u32[]{:S(2)}, u32[]{:S(2)}) collective-permute-start(f32[200,128]{1,0:T(8,128)S(1)} %get-tuple-element.18.refs_4_), channel_id=1, source_target_pairs={{0,1},{1,0},{8,9},{9,8},{16,17},{17,16},{24,25},{25,24},{2,3},{3,2... | collective-permute-start | bytes 307208 | tf_op jit(solution)/shard_map/ppermute | solution.py:511
  23.1 5.4 %collective-permute-start.4 = (f32[200,128]{1,0:T(8,128)S(1)}, f32[200,128]{1,0:T(8,128)S(1)}, u32[]{:S(2)}, u32[]{:S(2)}) collective-permute-start(f32[200,128]{1,0:T(8,128)S(1)} %get-tuple-element.19.refs_5_), channel_id=1, source_target_pairs={{0,25},{1,8},{8,1},{9,16},{16,9},{17,24},{24,17},{25,0},{2,27},{3,... | collective-permute-start | bytes 307208 | tf_op jit(solution)/shard_map/ppermute | solution.py:512
  28.5 1.9 %copy-start.1 = (f32[19,4,80,128]{3,2,1,0:T(8,128)S(1)}, f32[19,4,80,128]{3,2,1,0:T(8,128)}, u32[]{:S(2)}) copy-start(f32[19,4,80,128]{3,2,1,0:T(8,128)} %get-tuple-element.14.refs_0_) | copy-start | bytes 9338884
where the time goes:
time: 36.3 us; the launch traced here: 36 us
  Pallas kernels  11.4 us (31%)
  starting transfers between devices  9.14 us (25%)
  local copies, waits for them, and re-layouts  7.4 us (20%)
  waiting for transfers between devices  7.37 us (20%)
  between operations  0.68 us (2%)
    unnamed x20, local copies, waits for them, and re-layouts  7.4 us
    ppermute x1, starting transfers between devices, shards(): ra = lax.ppermute(za, 'gz', swap_pairs(nz, 0))  5.9 us
    pallas_call x1, Pallas kernels, shards(): pl.pallas_call(lambda *refs: final_kernel(nz, ny, *refs), out_shape=(f32(...  5.62 us
    pallas_call x1, Pallas kernels, shards(): pl.pallas_call(lambda *refs: column_kernel(nz, ny, *refs), out_shape=(f32...  5.48 us
    ppermute x1, waiting for transfers between devices, shards(): rc = lax.ppermute(z2, 'gz', swap_pairs(nz, 0, 2))  4.55 us
    ppermute x1, waiting for transfers between devices, shards(): qb = lax.ppermute(yb, ('gy', 'col'), ring_pairs(ny, 1))  2.81 us
    ppermute x1, starting transfers between devices, shards(): qb = lax.ppermute(yb, ('gy', 'col'), ring_pairs(ny, 1))  2.56 us
  transfers between devices with their start and end apart: 5, of which 2 were waited for; matrix products, arithmetic and copies ran while one was open for 0% of the time, Pallas kernels for 0%

commit v1 on v0

--- a/solution.py
+++ b/solution.py
@@ -30,7 +30,6 @@
 ROW_PARAM = 80
 ROW_NOISE = 88
 PAD = 8
-VMEM_BYTES = 48 * 1024 * 1024
 
 
 def taps():
@@ -110,18 +109,40 @@
     return ((rows == 0) & (kz == 0)) | ((rows == height - 1) & (kz == nz - 1))
 
 
-def edge_kernel(nz, pops, mask, noise, mean, diag, off, za, zb, z2, edge):
+def edge_kernel(
+    nz, pops, mask, noise, mean, diag, off, za, zb, z2, raw, flags, mean_v, diag_v, off_v, edge, sems
+):
     height = pops.shape[2]
     kz = lax.axis_index("gz")
     upward = lax.rem(kz, 2) == 0
+    upper = pl.ds(height - 8, 8)
+    copies = [
+        (pops.at[:, :, 0:8, :], raw.at[:, :, 0:8, :]),
+        (pops.at[:, :, upper, :], raw.at[:, :, 8:16, :]),
+        (mask.at[:, 0:8, :], flags.at[:, 0:8, :]),
+        (mask.at[:, upper, :], flags.at[:, 8:16, :]),
+        (mean, mean_v),
+        (diag, diag_v),
+        (off, off_v),
+    ]
+    for c in range(3):
+        at = slice(ROW_NOISE + height * c, ROW_NOISE + height * (c + 1))
+        copies.append((noise.at[c], za.at[at, :]))
+        copies.append((noise.at[c], zb.at[at, :]))
+    copies = [pltpu.make_async_copy(src, dst, sems.at[n]) for n, (src, dst) in enumerate(copies)]
+    for copy in copies:
+        copy.start()
+    for copy in copies[:4]:
+        copy.wait()
     for part, row in ((0, 0), (1, height - 8)):
         wall = wall_rows(row, height, kz, nz)
+        at = slice(8 * part, 8 * part + 8)
         for x in range(4):
-            solid = (mask[x, row : row + 8, :] == 1) | wall
-            post = collide([pops[i, x, row : row + 8, :] for i in range(19)], solid)
+            solid = (flags[x, at, :] == 1) | wall
+            post = collide([raw[i, x, at, :] for i in range(19)], solid)
             for i in range(19):
-                edge[i, x, 8 * part : 8 * part + 8, :] = post[i]
-            edge[19, x, 8 * part : 8 * part + 8, :] = solid.astype(jnp.float32)
+                edge[i, x, at, :] = post[i]
+            edge[19, x, at, :] = solid.astype(jnp.float32)
 
     def put(row, up, down):
         za[row : row + 1, :] = jnp.where(upward, up, down)
@@ -138,47 +159,79 @@
         q += 1
     for x in range(4):
         put(4 * q + x, edge[19, x, 15:16, :], edge[19, x, 0:1, :])
+    for copy in copies[4:]:
+        copy.wait()
     for ref in (za, zb):
         ref[ROW_PARAM : ROW_PARAM + 8, :] = jnp.zeros((8, 128), jnp.float32)
-        ref[ROW_PARAM : ROW_PARAM + 1, 0:height] = mean[...]
-        ref[ROW_PARAM + 1 : ROW_PARAM + 4, 0:height] = diag[...]
-        ref[ROW_PARAM + 4 : ROW_PARAM + 7, 0:height] = off[...]
-        for c in range(3):
-            ref[ROW_NOISE + height * c : ROW_NOISE + height * (c + 1), :] = noise[c]
+        ref[ROW_PARAM : ROW_PARAM + 1, 0:height] = mean_v[...]
+        ref[ROW_PARAM + 1 : ROW_PARAM + 4, 0:height] = diag_v[...]
+        ref[ROW_PARAM + 4 : ROW_PARAM + 7, 0:height] = off_v[...]
     low_half = lax.rem(kz, 4) < 2
     z2[...] = jnp.zeros((16, 128), jnp.float32)
     for c in range(3):
-        last = noise[c, height - 1 : height, :]
-        first = noise[c, 0:1, :]
+        base = ROW_NOISE + height * c
+        last = za[base + height - 1 : base + height, :]
+        first = za[base : base + 1, :]
         z2[c : c + 1, :] = jnp.where(low_half, last, first)
         z2[8 + c : 9 + c, :] = jnp.where(low_half, first, last)
 
 
+def pick(lane, k, value, column, into):
+    return jnp.where(lane == k, pltpu.roll(value, (k - column) % 128, 1), into)
+
+
+def bulk_kernel(nz, pops, mask, post, solidp, right_cols, left_cols, raw, flags, sems):
+    height = pops.shape[2]
+    kz = lax.axis_index("gz")
+    lane = lax.broadcasted_iota(jnp.int32, (8, 128), 1)
+    copies = [pltpu.make_async_copy(mask, flags, sems.at[4])]
+    copies += [
+        pltpu.make_async_copy(pops.at[:, x], raw.at[:, x], sems.at[x]) for x in range(4)
+    ]
+    for copy in copies:
+        copy.start()
+    copies[0].wait()
+    for x in range(4):
+        copies[1 + x].wait()
+
+        def body(t, carry):
+            row = pl.multiple_of(t * 8, 8)
+            out = pl.ds(row + PAD, 8)
+            solid = (flags[x, pl.ds(row, 8), :] == 1) | wall_rows(row, height, kz, nz)
+            p = collide([raw[i, x, pl.ds(row, 8), :] for i in range(19)], solid)
+            for i in range(19):
+                post[i, x, out, :] = p[i]
+            flag = solid.astype(jnp.float32)
+            solidp[x, out, :] = flag
+            if x == 0:
+                right = left = jnp.zeros((8, 128), jnp.float32)
+            else:
+                right, left = right_cols[out, :], left_cols[out, :]
+            q = 0
+            for items, depth in ((Y_EDGE, 0), (Y_SECOND, 1)):
+                for i in items:
+                    right = pick(lane, 4 * q + x, p[i], 127 - depth, right)
+                    left = pick(lane, 4 * q + x, p[MIRROR_Y[i]], depth, left)
+                    q += 1
+            right_cols[out, :] = pick(lane, 4 * q + x, flag, 127, right)
+            left_cols[out, :] = pick(lane, 4 * q + x, flag, 0, left)
+            return carry
+
+        lax.fori_loop(0, height // 8, body, 0)
+
+
 def column_kernel(
-    nz, ny, pops, mask, noise, sent, za, zb, z2c, z2d, bandz,
+    nz, post_in, solid_in, right_in, left_in, sent, za, zb, z2c, z2d, bandz,
     post, solidp, ya, yb, linear, meanrow,
     wide, filt,
 ):
-    height = pops.shape[2]
+    height = post.shape[2] - 2 * PAD
     rows = height + 2 * PAD
     kz = lax.axis_index("gz")
     ky = lax.axis_index("gy") * lax.axis_size("col") + lax.axis_index("col")
     z_even = lax.rem(kz, 2) == 0
     y_even = lax.rem(ky, 2) == 0
     low_half = lax.rem(kz, 4) < 2
-
-    def body(t, carry):
-        row = pl.multiple_of(t * 8, 8)
-        wall = wall_rows(row, height, kz, nz)
-        for x in range(4):
-            solid = (mask[x, pl.ds(row, 8), :] == 1) | wall
-            p = collide([pops[i, x, pl.ds(row, 8), :] for i in range(19)], solid)
-            for i in range(19):
-                post[i, x, pl.ds(row + PAD, 8), :] = p[i]
-            solidp[x, pl.ds(row + PAD, 8), :] = solid.astype(jnp.float32)
-        return carry
-
-    lax.fori_loop(0, height // 8, body, 0)
 
     def below(row, n=1):
         return jnp.where(z_even, zb[row : row + n, :], za[row : row + n, :])
@@ -213,8 +266,9 @@
 
     for c in range(3):
         lanes = slice(128 * c, 128 * c + 128)
+        at = slice(ROW_NOISE + height * c, ROW_NOISE + height * (c + 1))
         wide[0:height, lanes] = below(ROW_NOISE + height * c, height)
-        wide[height : 2 * height, lanes] = noise[c]
+        wide[height : 2 * height, lanes] = sent[at, :]
         wide[2 * height : 3 * height, lanes] = above(ROW_NOISE + height * c, height)
     filt[...] = jnp.dot(
         bandz[...], wide[...], precision=lax.Precision.HIGHEST, preferred_element_type=jnp.float32
@@ -232,34 +286,29 @@
     linear[2] = cols[:, 5:6] * f0 + cols[:, 6:7] * f1 + cols[:, 3:4] * f2
     linear[3] = jnp.broadcast_to(cols[:, 0:1], (rows, 128))
 
-    def edges(t, carry):
-        row = pl.multiple_of(t * 8, 8)
-        right = jnp.zeros((8, 128), jnp.float32)
-        left = jnp.zeros((8, 128), jnp.float32)
-        k = 0
-        for items, depth in ((Y_EDGE, 0), (Y_SECOND, 1)):
-            for i in items:
-                for x in range(4):
-                    vr = post[i, x, pl.ds(row, 8), :]
-                    vl = post[MIRROR_Y[i], x, pl.ds(row, 8), :]
-                    right = jnp.where(lane == k, pltpu.roll(vr, (k - (127 - depth)) % 128, 1), right)
-                    left = jnp.where(lane == k, pltpu.roll(vl, (k - depth) % 128, 1), left)
-                    k += 1
-        for x in range(4):
-            v = solidp[x, pl.ds(row, 8), :]
-            right = jnp.where(lane == k, pltpu.roll(v, (k - 127) % 128, 1), right)
-            left = jnp.where(lane == k, pltpu.roll(v, k, 1), left)
-            k += 1
+    for row in range(0, rows, 8):
+        out = slice(row, row + 8)
+        if row == 0 or row == rows - 8:
+            right = left = jnp.zeros((8, 128), jnp.float32)
+            k = 0
+            for items, depth in ((Y_EDGE, 0), (Y_SECOND, 1)):
+                for i in items:
+                    for x in range(4):
+                        right = pick(lane, k, post[i, x, out, :], 127 - depth, right)
+                        left = pick(lane, k, post[MIRROR_Y[i], x, out, :], depth, left)
+                        k += 1
+            for x in range(4):
+                right = pick(lane, k, solidp[x, out, :], 127, right)
+                left = pick(lane, k, solidp[x, out, :], 0, left)
+                k += 1
+        else:
+            right, left = right_in[out, :], left_in[out, :]
         for c in range(3):
-            v = linear[c, pl.ds(row, 8), :]
-            right = jnp.where(lane == k, pltpu.roll(v, (k - 63) % 128, 1), right)
-            left = jnp.where(lane == k, pltpu.roll(v, (k - 64) % 128, 1), left)
-            k += 1
-        ya[pl.ds(row, 8), :] = jnp.where(y_even, right, left)
-        yb[pl.ds(row, 8), :] = jnp.where(y_even, left, right)
-        return carry
-
-    lax.fori_loop(0, rows // 8, edges, 0)
+            v = linear[c, out, :]
+            right = pick(lane, 80 + c, v, 63, right)
+            left = pick(lane, 80 + c, v, 64, left)
+        ya[out, :] = jnp.where(y_even, right, left)
+        yb[out, :] = jnp.where(y_even, left, right)
     half = rows // 2
     lane_h = lax.broadcasted_iota(jnp.int32, (half, 128), 1)
     for c in range(3):
@@ -272,9 +321,10 @@
 
 
 def final_kernel(
-    nz, ny, post, solidp, linear, meanrow, sa, sb, ya, yb, wy, wg,
-    inflow, state,
+    nz, post, solidp, linear, meanrow, sa, sb, ya, yb, wy, wg,
+    inflow, state_out,
     lhs, flow, post2, strip_l, strip_r, own_l, own_r, sx_l, sx_r, ghosts, ghost_cols, tl, tr,
+    state, flow_own, sems,
 ):
     height = state.shape[2]
     rows = height + 2 * PAD
@@ -313,7 +363,9 @@
     flow[...] = prod
     flow[0:rows, :] = prod[0:rows] + linear[3]
     for c in range(3):
-        inflow[c] = flow[rows * c + PAD : rows * c + top, :]
+        flow_own[c] = flow[rows * c + PAD : rows * c + top, :]
+    flow_copy = pltpu.make_async_copy(flow_own, inflow, sems.at[height // 8])
+    flow_copy.start()
     b_end = float(taps()[0])
     ghost_flow = []
     for c in range(3):
@@ -418,14 +470,11 @@
     step_one(PAD - 1, PAD - 1, (sub == 0) & (kz == 0))
     step_one(top - 7, top - 7, (sub == 7) & (kz == nz - 1))
 
-    def main(t, carry):
-        row = pl.multiple_of(t * 8 + PAD, 8)
-        step_one(row, row, None)
-        return carry
-
-    lax.fori_loop(0, height // 8, main, 0)
-
-    def last(t, carry):
+    def out_copy(t):
+        at = pl.ds(pl.multiple_of(t * 8, 8), 8)
+        return pltpu.make_async_copy(state.at[:, :, at, :], state_out.at[:, :, at, :], sems.at[t])
+
+    def last(t):
         row = pl.multiple_of(t * 8 + PAD, 8)
         us = [INLET * flow[pl.ds(rows * c + row, 8), :] for c in range(3)]
         eq = inlet_state(*us)
@@ -436,9 +485,22 @@
                 if x == 0:
                     g = jnp.where(solid, g, eq[i])
                 state[i, x, pl.ds(row - PAD, 8), :] = g
+        out_copy(t).start()
+
+    step_one(PAD, PAD, None)
+
+    def main(t, carry):
+        row = pl.multiple_of(t * 8 + PAD, 8)
+        step_one(row, row, None)
+        last(t - 1)
         return carry
 
-    lax.fori_loop(0, height // 8, last, 0)
+    tiles = height // 8
+    lax.fori_loop(1, tiles, main, 0)
+    last(tiles - 1)
+    for t in range(tiles):
+        out_copy(t).wait()
+    flow_copy.wait()
 
 
 def swap_pairs(count, phase, distance=1):
@@ -461,52 +523,87 @@
     return [pl.BlockSpec(memory_space=pltpu.VMEM)] * n
 
 
+def hbm(n):
+    return [pl.BlockSpec(memory_space=pltpu.HBM)] * n
+
+
 def f32(*shape):
     return jax.ShapeDtypeStruct(shape, jnp.float32)
 
 
 def scratch(*shape):
     return pltpu.VMEM(shape, jnp.float32)
+
+
+def flags(*shape):
+    return pltpu.VMEM(shape, jnp.int32)
+
+
+def params(mib):
+    return pltpu.CompilerParams(vmem_limit_bytes=mib * 1024 * 1024)
+
+
+def cost(flops, size):
+    return pl.CostEstimate(flops=flops, bytes_accessed=size, transcendentals=0)
 
 
 def shards(nz, ny, noise, mean_profile, lund_diag, lund_off, populations, mask):
     height, span = noise.shape[1], noise.shape[2]
     rows = height + 2 * PAD
-    params = pltpu.CompilerParams(vmem_limit_bytes=VMEM_BYTES)
     message = ROW_NOISE + 3 * height
+    dma = pltpu.SemaphoreType.DMA
+    here = lambda value: pltpu.with_memory_space_constraint(value, pltpu.HBM)
+    mean_profile = mean_profile.reshape(1, height)
+    noise, mean_profile, lund_diag, lund_off, populations, mask = map(
+        here, (noise, mean_profile, lund_diag, lund_off, populations, mask)
+    )
 
     za, zb, z2 = pl.pallas_call(
         lambda *refs: edge_kernel(nz, *refs),
         out_shape=(f32(message, 128), f32(message, 128), f32(16, 128)),
-        in_specs=vm(6),
+        in_specs=hbm(6),
         out_specs=vm(3),
-        scratch_shapes=[scratch(20, 4, 16, 128)],
-        compiler_params=params,
+        scratch_shapes=[
+            scratch(19, 4, 16, 128), flags(4, 16, 128), scratch(1, height), scratch(3, height),
+            scratch(3, height), scratch(20, 4, 16, 128), dma((13,)),
+        ],
+        compiler_params=params(8),
         name="edge_rows",
-    )(populations, mask, noise, mean_profile.reshape(1, height), lund_diag, lund_off)
+    )(populations, mask, noise, mean_profile, lund_diag, lund_off)
 
     ra = lax.ppermute(za, "gz", swap_pairs(nz, 0))
     rb = lax.ppermute(zb, "gz", swap_pairs(nz, 1))
     rc = lax.ppermute(z2, "gz", swap_pairs(nz, 0, 2))
     far = swap_pairs(nz, 1, 2)
-    far = [pair for pair in far if abs(pair[0] - pair[1]) == 2]
     rd = lax.ppermute(z2, "gz", far) if far else jnp.zeros_like(z2)
+
+    post, solidp, right_cols, left_cols = pl.pallas_call(
+        lambda *refs: bulk_kernel(nz, *refs),
+        out_shape=(f32(19, 4, rows, 128), f32(4, rows, 128), f32(rows, 128), f32(rows, 128)),
+        in_specs=hbm(2),
+        out_specs=vm(4),
+        scratch_shapes=[scratch(19, 4, height, 128), flags(4, height, 128), dma((5,))],
+        compiler_params=params(8),
+        cost_estimate=cost(4_000_000_000, 8_000_000),
+        name="bulk",
+    )(populations, mask)
 
     line = np.arange(rows) - PAD
     used = (line >= -1) & (line <= height)
     bandz = np.where(used[:, None], band(np.arange(-height, 2 * height), line).T, 0.0)
     post, solidp, ya, yb, linear, meanrow = pl.pallas_call(
-        lambda *refs: column_kernel(nz, ny, *refs),
+        lambda *refs: column_kernel(nz, *refs),
         out_shape=(
             f32(19, 4, rows, 128), f32(4, rows, 128), f32(rows + 3 * rows // 2, 128),
             f32(rows + 3 * rows // 2, 128), f32(4, rows, 128), f32(8, 128),
         ),
-        in_specs=vm(9),
+        in_specs=vm(10),
         out_specs=vm(6),
         scratch_shapes=[scratch(3 * height, 384), scratch(rows, 384)],
-        compiler_params=params,
+        input_output_aliases={0: 0, 1: 1},
+        compiler_params=params(4),
         name="columns",
-    )(populations, mask, noise, za, ra, rb, rc, rd, jnp.asarray(bandz, jnp.float32))
+    )(post, solidp, right_cols, left_cols, za, ra, rb, rc, rd, jnp.asarray(bandz, jnp.float32))
 
     qa = lax.ppermute(ya, ("gy", "col"), ring_pairs(ny, 0))
     qb = lax.ppermute(yb, ("gy", "col"), ring_pairs(ny, 1))
@@ -519,17 +616,18 @@
     wg = np.zeros((8, 384), np.float32)
     wg[0:2] = band(source, np.array([-1, span])).T
     inflow, state = pl.pallas_call(
-        lambda *refs: final_kernel(nz, ny, *refs),
+        lambda *refs: final_kernel(nz, *refs),
         out_shape=(f32(3, height, span), f32(19, 4, height, span)),
         in_specs=vm(10),
-        out_specs=vm(2),
+        out_specs=hbm(2),
         scratch_shapes=[
             scratch(3 * rows, 384), scratch(3 * rows, 128), scratch(19, 4, rows, 128),
             scratch(128, 128), scratch(128, 128), scratch(128, 128), scratch(128, 128),
             scratch(16, 128), scratch(16, 128), scratch(128, 128), scratch(128, 128),
-            scratch(rows, 128), scratch(rows, 128),
+            scratch(rows, 128), scratch(rows, 128), scratch(19, 4, height, span),
+            scratch(3, height, span), dma((height // 8 + 1,)),
         ],
-        compiler_params=params,
+        compiler_params=params(12),
         name="stream",
     )(post, solidp, linear, meanrow, ya, yb, qa, qb, jnp.asarray(wy), jnp.asarray(wg))
     return inflow, state

time: 36.3 us -> 27 us (0.74)
  local copies, waits for them, and re-layouts: 7.4 us -> 0.02 us
  waiting for transfers between devices: 7.37 us -> 2.99 us
  Pallas kernels: 11.4 us -> 12.8 us
  starting transfers between devices: 9.14 us -> 10.3 us
    unnamed x20 -> x6, local copies, waits for them, and re-layouts: 7.4 us -> 0.02 us
    ppermute x1, waiting for transfers between devices: 4.55 us -> 0.01 us  [shards(): rc = lax.ppermute(z2, 'gz', swap_pairs(nz, 0, 2))]
    ppermute x1, starting transfers between devices: 0.01 us -> 4.1 us  [shards(): rc = lax.ppermute(z2, 'gz', swap_pairs(nz, 0, 2))]
    ppermute x1, starting transfers between devices: 5.9 us -> 2.89 us  [shards(): ra = lax.ppermute(za, 'gz', swap_pairs(nz, 0))]
    pallas_call x1, Pallas kernels: 0.28 us -> 1.49 us  [shards(): pl.pallas_call(lambda *refs: edge_kernel(nz, *refs), out_shape=(f32(messa...]
    pallas_call x2 -> x3, Pallas kernels: 11.1 us -> 11.3 us  [the longest x1 5.76 us: shards(): pl.pallas_call(lambda *refs: bulk_kernel(nz, *refs), out_shape=(f32(19, 4...]
  transfers between devices with their start and end apart: 5 -> 5, of which waited for: 2 -> 1; matrix products, arithmetic and copies ran while one was open for 0% -> 0% of each run, Pallas kernels for 0% -> 22%
where the time goes in v1:
time: 27 us; the launch traced here: 26.8 us
  Pallas kernels  12.8 us (47%)
  starting transfers between devices  10.3 us (38%)
  waiting for transfers between devices  2.99 us (11%)
  between operations  0.74 us (3%)
    pallas_call x1, Pallas kernels, shards(): pl.pallas_call(lambda *refs: bulk_kernel(nz, *refs), out_shape=(f32(19, 4...  5.76 us
    pallas_call x1, Pallas kernels, shards(): pl.pallas_call(lambda *refs: final_kernel(nz, *refs), out_shape=(f32(3, h...  4.77 us
    ppermute x1, starting transfers between devices, shards(): rc = lax.ppermute(z2, 'gz', swap_pairs(nz, 0, 2))  4.1 us
    ppermute x1, waiting for transfers between devices, shards(): qb = lax.ppermute(yb, ('gy', 'col'), ring_pairs(ny, 1))  2.98 us
    ppermute x1, starting transfers between devices, shards(): ra = lax.ppermute(za, 'gz', swap_pairs(nz, 0))  2.89 us
    ppermute x1, starting transfers between devices, shards(): qb = lax.ppermute(yb, ('gy', 'col'), ring_pairs(ny, 1))  2.55 us
    pallas_call x1, Pallas kernels, shards(): pl.pallas_call(lambda *refs: edge_kernel(nz, *refs), out_shape=(f32(messa...  1.49 us
    pallas_call x1, Pallas kernels, shards(): pl.pallas_call(lambda *refs: column_kernel(nz, *refs), out_shape=(f32(19,...  0.81 us
  transfers between devices with their start and end apart: 5, of which 1 were waited for; matrix products, arithmetic and copies ran while one was open for 0% of the time, Pallas kernels for 22%

profile of v1, /device:TPU:0, one launch (start us, length us, event | category | flops | bytes accessed | tf_op | source)
XLA Modules:
  0.0 26.8 jit_solution(11603411016003252322)
XLA Ops:
  0.6 1.5 %edge_rows.1 = (f32[280,128]{1,0:T(8,128)S(1)}, f32[280,128]{1,0:T(8,128)S(1)}, f32[16,128]{1,0:T(8,128)S(1)}) custom-call(f32[19,4,64,128]{3,2,1,0:T(8,128)} %refs_0_.3, s32[4,64,128]{2,1,0:T(8,128)} %refs_1_.3, f32[3,64,128]{2,1,0:T(8,128)} %refs_2_.1, f32[1,64]{1,0:T(1,128)} %bitcast.1, f32[3,64]{1,0:T(4,128)} %refs_4_.1, f32[3,64]{1,0:T(4,128)} %refs_5_.1), custom_call_target="tpu_custom_call" | custom-call | tf_op jit(solution)/shard_map/edge_rows/pallas_call | solution.py:561
  2.1 4.1 %collective-permute-start.2 = (f32[16,128]{1,0:T(8,128)S(1)}, f32[16,128]{1,0:T(8,128)S(1)}, u32[]{:S(2)}, u32[]{:S(2)}) collective-permute-start(f32[16,128]{1,0:T(8,128)S(1)} %get-tuple-element.21), channel_id=1, source_target_pairs={{0,4},{2,6},{4,0},{6,2},{1,5},{3,7},{5,1},{7,3},{8,12},{10,14},{12... | collective-permute-start | bytes 24584 | tf_op jit(solution)/shard_map/ppermute | solution.py:576
  6.2 0.7 %collective-permute-start.1 = (f32[280,128]{1,0:T(8,128)S(1)}, f32[280,128]{1,0:T(8,128)S(1)}, u32[]{:S(2)}, u32[]{:S(2)}) collective-permute-start(f32[280,128]{1,0:T(8,128)S(1)} %get-tuple-element.20), channel_id=1, source_target_pairs={{2,4},{4,2},{3,5},{5,3},{10,12},{12,10},{11,13},{13,11},{18,20},{2... | collective-permute-start | bytes 430088 | tf_op jit(solution)/shard_map/ppermute | solution.py:575
  6.9 0.0 copy-start.1
  6.9 2.9 %collective-permute-start = (f32[280,128]{1,0:T(8,128)S(1)}, f32[280,128]{1,0:T(8,128)S(1)}, u32[]{:S(2)}, u32[]{:S(2)}) collective-permute-start(f32[280,128]{1,0:T(8,128)S(1)} %get-tuple-element.19.refs_4_), channel_id=1, source_target_pairs={{0,2},{2,0},{4,6},{6,4},{1,3},{3,1},{5,7},{7,5},{8,10},{10,8},{12,... | collective-permute-start | bytes 430088 | tf_op jit(solution)/shard_map/ppermute | solution.py:574
  9.8 5.8 %bulk.1 = (f32[19,4,80,128]{3,2,1,0:T(8,128)S(1)}, f32[4,80,128]{2,1,0:T(8,128)S(1)}, f32[80,128]{1,0:T(8,128)S(1)}, f32[80,128]{1,0:T(8,128)S(1)}) custom-call(f32[19,4,64,128]{3,2,1,0:T(8,128)} %refs_0_.3, s32[4,64,128]{2,1,0:T(8,128)} %refs_1_.3), custom_call_target="tpu_custom_call" | custom-call | flops 4000000000 | bytes 8000000 | tf_op jit(solution)/shard_map/bulk/pallas_call | solution.py:580
  15.6 0.0 copy-start
  15.6 0.0 copy-start.2
  15.6 0.0 collective-permute-done.2.refs_7_
  15.6 0.0 collective-permute-done.1.refs_6_
  15.6 0.0 collective-permute-done.refs_5_
  15.6 0.0 copy-done.1
  15.6 0.8 %columns.1 = (f32[19,4,80,128]{3,2,1,0:T(8,128)S(1)}, f32[4,80,128]{2,1,0:T(8,128)S(1)}, f32[200,128]{1,0:T(8,128)S(1)}, f32[200,128]{1,0:T(8,128)S(1)}, f32[4,8...) custom-call(f32[19,4,80,128]{3,2,1,0:T(8,128)S(1)} %get-tuple-element.15.refs_0_, ...), custom_call_target="tpu_custom_call", output_to_operand_aliasing={{0}: (0, {}), {1}: (1, {})} | custom-call | tf_op jit(solution)/shard_map/columns/pallas_call | solution.py:594
  16.5 0.1 collective-permute-start.3
  16.5 2.5 %collective-permute-start.4 = (f32[200,128]{1,0:T(8,128)S(1)}, f32[200,128]{1,0:T(8,128)S(1)}, u32[]{:S(2)}, u32[]{:S(2)}) collective-permute-start(f32[200,128]{1,0:T(8,128)S(1)} %get-tuple-element.27.refs_5_), channel_id=1, source_target_pairs={{0,25},{1,8},{8,1},{9,16},{16,9},{17,24},{24,17},{25,0},{2,27},{3,... | collective-permute-start | bytes 307208 | tf_op jit(solution)/shard_map/ppermute | solution.py:609
  19.1 0.0 collective-permute-done.3.refs_6_
  19.1 3.0 %collective-permute-done.4.refs_7_ = f32[200,128]{1,0:T(8,128)S(1)} collective-permute-done((f32[200,128]{1,0:T(8,128)S(1)}, f32[200,128]{1,0:T(8,128)S(1)}, u32[]{:S(2)}, u32[]{:S(2)}) %collective-permute-start.4) | collective-permute-done | bytes 102432 | tf_op jit(solution)/shard_map/ppermute | solution.py:609
  22.1 0.0 copy-done
  22.1 0.0 copy-done.2
  22.1 4.8 %stream.1 = (f32[3,64,128]{2,1,0:T(8,128)}, f32[19,4,64,128]{3,2,1,0:T(8,128)}) custom-call(f32[19,4,80,128]{3,2,1,0:T(8,128)S(1)} %get-tuple-element.22.refs_0_, f32[4,80,128]{2,1,0:T(8,128)S(1)} %get-tuple-element.23.refs_1_, f32[4,80,128]{2,1,0:T(8,128)S(1)} %get-tuple-element.24.refs_2_, f32[8,128]{1,0:T(8,128)S(1)} %get-tuple-element.25.refs_3_, ...), custom_call_target="tpu_custom_call" | custom-call | tf_op jit(solution)/shard_map/stream/pallas_call | solution.py:618
  (1 shorter events, 0.0 us)
Async XLA Ops:
  2.1 13.5 %collective-permute-start.2 = (f32[16,128]{1,0:T(8,128)S(1)}, f32[16,128]{1,0:T(8,128)S(1)}, u32[]{:S(2)}, u32[]{:S(2)}) collective-permute-start(f32[16,128]{1,0:T(8,128)S(1)} %get-tuple-element.21), channel_id=1, source_target_pairs={{0,4},{2,6},{4,0},{6,2},{1,5},{3,7},{5,1},{7,3},{8,12},{10,14},{12... | collective-permute-start | bytes 24584 | tf_op jit(solution)/shard_map/ppermute | solution.py:576
  6.2 9.4 %collective-permute-start.1 = (f32[280,128]{1,0:T(8,128)S(1)}, f32[280,128]{1,0:T(8,128)S(1)}, u32[]{:S(2)}, u32[]{:S(2)}) collective-permute-start(f32[280,128]{1,0:T(8,128)S(1)} %get-tuple-element.20), channel_id=1, source_target_pairs={{2,4},{4,2},{3,5},{5,3},{10,12},{12,10},{11,13},{13,11},{18,20},{2... | collective-permute-start | bytes 430088 | tf_op jit(solution)/shard_map/ppermute | solution.py:575
  6.9 8.7 %copy-start.1 = (f32[80,192]{1,0:T(8,128)S(1)}, f32[80,192]{1,0:T(8,128)}, u32[]{:S(2)}) copy-start(f32[80,192]{1,0:T(8,128)} %constant.8.clone.refs_9_) | copy-start | bytes 184324
  6.9 8.7 %collective-permute-start = (f32[280,128]{1,0:T(8,128)S(1)}, f32[280,128]{1,0:T(8,128)S(1)}, u32[]{:S(2)}, u32[]{:S(2)}) collective-permute-start(f32[280,128]{1,0:T(8,128)S(1)} %get-tuple-element.19.refs_4_), channel_id=1, source_target_pairs={{0,2},{2,0},{4,6},{6,4},{1,3},{3,1},{5,7},{7,5},{8,10},{10,8},{12,... | collective-permute-start | bytes 430088 | tf_op jit(solution)/shard_map/ppermute | solution.py:574
  15.6 6.5 %copy-start = (f32[384,128]{1,0:T(8,128)S(1)}, f32[384,128]{1,0:T(8,128)}, u32[]{:S(2)}) copy-start(f32[384,128]{1,0:T(8,128)} %constant.9.clone.refs_8_) | copy-start | bytes 589828
  15.6 6.5 %copy-start.2 = (f32[8,384]{1,0:T(8,128)S(1)}, f32[8,384]{1,0:T(8,128)}, u32[]{:S(2)}) copy-start(f32[8,384]{1,0:T(8,128)} %constant.10.clone.refs_9_) | copy-start | bytes 36868
  16.5 2.6 %collective-permute-start.3 = (f32[200,128]{1,0:T(8,128)S(1)}, f32[200,128]{1,0:T(8,128)S(1)}, u32[]{:S(2)}, u32[]{:S(2)}) collective-permute-start(f32[200,128]{1,0:T(8,128)S(1)} %get-tuple-element.26.refs_4_), channel_id=1, source_target_pairs={{0,1},{1,0},{8,9},{9,8},{16,17},{17,16},{24,25},{25,24},{2,3},{3,2... | collective-permute-start | bytes 307208 | tf_op jit(solution)/shard_map/ppermute | solution.py:608
  16.5 5.5 %collective-permute-start.4 = (f32[200,128]{1,0:T(8,128)S(1)}, f32[200,128]{1,0:T(8,128)S(1)}, u32[]{:S(2)}, u32[]{:S(2)}) collective-permute-start(f32[200,128]{1,0:T(8,128)S(1)} %get-tuple-element.27.refs_5_), channel_id=1, source_target_pairs={{0,25},{1,8},{8,1},{9,16},{16,9},{17,24},{24,17},{25,0},{2,27},{3,... | collective-permute-start | bytes 307208 | tf_op jit(solution)/shard_map/ppermute | solution.py:609

commit v2 on v1

--- a/solution.py
+++ b/solution.py
@@ -23,8 +23,11 @@
 
 Z_EDGE = [i for i in range(19) if DIRS[i][2] == 0] + [i for i in range(19) if DIRS[i][2] == 1]
 Z_SECOND = [i for i in range(19) if DIRS[i][2] == 1]
-Y_EDGE = [i for i in range(19) if DIRS[i][1] == 0] + [i for i in range(19) if DIRS[i][1] == 1]
-Y_SECOND = [i for i in range(19) if DIRS[i][1] == 1]
+Y_FLAT = [i for i in range(19) if DIRS[i][1] == 0]
+Y_PLUS = [i for i in range(19) if DIRS[i][1] == 1]
+FLAG_PLANE = 4 * len(Y_FLAT)
+LANE_PLUS = 2 * FLAG_PLANE + 8
+LANE_FAR = LANE_PLUS + 8 * len(Y_PLUS)
 
 ROW_SOLID = 76
 ROW_PARAM = 80
@@ -176,54 +179,61 @@
         z2[8 + c : 9 + c, :] = jnp.where(low_half, first, last)
 
 
-def pick(lane, k, value, column, into):
-    return jnp.where(lane == k, pltpu.roll(value, (k - column) % 128, 1), into)
-
-
-def bulk_kernel(nz, pops, mask, post, solidp, right_cols, left_cols, raw, flags, sems):
+def dot3(a, b, dims=(((1,), (0,)), ((), ()))):
+    a_hi, b_hi = a.astype(jnp.bfloat16), b.astype(jnp.bfloat16)
+    a_lo = (a - a_hi.astype(jnp.float32)).astype(jnp.bfloat16)
+    b_lo = (b - b_hi.astype(jnp.float32)).astype(jnp.bfloat16)
+
+    def dot(u, v):
+        return lax.dot_general(u, v, dims, preferred_element_type=jnp.float32)
+
+    return dot(a_hi, b_hi) + (dot(a_lo, b_hi) + dot(a_hi, b_lo))
+
+
+NT = (((1,), (1,)), ((), ()))
+
+
+def put_pair(pair, slot, value, first_column, into):
+    return jnp.where(pair == slot, pltpu.roll(value, (2 * slot - first_column) % 128, 1), into)
+
+
+def bulk_kernel(nz, pops, mask, post, solidp, right_cols, left_cols):
     height = pops.shape[2]
     kz = lax.axis_index("gz")
-    lane = lax.broadcasted_iota(jnp.int32, (8, 128), 1)
-    copies = [pltpu.make_async_copy(mask, flags, sems.at[4])]
-    copies += [
-        pltpu.make_async_copy(pops.at[:, x], raw.at[:, x], sems.at[x]) for x in range(4)
-    ]
-    for copy in copies:
-        copy.start()
-    copies[0].wait()
-    for x in range(4):
-        copies[1 + x].wait()
-
-        def body(t, carry):
-            row = pl.multiple_of(t * 8, 8)
-            out = pl.ds(row + PAD, 8)
-            solid = (flags[x, pl.ds(row, 8), :] == 1) | wall_rows(row, height, kz, nz)
-            p = collide([raw[i, x, pl.ds(row, 8), :] for i in range(19)], solid)
-            for i in range(19):
-                post[i, x, out, :] = p[i]
+    pair = lax.broadcasted_iota(jnp.int32, (8, 128), 1) // 2
+
+    def body(t, carry):
+        row = pl.multiple_of(t * 8, 8)
+        out = pl.ds(row + PAD, 8)
+        wall = wall_rows(row, height, kz, nz)
+        flat = right = left = jnp.zeros((8, 128), jnp.float32)
+        for x in range(4):
+            solid = (mask[x, pl.ds(row, 8), :] == 1) | wall
+            p = collide([pops[i, x, pl.ds(row, 8), :] for i in range(19)], solid)
             flag = solid.astype(jnp.float32)
             solidp[x, out, :] = flag
-            if x == 0:
-                right = left = jnp.zeros((8, 128), jnp.float32)
-            else:
-                right, left = right_cols[out, :], left_cols[out, :]
-            q = 0
-            for items, depth in ((Y_EDGE, 0), (Y_SECOND, 1)):
-                for i in items:
-                    right = pick(lane, 4 * q + x, p[i], 127 - depth, right)
-                    left = pick(lane, 4 * q + x, p[MIRROR_Y[i]], depth, left)
-                    q += 1
-            right_cols[out, :] = pick(lane, 4 * q + x, flag, 127, right)
-            left_cols[out, :] = pick(lane, 4 * q + x, flag, 0, left)
-            return carry
-
-        lax.fori_loop(0, height // 8, body, 0)
+            flat = put_pair(pair, FLAG_PLANE + x, flag, 127, flat)
+            for q, i in enumerate(Y_FLAT):
+                post[i, x, out, :] = p[i]
+                flat = put_pair(pair, 4 * q + x, p[i], 127, flat)
+            for n, i in enumerate(Y_PLUS):
+                j = MIRROR_Y[i]
+                slot = LANE_PLUS // 2 + 4 * n + x
+                post[i, x, out, :] = pltpu.roll(p[i], 1, 1)
+                post[j, x, out, :] = pltpu.roll(p[j], 127, 1)
+                right = put_pair(pair, slot, p[i], 126, right)
+                left = put_pair(pair, slot, p[j], 0, left)
+        right_cols[out, :] = jnp.where(pair < LANE_PLUS // 2, flat, right)
+        left_cols[out, :] = jnp.where(pair < LANE_PLUS // 2, flat, left)
+        return carry
+
+    lax.fori_loop(0, height // 8, body, 0)
 
 
 def column_kernel(
     nz, post_in, solid_in, right_in, left_in, sent, za, zb, z2c, z2d, bandz,
     post, solidp, ya, yb, linear, meanrow,
-    wide, filt,
+    wide, filt, moved,
 ):
     height = post.shape[2] - 2 * PAD
     rows = height + 2 * PAD
@@ -240,20 +250,20 @@
         return jnp.where(z_even, za[row : row + n, :], zb[row : row + n, :])
 
     top = PAD + height
-    q = 0
-    for i in Z_EDGE:
-        for x in range(4):
-            post[i, x, PAD - 1 : PAD, :] = below(4 * q + x)
-            post[MIRROR_Z[i], x, top : top + 1, :] = above(4 * q + x)
-        q += 1
-    for i in Z_SECOND:
-        for x in range(4):
-            post[i, x, PAD - 2 : PAD - 1, :] = below(4 * q + x)
-            post[MIRROR_Z[i], x, top + 1 : top + 2, :] = above(4 * q + x)
-        q += 1
+    low, high = below(0, ROW_PARAM), above(0, ROW_PARAM)
+    for n, shift in enumerate((0, 1, 127)):
+        moved[n, 0] = low if shift == 0 else pltpu.roll(low, shift, 1)
+        moved[n, 1] = high if shift == 0 else pltpu.roll(high, shift, 1)
+    for items, first, depth in ((Z_EDGE, 0, 0), (Z_SECOND, len(Z_EDGE), 1)):
+        for q, i in enumerate(items):
+            n = DIRS[i][1] % 3
+            for x in range(4):
+                at = slice(4 * (first + q) + x, 4 * (first + q) + x + 1)
+                post[i, x, PAD - 1 - depth : PAD - depth, :] = moved[n, 0, at, :]
+                post[MIRROR_Z[i], x, top + depth : top + depth + 1, :] = moved[n, 1, at, :]
     for x in range(4):
-        solidp[x, PAD - 1 : PAD, :] = below(4 * q + x)
-        solidp[x, top : top + 1, :] = above(4 * q + x)
+        solidp[x, PAD - 1 : PAD, :] = moved[0, 0, ROW_SOLID + x : ROW_SOLID + x + 1, :]
+        solidp[x, top : top + 1, :] = moved[0, 1, ROW_SOLID + x : ROW_SOLID + x + 1, :]
 
     lane = lax.broadcasted_iota(jnp.int32, (8, 128), 1)
     own_par = pltpu.roll(sent[ROW_PARAM : ROW_PARAM + 8, :], PAD, 1)
@@ -270,9 +280,7 @@
         wide[0:height, lanes] = below(ROW_NOISE + height * c, height)
         wide[height : 2 * height, lanes] = sent[at, :]
         wide[2 * height : 3 * height, lanes] = above(ROW_NOISE + height * c, height)
-    filt[...] = jnp.dot(
-        bandz[...], wide[...], precision=lax.Precision.HIGHEST, preferred_element_type=jnp.float32
-    )
+    filt[...] = dot3(bandz[...], wide[...])
     b_end = float(taps()[0])
     far_low = jnp.where(low_half, z2d[8:16, :], z2c[0:8, :])
     far_high = jnp.where(low_half, z2c[0:8, :], z2d[8:16, :])
@@ -286,27 +294,28 @@
     linear[2] = cols[:, 5:6] * f0 + cols[:, 6:7] * f1 + cols[:, 3:4] * f2
     linear[3] = jnp.broadcast_to(cols[:, 0:1], (rows, 128))
 
+    pair = lane // 2
     for row in range(0, rows, 8):
         out = slice(row, row + 8)
         if row == 0 or row == rows - 8:
-            right = left = jnp.zeros((8, 128), jnp.float32)
-            k = 0
-            for items, depth in ((Y_EDGE, 0), (Y_SECOND, 1)):
-                for i in items:
-                    for x in range(4):
-                        right = pick(lane, k, post[i, x, out, :], 127 - depth, right)
-                        left = pick(lane, k, post[MIRROR_Y[i], x, out, :], depth, left)
-                        k += 1
+            flat = right = left = jnp.zeros((8, 128), jnp.float32)
             for x in range(4):
-                right = pick(lane, k, solidp[x, out, :], 127, right)
-                left = pick(lane, k, solidp[x, out, :], 0, left)
-                k += 1
+                flat = put_pair(pair, FLAG_PLANE + x, solidp[x, out, :], 127, flat)
+                for q, i in enumerate(Y_FLAT):
+                    flat = put_pair(pair, 4 * q + x, post[i, x, out, :], 127, flat)
+                for n, i in enumerate(Y_PLUS):
+                    slot = LANE_PLUS // 2 + 4 * n + x
+                    right = put_pair(pair, slot, post[i, x, out, :], 127, right)
+                    left = put_pair(pair, slot, post[MIRROR_Y[i], x, out, :], 127, left)
+            right = jnp.where(pair < LANE_PLUS // 2, flat, right)
+            left = jnp.where(pair < LANE_PLUS // 2, flat, left)
         else:
             right, left = right_in[out, :], left_in[out, :]
         for c in range(3):
             v = linear[c, out, :]
-            right = pick(lane, 80 + c, v, 63, right)
-            left = pick(lane, 80 + c, v, 64, left)
+            far = LANE_FAR + c
+            right = jnp.where(lane == far, pltpu.roll(v, (far - 63) % 128, 1), right)
+            left = jnp.where(lane == far, pltpu.roll(v, (far - 64) % 128, 1), left)
         ya[out, :] = jnp.where(y_even, right, left)
         yb[out, :] = jnp.where(y_even, left, right)
     half = rows // 2
@@ -320,11 +329,57 @@
         yb[at, :] = jnp.where(y_even, left, right)
 
 
+def streamed(i, x):
+    source = x - DIRS[i][0]
+    return None if source < 0 else min(source, 3)
+
+
+def interior_kernel(
+    nz, post, solidp, linear, ya, yb, wy, wg, post2, flow_own, ghost_own, own_right, own_left
+):
+    rows = post.shape[2]
+    top = rows - PAD
+    kz = lax.axis_index("gz")
+    ky = lax.axis_index("gy") * lax.axis_size("col") + lax.axis_index("col")
+    y_even = lax.rem(ky, 2) == 0
+    sub = lax.broadcasted_iota(jnp.int32, (8, 128), 0)
+
+    def step(row, outside):
+        for x in range(1, 4):
+            solid = solidp[x, pl.ds(row, 8), :] > 0.5
+            g = [post[i, streamed(i, x), pl.ds(row - DIRS[i][2], 8), :] for i in range(19)]
+            p = collide(g, solid)
+            for i in range(19):
+                value = p[i] if outside is None else jnp.where(outside, 0.0, p[i])
+                if DIRS[i][1]:
+                    value = pltpu.roll(value, DIRS[i][1] % 128, 1)
+                post2[i, x - 1, pl.ds(row, 8), :] = value
+
+    step(PAD - 1, (sub == 0) & (kz == 0))
+    step(top - 7, (sub == 7) & (kz == nz - 1))
+
+    def body(t, carry):
+        step(pl.multiple_of(t * 8 + PAD, 8), None)
+        return carry
+
+    lax.fori_loop(0, rows // 8 - 2, body, 0)
+
+    flow_own[...] = dot3(linear[0:3].reshape(3 * rows, 128), wy[0:128, :])
+    flow_own[0:rows, :] += linear[3]
+    for c in range(3):
+        ghost_own[8 * c : 8 * c + 8, 0:rows] = dot3(wg[:, 0:128], linear[c], NT)
+        ghost_own[8 * c : 8 * c + 8, rows:128] = jnp.zeros((8, 128 - rows), jnp.float32)
+    fill = jnp.zeros((128 - rows, 128), jnp.float32)
+    a, b = ya[0:rows, :], yb[0:rows, :]
+    own_right[0:128, :] = jnp.transpose(jnp.concatenate([jnp.where(y_even, a, b), fill], axis=0))
+    own_left[0:128, :] = jnp.transpose(jnp.concatenate([jnp.where(y_even, b, a), fill], axis=0))
+
+
 def final_kernel(
-    nz, post, solidp, linear, meanrow, sa, sb, ya, yb, wy, wg,
+    nz, post, solidp, post2, flow_own, ghost_own, own_right, own_left, meanrow, ya, yb, wy, wg,
     inflow, state_out,
-    lhs, flow, post2, strip_l, strip_r, own_l, own_r, sx_l, sx_r, ghosts, ghost_cols, tl, tr,
-    state, flow_own, sems,
+    lhs, flow, inlet2, strip_left, strip_right, moving, still, ghost_moving, ghost_still,
+    state, flow_out, sems,
 ):
     height = state.shape[2]
     rows = height + 2 * PAD
@@ -336,15 +391,10 @@
     lane = lax.broadcasted_iota(jnp.int32, (8, 128), 1)
     sub = lax.broadcasted_iota(jnp.int32, (8, 128), 0)
 
-    tl[0:rows, :] = jnp.where(y_even, yb[0:rows, :], ya[0:rows, :])
-    tr[0:rows, :] = jnp.where(y_even, ya[0:rows, :], yb[0:rows, :])
     fill = jnp.zeros((128 - rows, 128), jnp.float32)
-    strip_l[...] = jnp.transpose(jnp.concatenate([tl[0:rows, :], fill], axis=0))
-    strip_r[...] = jnp.transpose(jnp.concatenate([tr[0:rows, :], fill], axis=0))
-    mine_right = jnp.where(y_even, sa[0:rows, :], sb[0:rows, :])
-    mine_left = jnp.where(y_even, sb[0:rows, :], sa[0:rows, :])
-    own_l[...] = jnp.transpose(jnp.concatenate([mine_left, fill], axis=0))
-    own_r[...] = jnp.transpose(jnp.concatenate([mine_right, fill], axis=0))
+    a, b = ya[0:rows, :], yb[0:rows, :]
+    strip_left[0:128, :] = jnp.transpose(jnp.concatenate([jnp.where(y_even, b, a), fill], axis=0))
+    strip_right[0:128, :] = jnp.transpose(jnp.concatenate([jnp.where(y_even, a, b), fill], axis=0))
 
     lane_h = lax.broadcasted_iota(jnp.int32, (half, 128), 1)
     for c in range(3):
@@ -352,123 +402,88 @@
         a, b = ya[at, :], yb[at, :]
         left, right = jnp.where(y_even, b, a), jnp.where(y_even, a, b)
         lo, hi = slice(rows * c, rows * c + half), slice(rows * c + half, rows * (c + 1))
-        lhs[rows * c : rows * (c + 1), 0:128] = linear[c]
-        lhs[lo, 128:256] = jnp.where(lane_h < 64, left, 0.0)
-        lhs[hi, 128:256] = jnp.where(lane_h < 64, 0.0, left)
-        lhs[lo, 256:384] = jnp.where(lane_h < 64, right, 0.0)
-        lhs[hi, 256:384] = jnp.where(lane_h < 64, 0.0, right)
-    prod = jnp.dot(
-        lhs[...], wy[...], precision=lax.Precision.HIGHEST, preferred_element_type=jnp.float32
-    )
-    flow[...] = prod
-    flow[0:rows, :] = prod[0:rows] + linear[3]
-    for c in range(3):
-        flow_own[c] = flow[rows * c + PAD : rows * c + top, :]
-    flow_copy = pltpu.make_async_copy(flow_own, inflow, sems.at[height // 8])
+        lhs[lo, 0:128] = jnp.where(lane_h < 64, left, 0.0)
+        lhs[hi, 0:128] = jnp.where(lane_h < 64, 0.0, left)
+        lhs[lo, 128:256] = jnp.where(lane_h < 64, right, 0.0)
+        lhs[hi, 128:256] = jnp.where(lane_h < 64, 0.0, right)
+    flow[...] = flow_own[...] + dot3(lhs[...], wy[128:384, :])
+    for c in range(3):
+        flow_out[c] = flow[rows * c + PAD : rows * c + top, :]
+    flow_copy = pltpu.make_async_copy(flow_out, inflow, sems.at[height // 8])
     flow_copy.start()
     b_end = float(taps()[0])
-    ghost_flow = []
-    for c in range(3):
-        g = lax.dot_general(
-            wg[...],
-            lhs[rows * c : rows * (c + 1), :],
-            (((1,), (1,)), ((), ())),
-            precision=lax.Precision.HIGHEST,
-            preferred_element_type=jnp.float32,
-        )
+    column_flow = []
+    for c in range(3):
+        g = dot3(wg[:, 128:384], lhs[rows * c : rows * (c + 1), :], NT)
         g = jnp.concatenate([g, jnp.zeros((8, 128 - rows), jnp.float32)], axis=1)
-        at_l = g[0:1, :] + b_end * strip_l[80 + c : 81 + c, :]
-        at_r = g[1:2, :] + b_end * strip_r[80 + c : 81 + c, :]
+        g = g + ghost_own[8 * c : 8 * c + 8, :]
+        far = slice(LANE_FAR + c, LANE_FAR + c + 1)
+        at = [g[n : n + 1, :] for n in range(4)]
+        at[0] = at[0] + b_end * strip_left[far, :]
+        at[3] = at[3] + b_end * strip_right[far, :]
         if c == 0:
-            at_l = at_l + meanrow[0:1, :]
-            at_r = at_r + meanrow[0:1, :]
-        ghost_flow.append((at_l, at_r))
+            at = [v + meanrow[0:1, :] for v in at]
+        column_flow.append(at)
 
     outside = ((lane < PAD) & (kz == 0)) | ((lane >= top) & (kz == nz - 1))
-    ghosts[...] = jnp.zeros((128, 128), jnp.float32)
-    for side, (got, own, sx, edge_items) in enumerate(
-        ((strip_l, own_l, sx_l, False), (strip_r, own_r, sx_r, True))
-    ):
-        mirror = (lambda i: MIRROR_Y[i]) if edge_items else (lambda i: i)
-        solid = got[76:84, :] > 0.5
+    sources = (
+        ((strip_left, 0), (strip_left, 0), (own_left, 0)),
+        ((own_left, 1), (strip_left, 1), (own_left, 1)),
+        ((own_right, 0), (own_right, 0), (strip_right, 0)),
+        ((strip_right, 1), (own_right, 1), (strip_right, 1)),
+    )
+    for column in range(4):
+        def rows_of(start):
+            return pl.ds(start, 8, stride=2)
+
+        src, odd = sources[column][0]
+        solid = src[rows_of(2 * FLAG_PLANE + odd), :] > 0.5
         g = [None] * 19
         for i in range(19):
-            j = mirror(i)
             cx, cy, cz = DIRS[i]
-            if DIRS[j][1] == 0:
-                q, src = Y_EDGE.index(j), got
-            elif DIRS[j][1] == 1:
-                q, src = len(Y_EDGE) + Y_SECOND.index(j), got
+            src, odd = sources[column][cy % 3]
+            if cy == 0:
+                start = 8 * Y_FLAT.index(i) + odd
             else:
-                q, src = Y_EDGE.index(MIRROR_Y[j]), own
-            v = src[4 * q : 4 * q + 4, :]
-            if cx == 0:
-                w = src[4 * q : 4 * q + 8, :]
-            else:
-                sx[0:1, :] = jnp.zeros((1, 128), jnp.float32)
-                sx[1:5, :] = v
-                sx[5:6, :] = v[3:4, :]
-                w = sx[1 - cx : 9 - cx, :]
-            g[i] = w if cz == 0 else pltpu.roll(w, cz % 128, 1)
-        us = [INLET * jnp.broadcast_to(ghost_flow[c][side], (8, 128)) for c in range(3)]
+                start = LANE_PLUS + 8 * Y_PLUS.index(i if cy == 1 else MIRROR_Y[i]) + odd
+            v = src[rows_of(start - 2 * cx), :]
+            if cx == 1:
+                v = jnp.where(sub == 0, 0.0, v)
+            elif cx == -1:
+                v = jnp.where(sub == 3, src[rows_of(start), :], v)
+            g[i] = v if cz == 0 else pltpu.roll(v, cz % 128, 1)
+        us = [INLET * jnp.broadcast_to(column_flow[c][column], (8, 128)) for c in range(3)]
         eq = inlet_state(*us)
         put = (sub == 0) & jnp.logical_not(solid)
-        g = [jnp.where(put, eq[i], g[i]) for i in range(19)]
-        keep = [i for i in range(19) if DIRS[mirror(i)][1] == 1]
+        moves = 1 if column < 2 else -1
+        keep = [i for i in range(19) if DIRS[i][1] == moves or (DIRS[i][1] == 0 and column in (1, 2))]
         p = collide(g, solid, keep)
-        for n, i in enumerate(Y_SECOND):
-            value = jnp.where(outside, 0.0, p[mirror(i)])
-            at = 32 * side + 4 * n
-            ghosts[at : at + 4, :] = value[0:4, :]
-    ghost_cols[0:128, :] = jnp.transpose(ghosts[...])
-
-    def gather(src, i, x, row, from_left, from_right):
-        cx, cy, cz = DIRS[i]
-        sxx = x - cx
-        if sxx < 0:
-            return jnp.zeros((8, 128), jnp.float32)
-        sxx = min(sxx, 3)
-        v = src[i, sxx, pl.ds(row - cz, 8), :]
-        if cy == 0:
-            return v
-        v = pltpu.roll(v, cy % 128, 1)
-        if cy == 1:
-            cols, k = from_left(i, sxx)
-            ghost = pltpu.roll(cols[pl.ds(row - cz, 8), :], (-k) % 128, 1)
-            return jnp.where(lane == 0, ghost, v)
-        cols, k = from_right(i, sxx)
-        ghost = pltpu.roll(cols[pl.ds(row - cz, 8), :], (127 - k) % 128, 1)
-        return jnp.where(lane == 127, ghost, v)
-
-    def first_left(i, x):
-        return tl, 4 * Y_EDGE.index(i) + x
-
-    def first_right(i, x):
-        return tr, 4 * Y_EDGE.index(MIRROR_Y[i]) + x
-
-    def second_left(i, x):
-        return ghost_cols, 4 * Y_SECOND.index(i) + x
-
-    def second_right(i, x):
-        return ghost_cols, 32 + 4 * Y_SECOND.index(MIRROR_Y[i]) + x
-
-    def step_one(row, store_row, outside_rows):
+        for i in keep:
+            value = jnp.where(outside, 0.0, jnp.where(put, eq[i], p[i]))[0:4, :]
+            if DIRS[i][1]:
+                n = Y_PLUS.index(i if moves == 1 else MIRROR_Y[i])
+                moving[pl.ds(16 * n + (column + 2) % 4, 4, stride=4), :] = value
+            else:
+                still[pl.ds(8 * Y_FLAT.index(i) + 2 - column, 4, stride=2), :] = value
+    ghost_moving[...] = jnp.transpose(moving[...])
+    ghost_still[...] = jnp.transpose(still[...])
+
+    def inlet(row, outside_rows):
         us = [INLET * flow[pl.ds(rows * c + row, 8), :] for c in range(3)]
         eq = inlet_state(*us)
-        for x in range(4):
-            solid = solidp[x, pl.ds(row, 8), :] > 0.5
-            g = [gather(post, i, x, row, first_left, first_right) for i in range(19)]
-            if x == 0:
-                g = [jnp.where(solid, g[i], eq[i]) for i in range(19)]
-            p = collide(g, solid)
-            for i in range(19):
-                value = p[i]
-                if outside_rows is not None:
-                    value = jnp.where(outside_rows, 0.0, value)
-                post2[i, x, pl.ds(store_row, 8), :] = value
-
-    step_one(PAD - 1, PAD - 1, (sub == 0) & (kz == 0))
-    step_one(top - 7, top - 7, (sub == 7) & (kz == nz - 1))
+        solid = solidp[0, pl.ds(row, 8), :] > 0.5
+        for i in range(19):
+            j = OPP[i]
+            source = streamed(j, 0)
+            if source is None:
+                value = jnp.where(solid, 0.0, eq[i])
+            else:
+                value = jnp.where(solid, post[j, source, pl.ds(row - DIRS[j][2], 8), :], eq[i])
+            if outside_rows is not None:
+                value = jnp.where(outside_rows, 0.0, value)
+            if DIRS[i][1]:
+                value = pltpu.roll(value, DIRS[i][1] % 128, 1)
+            inlet2[i, pl.ds(row, 8), :] = value
 
     def out_copy(t):
         at = pl.ds(pl.multiple_of(t * 8, 8), 8)
@@ -478,20 +493,48 @@
         row = pl.multiple_of(t * 8 + PAD, 8)
         us = [INLET * flow[pl.ds(rows * c + row, 8), :] for c in range(3)]
         eq = inlet_state(*us)
-        for x in range(4):
-            solid = solidp[x, pl.ds(row, 8), :] > 0.5
-            for i in range(19):
-                g = gather(post2, i, x, row, second_left, second_right)
-                if x == 0:
-                    g = jnp.where(solid, g, eq[i])
-                state[i, x, pl.ds(row - PAD, 8), :] = g
+        solid = solidp[0, pl.ds(row, 8), :] > 0.5
+        ends = (lane == 0) | (lane == 127)
+
+        def read(i, source, ghost):
+            at = pl.ds(row - DIRS[i][2], 8)
+            v = inlet2[i, at, :] if source == 0 else post2[i, source - 1, at, :]
+            where = ends if DIRS[i][1] == 0 else (lane < 2 if DIRS[i][1] == 1 else lane >= 126)
+            return jnp.where(where, ghost, v)
+
+        def write(i, x, value):
+            if x == 0:
+                value = jnp.where(solid, value, eq[i])
+            state[i, x, pl.ds(row - PAD, 8), :] = value
+
+        for i in Y_FLAT + Y_PLUS:
+            both = [i] if DIRS[i][1] == 0 else [i, MIRROR_Y[i]]
+            at = pl.ds(row - DIRS[i][2], 8)
+            for source in range(4):
+                targets = [x for x in range(4) if streamed(i, x) == source]
+                if not targets:
+                    continue
+                if DIRS[i][1] == 0:
+                    slot = 2 * (4 * Y_FLAT.index(i) + source)
+                    ghost = pltpu.roll(ghost_still[at, :], (127 - slot) % 128, 1)
+                else:
+                    slot = 4 * (4 * Y_PLUS.index(i) + source)
+                    ghost = pltpu.roll(ghost_moving[at, :], (126 - slot) % 128, 1)
+                for j in both:
+                    value = read(j, source, ghost)
+                    for x in targets:
+                        write(j, x, value)
+            for j in both:
+                if streamed(j, 0) is None:
+                    write(j, 0, jnp.zeros((8, 128), jnp.float32))
         out_copy(t).start()
 
-    step_one(PAD, PAD, None)
+    inlet(PAD - 1, (sub == 0) & (kz == 0))
+    inlet(top - 7, (sub == 7) & (kz == nz - 1))
+    inlet(PAD, None)
 
     def main(t, carry):
-        row = pl.multiple_of(t * 8 + PAD, 8)
-        step_one(row, row, None)
+        inlet(pl.multiple_of(t * 8 + PAD, 8), None)
         last(t - 1)
         return carry
 
@@ -554,9 +597,7 @@
     dma = pltpu.SemaphoreType.DMA
     here = lambda value: pltpu.with_memory_space_constraint(value, pltpu.HBM)
     mean_profile = mean_profile.reshape(1, height)
-    noise, mean_profile, lund_diag, lund_off, populations, mask = map(
-        here, (noise, mean_profile, lund_diag, lund_off, populations, mask)
-    )
+    operands = populations, mask, noise, mean_profile, lund_diag, lund_off
 
     za, zb, z2 = pl.pallas_call(
         lambda *refs: edge_kernel(nz, *refs),
@@ -569,7 +610,7 @@
         ],
         compiler_params=params(8),
         name="edge_rows",
-    )(populations, mask, noise, mean_profile, lund_diag, lund_off)
+    )(*map(here, operands))
 
     ra = lax.ppermute(za, "gz", swap_pairs(nz, 0))
     rb = lax.ppermute(zb, "gz", swap_pairs(nz, 1))
@@ -580,10 +621,9 @@
     post, solidp, right_cols, left_cols = pl.pallas_call(
         lambda *refs: bulk_kernel(nz, *refs),
         out_shape=(f32(19, 4, rows, 128), f32(4, rows, 128), f32(rows, 128), f32(rows, 128)),
-        in_specs=hbm(2),
+        in_specs=vm(2),
         out_specs=vm(4),
-        scratch_shapes=[scratch(19, 4, height, 128), flags(4, height, 128), dma((5,))],
-        compiler_params=params(8),
+        compiler_params=params(4),
         cost_estimate=cost(4_000_000_000, 8_000_000),
         name="bulk",
     )(populations, mask)
@@ -599,7 +639,9 @@
         ),
         in_specs=vm(10),
         out_specs=vm(6),
-        scratch_shapes=[scratch(3 * height, 384), scratch(rows, 384)],
+        scratch_shapes=[
+            scratch(3 * height, 384), scratch(rows, 384), scratch(3, 2, ROW_PARAM, 128),
+        ],
         input_output_aliases={0: 0, 1: 1},
         compiler_params=params(4),
         name="columns",
@@ -612,24 +654,35 @@
     left = np.arange(128) % 64 - 64
     right = np.arange(128) % 64 + span
     source = np.concatenate([own, left, right])
-    wy = band(source, own)
+    wy = jnp.asarray(band(source, own))
     wg = np.zeros((8, 384), np.float32)
-    wg[0:2] = band(source, np.array([-1, span])).T
+    wg[0:4] = band(source, np.array([-1, 0, span - 1, span])).T
+    wg = jnp.asarray(wg)
+    post2, flow_own, ghost_own, own_right, own_left = pl.pallas_call(
+        lambda *refs: interior_kernel(nz, *refs),
+        out_shape=(
+            f32(19, 3, rows, 128), f32(3 * rows, 128), f32(24, 128), f32(144, 128), f32(144, 128),
+        ),
+        in_specs=vm(7),
+        out_specs=vm(5),
+        compiler_params=params(4),
+        cost_estimate=cost(4_000_000_000, 8_000_000),
+        name="interior",
+    )(post, solidp, linear, ya, yb, wy, wg)
     inflow, state = pl.pallas_call(
         lambda *refs: final_kernel(nz, *refs),
         out_shape=(f32(3, height, span), f32(19, 4, height, span)),
-        in_specs=vm(10),
+        in_specs=vm(12),
         out_specs=hbm(2),
         scratch_shapes=[
-            scratch(3 * rows, 384), scratch(3 * rows, 128), scratch(19, 4, rows, 128),
-            scratch(128, 128), scratch(128, 128), scratch(128, 128), scratch(128, 128),
-            scratch(16, 128), scratch(16, 128), scratch(128, 128), scratch(128, 128),
-            scratch(rows, 128), scratch(rows, 128), scratch(19, 4, height, span),
+            scratch(3 * rows, 256), scratch(3 * rows, 128), scratch(19, rows, 128),
+            scratch(144, 128), scratch(144, 128), scratch(128, 128), scratch(128, 128),
+            scratch(128, 128), scratch(128, 128), scratch(19, 4, height, span),
             scratch(3, height, span), dma((height // 8 + 1,)),
         ],
-        compiler_params=params(12),
+        compiler_params=params(8),
         name="stream",
-    )(post, solidp, linear, meanrow, ya, yb, qa, qb, jnp.asarray(wy), jnp.asarray(wg))
+    )(post, solidp, post2, flow_own, ghost_own, own_right, own_left, meanrow, qa, qb, wy, wg)
     return inflow, state
 
 

time: 27 us -> 22.4 us (0.83)
  Pallas kernels: 12.8 us -> 8.57 us
  waiting for transfers between devices: 2.99 us -> 2.59 us
    pallas_call x1, Pallas kernels: 5.76 us -> 1.87 us  [shards(): pl.pallas_call(lambda *refs: bulk_kernel(nz, *refs), out_shape=(f32(19, 4...]
    pallas_call x1, Pallas kernels: 4.77 us -> 2.45 us  [shards(): pl.pallas_call(lambda *refs: final_kernel(nz, *refs), out_shape=(f32(3, h...]
    ppermute x1, waiting for transfers between devices: 2.98 us -> 1.03 us  [shards(): qb = lax.ppermute(yb, ('gy', 'col'), ring_pairs(ny, 1))]
    pallas_call x0 -> x1, Pallas kernels: none -> 1.92 us  [shards(): pl.pallas_call(lambda *refs: interior_kernel(nz, *refs), out_shape=(f32(1...]
    ppermute x1, waiting for transfers between devices: 0.01 us -> 1.55 us  [shards(): ra = lax.ppermute(za, 'gz', swap_pairs(nz, 0))]
  transfers between devices with their start and end apart: 5 -> 5, of which waited for: 1 -> 2; matrix products, arithmetic and copies ran while one was open for 0% -> 0% of each run, Pallas kernels for 22% -> 17%
where the time goes in v2:
time: 22.4 us; the launch traced here: 22.2 us
  starting transfers between devices  10.3 us (46%)
  Pallas kernels  8.57 us (38%)
  waiting for transfers between devices  2.59 us (12%)
  between operations  0.74 us (3%)
    ppermute x1, starting transfers between devices, shards(): rc = lax.ppermute(z2, 'gz', swap_pairs(nz, 0, 2))  4.1 us
    ppermute x1, starting transfers between devices, shards(): ra = lax.ppermute(za, 'gz', swap_pairs(nz, 0))  2.89 us
    ppermute x1, starting transfers between devices, shards(): qb = lax.ppermute(yb, ('gy', 'col'), ring_pairs(ny, 1))  2.55 us
    pallas_call x1, Pallas kernels, shards(): pl.pallas_call(lambda *refs: final_kernel(nz, *refs), out_shape=(f32(3, h...  2.45 us
    pallas_call x1, Pallas kernels, shards(): pl.pallas_call(lambda *refs: interior_kernel(nz, *refs), out_shape=(f32(1...  1.92 us
    pallas_call x1, Pallas kernels, shards(): pl.pallas_call(lambda *refs: bulk_kernel(nz, *refs), out_shape=(f32(19, 4...  1.87 us
    pallas_call x1, Pallas kernels, shards(): pl.pallas_call(lambda *refs: edge_kernel(nz, *refs), out_shape=(f32(messa...  1.63 us
    ppermute x1, waiting for transfers between devices, shards(): ra = lax.ppermute(za, 'gz', swap_pairs(nz, 0))  1.55 us
  transfers between devices with their start and end apart: 5, of which 2 were waited for; matrix products, arithmetic and copies ran while one was open for 0% of the time, Pallas kernels for 17%

profile of v2, /device:TPU:0, one launch (start us, length us, event | category | flops | bytes accessed | tf_op | source)
XLA Modules:
  0.0 22.2 jit_solution(8232396211460444491)
XLA Ops:
  0.6 0.0 copy-start.2
  0.6 0.0 copy-start
  0.7 1.6 %edge_rows.1 = (f32[280,128]{1,0:T(8,128)S(1)}, f32[280,128]{1,0:T(8,128)S(1)}, f32[16,128]{1,0:T(8,128)S(1)}) custom-call(f32[19,4,64,128]{3,2,1,0:T(8,128)} %refs_0_.3, s32[4,64,128]{2,1,0:T(8,128)} %refs_1_.3, f32[3,64,128]{2,1,0:T(8,128)} %refs_2_.1, f32[1,64]{1,0:T(1,128)} %bitcast.1, f32[3,64]{1,0:T(4,128)} %refs_4_.1, f32[3,64]{1,0:T(4,128)} %refs_5_.2), custom_call_target="tpu_custom_call" | custom-call | tf_op jit(solution)/shard_map/edge_rows/pallas_call | solution.py:602
  2.3 4.1 %collective-permute-start.2 = (f32[16,128]{1,0:T(8,128)S(1)}, f32[16,128]{1,0:T(8,128)S(1)}, u32[]{:S(2)}, u32[]{:S(2)}) collective-permute-start(f32[16,128]{1,0:T(8,128)S(1)} %get-tuple-element.26), channel_id=1, source_target_pairs={{0,4},{2,6},{4,0},{6,2},{1,5},{3,7},{5,1},{7,3},{8,12},{10,14},{12... | collective-permute-start | bytes 24584 | tf_op jit(solution)/shard_map/ppermute | solution.py:617
  6.4 0.7 %collective-permute-start.1 = (f32[280,128]{1,0:T(8,128)S(1)}, f32[280,128]{1,0:T(8,128)S(1)}, u32[]{:S(2)}, u32[]{:S(2)}) collective-permute-start(f32[280,128]{1,0:T(8,128)S(1)} %get-tuple-element.25), channel_id=1, source_target_pairs={{2,4},{4,2},{3,5},{5,3},{10,12},{12,10},{11,13},{13,11},{18,20},{2... | collective-permute-start | bytes 430088 | tf_op jit(solution)/shard_map/ppermute | solution.py:616
  7.1 0.0 copy-start.3
  7.1 2.9 %collective-permute-start = (f32[280,128]{1,0:T(8,128)S(1)}, f32[280,128]{1,0:T(8,128)S(1)}, u32[]{:S(2)}, u32[]{:S(2)}) collective-permute-start(f32[280,128]{1,0:T(8,128)S(1)} %get-tuple-element.24.refs_4_), channel_id=1, source_target_pairs={{0,2},{2,0},{4,6},{6,4},{1,3},{3,1},{5,7},{7,5},{8,10},{10,8},{12,... | collective-permute-start | bytes 430088 | tf_op jit(solution)/shard_map/ppermute | solution.py:615
  10.0 0.0 copy-done.2
  10.0 0.0 copy-done
  10.0 1.9 %bulk.1 = (f32[19,4,80,128]{3,2,1,0:T(8,128)S(1)}, f32[4,80,128]{2,1,0:T(8,128)S(1)}, f32[80,128]{1,0:T(8,128)S(1)}, f32[80,128]{1,0:T(8,128)S(1)}) custom-call(f32[19,4,64,128]{3,2,1,0:T(8,128)S(1)} %copy-done, s32[4,64,128]{2,1,0:T(8,128)S(1)} %copy-done.2), custom_call_target="tpu_custom_call" | custom-call | flops 4000000000 | bytes 8000000 | tf_op jit(solution)/shard_map/bulk/pallas_call | solution.py:621
  11.8 0.0 copy-start.1
  11.9 0.0 copy-start.4
  11.9 0.0 collective-permute-done.2.refs_7_
  11.9 0.0 collective-permute-done.1.refs_6_
  11.9 1.6 %collective-permute-done.refs_5_ = f32[280,128]{1,0:T(8,128)S(1)} collective-permute-done((f32[280,128]{1,0:T(8,128)S(1)}, f32[280,128]{1,0:T(8,128)S(1)}, u32[]{:S(2)}, u32[]{:S(2)}) %collective-permute-start) | collective-permute-done | bytes 143392 | tf_op jit(solution)/shard_map/ppermute | solution.py:615
  13.4 0.0 copy-done.3
  13.5 0.7 %columns.1 = (f32[19,4,80,128]{3,2,1,0:T(8,128)S(1)}, f32[4,80,128]{2,1,0:T(8,128)S(1)}, f32[200,128]{1,0:T(8,128)S(1)}, f32[200,128]{1,0:T(8,128)S(1)}, f32[4,8...) custom-call(f32[19,4,80,128]{3,2,1,0:T(8,128)S(1)} %get-tuple-element.20.refs_0_, ...), custom_call_target="tpu_custom_call", output_to_operand_aliasing={{0}: (0, {}), {1}: (1, {})} | custom-call | tf_op jit(solution)/shard_map/columns/pallas_call | solution.py:634
  14.2 0.1 collective-permute-start.3
  14.2 2.5 %collective-permute-start.4 = (f32[200,128]{1,0:T(8,128)S(1)}, f32[200,128]{1,0:T(8,128)S(1)}, u32[]{:S(2)}, u32[]{:S(2)}) collective-permute-start(f32[200,128]{1,0:T(8,128)S(1)} %get-tuple-element.31.refs_4_), channel_id=1, source_target_pairs={{0,25},{1,8},{8,1},{9,16},{16,9},{17,24},{24,17},{25,0},{2,27},{3,... | collective-permute-start | bytes 307208 | tf_op jit(solution)/shard_map/ppermute | solution.py:651
  16.8 0.0 copy-done.1
  16.8 0.0 copy-done.4
  16.8 1.9 %interior.1 = (f32[19,3,80,128]{3,2,1,0:T(8,128)S(1)}, f32[240,128]{1,0:T(8,128)S(1)}, f32[24,128]{1,0:T(8,128)S(1)}, f32[144,128]{1,0:T(8,128)S(1)}, f32[144,128]{1,0:T(8,128)S(1)}) custom-call(f32[19,4,80,128]{3,2,1,0:T(8,128)S(1)} %get-tuple-element.27.refs_0_, f32[4,80,128]{2,1,0:T(8,128)S(1)} %get-tuple-element.28.refs_1_, ...), custom_call_target="tpu_custom_call" | custom-call | flops 4000000000 | bytes 8000000 | tf_op jit(solution)/shard_map/interior/pallas_call | solution.py:661
  18.7 0.0 collective-permute-done.3.refs_8_
  18.7 1.0 %collective-permute-done.4.refs_9_ = f32[200,128]{1,0:T(8,128)S(1)} collective-permute-done((f32[200,128]{1,0:T(8,128)S(1)}, f32[200,128]{1,0:T(8,128)S(1)}, u32[]{:S(2)}, u32[]{:S(2)}) %collective-permute-start.4) | collective-permute-done | bytes 102432 | tf_op jit(solution)/shard_map/ppermute | solution.py:651
  19.8 2.4 %stream.1 = (f32[3,64,128]{2,1,0:T(8,128)}, f32[19,4,64,128]{3,2,1,0:T(8,128)}) custom-call(f32[19,4,80,128]{3,2,1,0:T(8,128)S(1)} %get-tuple-element.27.refs_0_, f32[4,80,128]{2,1,0:T(8,128)S(1)} %get-tuple-element.28.refs_1_, f32[19,3,80,128]{3,2,1,0:T(8,128)S(1)} %get-tuple-element.32.refs_2_, f32[240,128]{1,0:T(8,128)S(1)} %get-tuple-element.33.refs_3_, ...), custom_call_target="tpu_custom_call" | custom-call | tf_op jit(solution)/shard_map/stream/pallas_call | solution.py:672
  (1 shorter events, 0.0 us)
Async XLA Ops:
  0.6 9.3 %copy-start.2 = (s32[4,64,128]{2,1,0:T(8,128)S(1)}, s32[4,64,128]{2,1,0:T(8,128)}, u32[]{:S(2)}) copy-start(s32[4,64,128]{2,1,0:T(8,128)} %refs_1_.3) | copy-start | bytes 393220
  0.6 9.3 %copy-start = (f32[19,4,64,128]{3,2,1,0:T(8,128)S(1)}, f32[19,4,64,128]{3,2,1,0:T(8,128)}, u32[]{:S(2)}) copy-start(f32[19,4,64,128]{3,2,1,0:T(8,128)} %refs_0_.3) | copy-start | bytes 7471108
  2.3 9.6 %collective-permute-start.2 = (f32[16,128]{1,0:T(8,128)S(1)}, f32[16,128]{1,0:T(8,128)S(1)}, u32[]{:S(2)}, u32[]{:S(2)}) collective-permute-start(f32[16,128]{1,0:T(8,128)S(1)} %get-tuple-element.26), channel_id=1, source_target_pairs={{0,4},{2,6},{4,0},{6,2},{1,5},{3,7},{5,1},{7,3},{8,12},{10,14},{12... | collective-permute-start | bytes 24584 | tf_op jit(solution)/shard_map/ppermute | solution.py:617
  6.4 5.5 %collective-permute-start.1 = (f32[280,128]{1,0:T(8,128)S(1)}, f32[280,128]{1,0:T(8,128)S(1)}, u32[]{:S(2)}, u32[]{:S(2)}) collective-permute-start(f32[280,128]{1,0:T(8,128)S(1)} %get-tuple-element.25), channel_id=1, source_target_pairs={{2,4},{4,2},{3,5},{5,3},{10,12},{12,10},{11,13},{13,11},{18,20},{2... | collective-permute-start | bytes 430088 | tf_op jit(solution)/shard_map/ppermute | solution.py:616
  7.1 6.4 %copy-start.3 = (f32[80,192]{1,0:T(8,128)S(1)}, f32[80,192]{1,0:T(8,128)}, u32[]{:S(2)}) copy-start(f32[80,192]{1,0:T(8,128)} %constant.8.clone.refs_9_) | copy-start | bytes 184324
  7.1 6.4 %collective-permute-start = (f32[280,128]{1,0:T(8,128)S(1)}, f32[280,128]{1,0:T(8,128)S(1)}, u32[]{:S(2)}, u32[]{:S(2)}) collective-permute-start(f32[280,128]{1,0:T(8,128)S(1)} %get-tuple-element.24.refs_4_), channel_id=1, source_target_pairs={{0,2},{2,0},{4,6},{6,4},{1,3},{3,1},{5,7},{7,5},{8,10},{10,8},{12,... | collective-permute-start | bytes 430088 | tf_op jit(solution)/shard_map/ppermute | solution.py:615
  11.8 4.9 %copy-start.1 = (f32[384,128]{1,0:T(8,128)S(1)}, f32[384,128]{1,0:T(8,128)}, u32[]{:S(2)}) copy-start(f32[384,128]{1,0:T(8,128)} %constant.9.clone.refs_5_.refs_10_) | copy-start | bytes 589828
  11.9 4.9 %copy-start.4 = (f32[8,384]{1,0:T(8,128)S(1)}, f32[8,384]{1,0:T(8,128)}, u32[]{:S(2)}) copy-start(f32[8,384]{1,0:T(8,128)} %constant.10.clone.refs_6_.refs_11_) | copy-start | bytes 36868
  14.2 4.6 %collective-permute-start.3 = (f32[200,128]{1,0:T(8,128)S(1)}, f32[200,128]{1,0:T(8,128)S(1)}, u32[]{:S(2)}, u32[]{:S(2)}) collective-permute-start(f32[200,128]{1,0:T(8,128)S(1)} %get-tuple-element.30.refs_3_), channel_id=1, source_target_pairs={{0,1},{1,0},{8,9},{9,8},{16,17},{17,16},{24,25},{25,24},{2,3},{3,2... | collective-permute-start | bytes 307208 | tf_op jit(solution)/shard_map/ppermute | solution.py:650
  14.2 5.5 %collective-permute-start.4 = (f32[200,128]{1,0:T(8,128)S(1)}, f32[200,128]{1,0:T(8,128)S(1)}, u32[]{:S(2)}, u32[]{:S(2)}) collective-permute-start(f32[200,128]{1,0:T(8,128)S(1)} %get-tuple-element.31.refs_4_), channel_id=1, source_target_pairs={{0,25},{1,8},{8,1},{9,16},{16,9},{17,24},{24,17},{25,0},{2,27},{3,... | collective-permute-start | bytes 307208 | tf_op jit(solution)/shard_map/ppermute | solution.py:651

commit v3 on v2

--- a/solution.py
+++ b/solution.py
@@ -33,6 +33,11 @@
 ROW_PARAM = 80
 ROW_NOISE = 88
 PAD = 8
+FIRST = PAD - 2
+Y_ROWS = 68
+Y_HALF = 34
+Y_FILTER = 72
+Y_MESSAGE = 176
 
 
 def taps():
@@ -113,7 +118,7 @@
 
 
 def edge_kernel(
-    nz, pops, mask, noise, mean, diag, off, za, zb, z2, raw, flags, mean_v, diag_v, off_v, edge, sems
+    nz, pops, mask, noise, mean, diag, off, za, zb, raw, flags, mean_v, diag_v, off_v, edge, sems
 ):
     height = pops.shape[2]
     kz = lax.axis_index("gz")
@@ -169,6 +174,10 @@
         ref[ROW_PARAM : ROW_PARAM + 1, 0:height] = mean_v[...]
         ref[ROW_PARAM + 1 : ROW_PARAM + 4, 0:height] = diag_v[...]
         ref[ROW_PARAM + 4 : ROW_PARAM + 7, 0:height] = off_v[...]
+
+
+def far_kernel(height, za, z2):
+    kz = lax.axis_index("gz")
     low_half = lax.rem(kz, 4) < 2
     z2[...] = jnp.zeros((16, 128), jnp.float32)
     for c in range(3):
@@ -233,7 +242,7 @@
 def column_kernel(
     nz, post_in, solid_in, right_in, left_in, sent, za, zb, z2c, z2d, bandz,
     post, solidp, ya, yb, linear, meanrow,
-    wide, filt, moved,
+    wide, filt, moved, ends,
 ):
     height = post.shape[2] - 2 * PAD
     rows = height + 2 * PAD
@@ -316,15 +325,17 @@
             far = LANE_FAR + c
             right = jnp.where(lane == far, pltpu.roll(v, (far - 63) % 128, 1), right)
             left = jnp.where(lane == far, pltpu.roll(v, (far - 64) % 128, 1), left)
-        ya[out, :] = jnp.where(y_even, right, left)
-        yb[out, :] = jnp.where(y_even, left, right)
-    half = rows // 2
-    lane_h = lax.broadcasted_iota(jnp.int32, (half, 128), 1)
-    for c in range(3):
-        first, second = linear[c, 0:half, :], linear[c, half:rows, :]
+        ends[0, out, :] = jnp.where(y_even, right, left)
+        ends[1, out, :] = jnp.where(y_even, left, right)
+    ya[0:Y_ROWS, :] = ends[0, FIRST : FIRST + Y_ROWS, :]
+    yb[0:Y_ROWS, :] = ends[1, FIRST : FIRST + Y_ROWS, :]
+    middle = FIRST + Y_HALF
+    lane_h = lax.broadcasted_iota(jnp.int32, (Y_HALF, 128), 1)
+    for c in range(3):
+        first, second = linear[c, FIRST:middle, :], linear[c, middle : middle + Y_HALF, :]
         left = jnp.where(lane_h < 64, first, pltpu.roll(second, 64, 1))
         right = jnp.where(lane_h < 64, pltpu.roll(first, 64, 1), second)
-        at = slice(rows + half * c, rows + half * (c + 1))
+        at = slice(Y_FILTER + Y_HALF * c, Y_FILTER + Y_HALF * (c + 1))
         ya[at, :] = jnp.where(y_even, right, left)
         yb[at, :] = jnp.where(y_even, left, right)
 
@@ -335,7 +346,7 @@
 
 
 def interior_kernel(
-    nz, post, solidp, linear, ya, yb, wy, wg, post2, flow_own, ghost_own, own_right, own_left
+    nz, post, solidp, linear, ya, yb, wy, wg, post2, flow_own, ghost_own, own_right, own_left, tall
 ):
     rows = post.shape[2]
     top = rows - PAD
@@ -369,21 +380,21 @@
     for c in range(3):
         ghost_own[8 * c : 8 * c + 8, 0:rows] = dot3(wg[:, 0:128], linear[c], NT)
         ghost_own[8 * c : 8 * c + 8, rows:128] = jnp.zeros((8, 128 - rows), jnp.float32)
-    fill = jnp.zeros((128 - rows, 128), jnp.float32)
-    a, b = ya[0:rows, :], yb[0:rows, :]
-    own_right[0:128, :] = jnp.transpose(jnp.concatenate([jnp.where(y_even, a, b), fill], axis=0))
-    own_left[0:128, :] = jnp.transpose(jnp.concatenate([jnp.where(y_even, b, a), fill], axis=0))
+    a, b = ya[0:Y_ROWS, :], yb[0:Y_ROWS, :]
+    tall[0, FIRST : FIRST + Y_ROWS, :] = jnp.where(y_even, a, b)
+    tall[1, FIRST : FIRST + Y_ROWS, :] = jnp.where(y_even, b, a)
+    own_right[0:128, :] = jnp.transpose(tall[0])
+    own_left[0:128, :] = jnp.transpose(tall[1])
 
 
 def final_kernel(
     nz, post, solidp, post2, flow_own, ghost_own, own_right, own_left, meanrow, ya, yb, wy, wg,
     inflow, state_out,
     lhs, flow, inlet2, strip_left, strip_right, moving, still, ghost_moving, ghost_still,
-    state, flow_out, sems,
+    state, flow_out, tall, sems,
 ):
     height = state.shape[2]
     rows = height + 2 * PAD
-    half = rows // 2
     top = PAD + height
     kz = lax.axis_index("gz")
     ky = lax.axis_index("gy") * lax.axis_size("col") + lax.axis_index("col")
@@ -391,17 +402,19 @@
     lane = lax.broadcasted_iota(jnp.int32, (8, 128), 1)
     sub = lax.broadcasted_iota(jnp.int32, (8, 128), 0)
 
-    fill = jnp.zeros((128 - rows, 128), jnp.float32)
-    a, b = ya[0:rows, :], yb[0:rows, :]
-    strip_left[0:128, :] = jnp.transpose(jnp.concatenate([jnp.where(y_even, b, a), fill], axis=0))
-    strip_right[0:128, :] = jnp.transpose(jnp.concatenate([jnp.where(y_even, a, b), fill], axis=0))
-
-    lane_h = lax.broadcasted_iota(jnp.int32, (half, 128), 1)
-    for c in range(3):
-        at = slice(rows + half * c, rows + half * (c + 1))
+    a, b = ya[0:Y_ROWS, :], yb[0:Y_ROWS, :]
+    tall[0, FIRST : FIRST + Y_ROWS, :] = jnp.where(y_even, b, a)
+    tall[1, FIRST : FIRST + Y_ROWS, :] = jnp.where(y_even, a, b)
+    strip_left[0:128, :] = jnp.transpose(tall[0])
+    strip_right[0:128, :] = jnp.transpose(tall[1])
+
+    lane_h = lax.broadcasted_iota(jnp.int32, (Y_HALF, 128), 1)
+    for c in range(3):
+        at = slice(Y_FILTER + Y_HALF * c, Y_FILTER + Y_HALF * (c + 1))
         a, b = ya[at, :], yb[at, :]
         left, right = jnp.where(y_even, b, a), jnp.where(y_even, a, b)
-        lo, hi = slice(rows * c, rows * c + half), slice(rows * c + half, rows * (c + 1))
+        middle = rows * c + FIRST + Y_HALF
+        lo, hi = slice(middle - Y_HALF, middle), slice(middle, middle + Y_HALF)
         lhs[lo, 0:128] = jnp.where(lane_h < 64, left, 0.0)
         lhs[hi, 0:128] = jnp.where(lane_h < 64, 0.0, left)
         lhs[lo, 128:256] = jnp.where(lane_h < 64, right, 0.0)
@@ -599,11 +612,11 @@
     mean_profile = mean_profile.reshape(1, height)
     operands = populations, mask, noise, mean_profile, lund_diag, lund_off
 
-    za, zb, z2 = pl.pallas_call(
+    za, zb = pl.pallas_call(
         lambda *refs: edge_kernel(nz, *refs),
-        out_shape=(f32(message, 128), f32(message, 128), f32(16, 128)),
+        out_shape=(f32(message, 128), f32(message, 128)),
         in_specs=hbm(6),
-        out_specs=vm(3),
+        out_specs=vm(2),
         scratch_shapes=[
             scratch(19, 4, 16, 128), flags(4, 16, 128), scratch(1, height), scratch(3, height),
             scratch(3, height), scratch(20, 4, 16, 128), dma((13,)),
@@ -611,6 +624,15 @@
         compiler_params=params(8),
         name="edge_rows",
     )(*map(here, operands))
+
+    z2 = pl.pallas_call(
+        lambda *refs: far_kernel(height, *refs),
+        out_shape=f32(16, 128),
+        in_specs=vm(1),
+        out_specs=pl.BlockSpec(memory_space=pltpu.VMEM),
+        compiler_params=params(1),
+        name="far_rows",
+    )(za)
 
     ra = lax.ppermute(za, "gz", swap_pairs(nz, 0))
     rb = lax.ppermute(zb, "gz", swap_pairs(nz, 1))
@@ -634,13 +656,14 @@
     post, solidp, ya, yb, linear, meanrow = pl.pallas_call(
         lambda *refs: column_kernel(nz, *refs),
         out_shape=(
-            f32(19, 4, rows, 128), f32(4, rows, 128), f32(rows + 3 * rows // 2, 128),
-            f32(rows + 3 * rows // 2, 128), f32(4, rows, 128), f32(8, 128),
+            f32(19, 4, rows, 128), f32(4, rows, 128), f32(Y_MESSAGE, 128), f32(Y_MESSAGE, 128),
+            f32(4, rows, 128), f32(8, 128),
         ),
         in_specs=vm(10),
         out_specs=vm(6),
         scratch_shapes=[
             scratch(3 * height, 384), scratch(rows, 384), scratch(3, 2, ROW_PARAM, 128),
+            scratch(2, rows, 128),
         ],
         input_output_aliases={0: 0, 1: 1},
         compiler_params=params(4),
@@ -665,6 +688,7 @@
         ),
         in_specs=vm(7),
         out_specs=vm(5),
+        scratch_shapes=[scratch(2, 128, 128)],
         compiler_params=params(4),
         cost_estimate=cost(4_000_000_000, 8_000_000),
         name="interior",
@@ -678,7 +702,7 @@
             scratch(3 * rows, 256), scratch(3 * rows, 128), scratch(19, rows, 128),
             scratch(144, 128), scratch(144, 128), scratch(128, 128), scratch(128, 128),
             scratch(128, 128), scratch(128, 128), scratch(19, 4, height, span),
-            scratch(3, height, span), dma((height // 8 + 1,)),
+            scratch(3, height, span), scratch(2, 128, 128), dma((height // 8 + 1,)),
         ],
         compiler_params=params(8),
         name="stream",

time: 22.4 us -> 21.9 us (0.978)
  the two profiles are of different devices: /device:TPU:0 before, /device:TPU:11 now
where the time goes in v3:
time: 21.9 us; the launch traced here: 21.7 us
  Pallas kernels  8.61 us (39%)
  starting transfers between devices  8.37 us (38%)
  waiting for transfers between devices  3.97 us (18%)
  between operations  0.74 us (3%)
    ppermute x1, starting transfers between devices, shards(): qa = lax.ppermute(ya, ('gy', 'col'), ring_pairs(ny, 0))  2.45 us
    pallas_call x1, Pallas kernels, shards(): pl.pallas_call(lambda *refs: final_kernel(nz, *refs), out_shape=(f32(3, h...  2.44 us
    ppermute x1, starting transfers between devices, shards(): rc = lax.ppermute(z2, 'gz', swap_pairs(nz, 0, 2))  2.31 us
    ppermute x1, starting transfers between devices, shards(): rb = lax.ppermute(zb, 'gz', swap_pairs(nz, 1))  2.2 us
    ppermute x1, waiting for transfers between devices, shards(): qb = lax.ppermute(yb, ('gy', 'col'), ring_pairs(ny, 1))  2.14 us
    pallas_call x1, Pallas kernels, shards(): pl.pallas_call(lambda *refs: interior_kernel(nz, *refs), out_shape=(f32(1...  1.93 us
    pallas_call x1, Pallas kernels, shards(): pl.pallas_call(lambda *refs: bulk_kernel(nz, *refs), out_shape=(f32(19, 4...  1.88 us
    ppermute x1, waiting for transfers between devices, shards(): rb = lax.ppermute(zb, 'gz', swap_pairs(nz, 1))  1.82 us
  transfers between devices with their start and end apart: 5, of which 2 were waited for; matrix products, arithmetic and copies ran while one was open for 0% of the time, Pallas kernels for 18%

profile of v3, /device:TPU:11, one launch (start us, length us, event | category | flops | bytes accessed | tf_op | source)
XLA Modules:
  0.0 21.7 jit_solution(16689168807191379263)
XLA Ops:
  0.6 0.0 copy-start.2
  0.6 0.0 copy-start
  0.7 1.6 %edge_rows.1 = (f32[280,128]{1,0:T(8,128)S(1)}, f32[280,128]{1,0:T(8,128)S(1)}) custom-call(f32[19,4,64,128]{3,2,1,0:T(8,128)} %refs_0_.3, s32[4,64,128]{2,1,0:T(8,128)} %refs_1_.3, f32[3,64,128]{2,1,0:T(8,128)} %refs_2_.1, f32[1,64]{1,0:T(1,128)} %bitcast.1, f32[3,64]{1,0:T(4,128)} %refs_4_.1, f32[3,64]{1,0:T(4,128)} %refs_5_.2), custom_call_target="tpu_custom_call" | custom-call | tf_op jit(solution)/shard_map/edge_rows/pallas_call | solution.py:615
  2.3 0.2 %collective-permute-start = (f32[280,128]{1,0:T(8,128)S(1)}, f32[280,128]{1,0:T(8,128)S(1)}, u32[]{:S(2)}, u32[]{:S(2)}) collective-permute-start(f32[280,128]{1,0:T(8,128)S(1)} %get-tuple-element.23.refs_0_.refs_4_), channel_id=1, source_target_pairs={{0,2},{2,0},{4,6},{6,4},{1,3},{3,1},{5,7},{7,5},{8,10},{10,8},{12,... | collective-permute-start | bytes 430088 | tf_op jit(solution)/shard_map/ppermute | solution.py:637
  2.5 2.3 %collective-permute-start.2 = (f32[16,128]{1,0:T(8,128)S(1)}, f32[16,128]{1,0:T(8,128)S(1)}, u32[]{:S(2)}, u32[]{:S(2)}) collective-permute-start(f32[16,128]{1,0:T(8,128)S(1)} %far_rows.1), channel_id=1, source_target_pairs={{0,4},{2,6},{4,0},{6,2},{1,5},{3,7},{5,1},{7,3},{8,12},{10,14},{12... | collective-permute-start | bytes 24584 | tf_op jit(solution)/shard_map/ppermute | solution.py:639
  4.8 0.0 copy-start.3
  4.8 2.2 %collective-permute-start.1 = (f32[280,128]{1,0:T(8,128)S(1)}, f32[280,128]{1,0:T(8,128)S(1)}, u32[]{:S(2)}, u32[]{:S(2)}) collective-permute-start(f32[280,128]{1,0:T(8,128)S(1)} %get-tuple-element.24), channel_id=1, source_target_pairs={{2,4},{4,2},{3,5},{5,3},{10,12},{12,10},{11,13},{13,11},{18,20},{2... | collective-permute-start | bytes 430088 | tf_op jit(solution)/shard_map/ppermute | solution.py:638
  7.0 0.0 copy-done.2
  7.1 0.0 copy-done
  7.1 1.9 %bulk.1 = (f32[19,4,80,128]{3,2,1,0:T(8,128)S(1)}, f32[4,80,128]{2,1,0:T(8,128)S(1)}, f32[80,128]{1,0:T(8,128)S(1)}, f32[80,128]{1,0:T(8,128)S(1)}) custom-call(f32[19,4,64,128]{3,2,1,0:T(8,128)S(1)} %copy-done, s32[4,64,128]{2,1,0:T(8,128)S(1)} %copy-done.2), custom_call_target="tpu_custom_call" | custom-call | flops 4000000000 | bytes 8000000 | tf_op jit(solution)/shard_map/bulk/pallas_call | solution.py:643
  8.9 0.0 copy-start.1
  9.0 0.0 copy-start.4
  9.0 0.0 collective-permute-done.2.refs_7_
  9.0 1.8 %collective-permute-done.1.refs_6_ = f32[280,128]{1,0:T(8,128)S(1)} collective-permute-done((f32[280,128]{1,0:T(8,128)S(1)}, f32[280,128]{1,0:T(8,128)S(1)}, u32[]{:S(2)}, u32[]{:S(2)}) %collective-permute-start.1) | collective-permute-done | bytes 143392 | tf_op jit(solution)/shard_map/ppermute | solution.py:638
  10.8 0.0 collective-permute-done.refs_5_
  10.8 0.0 copy-done.3
  10.8 0.7 %columns.1 = (f32[19,4,80,128]{3,2,1,0:T(8,128)S(1)}, f32[4,80,128]{2,1,0:T(8,128)S(1)}, f32[176,128]{1,0:T(8,128)S(1)}, f32[176,128]{1,0:T(8,128)S(1)}, f32[4,8...) custom-call(f32[19,4,80,128]{3,2,1,0:T(8,128)S(1)} %get-tuple-element.19.refs_0_, ...), custom_call_target="tpu_custom_call", output_to_operand_aliasing={{0}: (0, {}), {1}: (1, {})} | custom-call | tf_op jit(solution)/shard_map/columns/pallas_call | solution.py:656
  11.5 2.5 %collective-permute-start.3 = (f32[176,128]{1,0:T(8,128)S(1)}, f32[176,128]{1,0:T(8,128)S(1)}, u32[]{:S(2)}, u32[]{:S(2)}) collective-permute-start(f32[176,128]{1,0:T(8,128)S(1)} %get-tuple-element.28.refs_3_), channel_id=1, source_target_pairs={{0,1},{1,0},{8,9},{9,8},{16,17},{17,16},{24,25},{25,24},{2,3},{3,2... | collective-permute-start | bytes 270344 | tf_op jit(solution)/shard_map/ppermute | solution.py:673
  14.0 1.2 %collective-permute-start.4 = (f32[176,128]{1,0:T(8,128)S(1)}, f32[176,128]{1,0:T(8,128)S(1)}, u32[]{:S(2)}, u32[]{:S(2)}) collective-permute-start(f32[176,128]{1,0:T(8,128)S(1)} %get-tuple-element.29.refs_4_), channel_id=1, source_target_pairs={{0,25},{1,8},{8,1},{9,16},{16,9},{17,24},{24,17},{25,0},{2,27},{3,... | collective-permute-start | bytes 270344 | tf_op jit(solution)/shard_map/ppermute | solution.py:674
  15.2 0.0 copy-done.1
  15.2 0.0 copy-done.4
  15.2 1.9 %interior.1 = (f32[19,3,80,128]{3,2,1,0:T(8,128)S(1)}, f32[240,128]{1,0:T(8,128)S(1)}, f32[24,128]{1,0:T(8,128)S(1)}, f32[144,128]{1,0:T(8,128)S(1)}, f32[144,128]{1,0:T(8,128)S(1)}) custom-call(f32[19,4,80,128]{3,2,1,0:T(8,128)S(1)} %get-tuple-element.25.refs_0_, f32[4,80,128]{2,1,0:T(8,128)S(1)} %get-tuple-element.26.refs_1_, ...), custom_call_target="tpu_custom_call" | custom-call | flops 4000000000 | bytes 8000000 | tf_op jit(solution)/shard_map/interior/pallas_call | solution.py:684
  17.1 0.0 collective-permute-done.3.refs_8_
  17.1 2.1 %collective-permute-done.4.refs_9_ = f32[176,128]{1,0:T(8,128)S(1)} collective-permute-done((f32[176,128]{1,0:T(8,128)S(1)}, f32[176,128]{1,0:T(8,128)S(1)}, u32[]{:S(2)}, u32[]{:S(2)}) %collective-permute-start.4) | collective-permute-done | bytes 90144 | tf_op jit(solution)/shard_map/ppermute | solution.py:674
  19.3 2.4 %stream.1 = (f32[3,64,128]{2,1,0:T(8,128)}, f32[19,4,64,128]{3,2,1,0:T(8,128)}) custom-call(f32[19,4,80,128]{3,2,1,0:T(8,128)S(1)} %get-tuple-element.25.refs_0_, f32[4,80,128]{2,1,0:T(8,128)S(1)} %get-tuple-element.26.refs_1_, f32[19,3,80,128]{3,2,1,0:T(8,128)S(1)} %get-tuple-element.30.refs_2_, f32[240,128]{1,0:T(8,128)S(1)} %get-tuple-element.31.refs_3_, ...), custom_call_target="tpu_custom_call" | custom-call | tf_op jit(solution)/shard_map/stream/pallas_call | solution.py:696
  (2 shorter events, 0.0 us)
Async XLA Ops:
  0.6 6.4 %copy-start.2 = (s32[4,64,128]{2,1,0:T(8,128)S(1)}, s32[4,64,128]{2,1,0:T(8,128)}, u32[]{:S(2)}) copy-start(s32[4,64,128]{2,1,0:T(8,128)} %refs_1_.3) | copy-start | bytes 393220
  0.6 6.4 %copy-start = (f32[19,4,64,128]{3,2,1,0:T(8,128)S(1)}, f32[19,4,64,128]{3,2,1,0:T(8,128)}, u32[]{:S(2)}) copy-start(f32[19,4,64,128]{3,2,1,0:T(8,128)} %refs_0_.3) | copy-start | bytes 7471108
  2.3 8.5 %collective-permute-start = (f32[280,128]{1,0:T(8,128)S(1)}, f32[280,128]{1,0:T(8,128)S(1)}, u32[]{:S(2)}, u32[]{:S(2)}) collective-permute-start(f32[280,128]{1,0:T(8,128)S(1)} %get-tuple-element.23.refs_0_.refs_4_), channel_id=1, source_target_pairs={{0,2},{2,0},{4,6},{6,4},{1,3},{3,1},{5,7},{7,5},{8,10},{10,8},{12,... | collective-permute-start | bytes 430088 | tf_op jit(solution)/shard_map/ppermute | solution.py:637
  2.5 6.4 %collective-permute-start.2 = (f32[16,128]{1,0:T(8,128)S(1)}, f32[16,128]{1,0:T(8,128)S(1)}, u32[]{:S(2)}, u32[]{:S(2)}) collective-permute-start(f32[16,128]{1,0:T(8,128)S(1)} %far_rows.1), channel_id=1, source_target_pairs={{0,4},{2,6},{4,0},{6,2},{1,5},{3,7},{5,1},{7,3},{8,12},{10,14},{12... | collective-permute-start | bytes 24584 | tf_op jit(solution)/shard_map/ppermute | solution.py:639
  4.8 6.0 %copy-start.3 = (f32[80,192]{1,0:T(8,128)S(1)}, f32[80,192]{1,0:T(8,128)}, u32[]{:S(2)}) copy-start(f32[80,192]{1,0:T(8,128)} %constant.8.clone.refs_9_) | copy-start | bytes 184324
  4.8 6.0 %collective-permute-start.1 = (f32[280,128]{1,0:T(8,128)S(1)}, f32[280,128]{1,0:T(8,128)S(1)}, u32[]{:S(2)}, u32[]{:S(2)}) collective-permute-start(f32[280,128]{1,0:T(8,128)S(1)} %get-tuple-element.24), channel_id=1, source_target_pairs={{2,4},{4,2},{3,5},{5,3},{10,12},{12,10},{11,13},{13,11},{18,20},{2... | collective-permute-start | bytes 430088 | tf_op jit(solution)/shard_map/ppermute | solution.py:638
  8.9 6.2 %copy-start.1 = (f32[384,128]{1,0:T(8,128)S(1)}, f32[384,128]{1,0:T(8,128)}, u32[]{:S(2)}) copy-start(f32[384,128]{1,0:T(8,128)} %constant.9.clone.refs_5_.refs_10_) | copy-start | bytes 589828
  9.0 6.2 %copy-start.4 = (f32[8,384]{1,0:T(8,128)S(1)}, f32[8,384]{1,0:T(8,128)}, u32[]{:S(2)}) copy-start(f32[8,384]{1,0:T(8,128)} %constant.10.clone.refs_6_.refs_11_) | copy-start | bytes 36868
  11.5 5.6 %collective-permute-start.3 = (f32[176,128]{1,0:T(8,128)S(1)}, f32[176,128]{1,0:T(8,128)S(1)}, u32[]{:S(2)}, u32[]{:S(2)}) collective-permute-start(f32[176,128]{1,0:T(8,128)S(1)} %get-tuple-element.28.refs_3_), channel_id=1, source_target_pairs={{0,1},{1,0},{8,9},{9,8},{16,17},{17,16},{24,25},{25,24},{2,3},{3,2... | collective-permute-start | bytes 270344 | tf_op jit(solution)/shard_map/ppermute | solution.py:673
  14.0 5.3 %collective-permute-start.4 = (f32[176,128]{1,0:T(8,128)S(1)}, f32[176,128]{1,0:T(8,128)S(1)}, u32[]{:S(2)}, u32[]{:S(2)}) collective-permute-start(f32[176,128]{1,0:T(8,128)S(1)} %get-tuple-element.29.refs_4_), channel_id=1, source_target_pairs={{0,25},{1,8},{8,1},{9,16},{16,9},{17,24},{24,17},{25,0},{2,27},{3,... | collective-permute-start | bytes 270344 | tf_op jit(solution)/shard_map/ppermute | solution.py:674

commit v4 on v3

--- a/solution.py
+++ b/solution.py
@@ -27,17 +27,16 @@
 Y_PLUS = [i for i in range(19) if DIRS[i][1] == 1]
 FLAG_PLANE = 4 * len(Y_FLAT)
 LANE_PLUS = 2 * FLAG_PLANE + 8
-LANE_FAR = LANE_PLUS + 8 * len(Y_PLUS)
 
 ROW_SOLID = 76
 ROW_PARAM = 80
 ROW_NOISE = 88
 PAD = 8
 FIRST = PAD - 2
-Y_ROWS = 68
 Y_HALF = 34
-Y_FILTER = 72
-Y_MESSAGE = 176
+Y_FAR = 2
+Y_FILTER = 8
+Y_MESSAGE = 112
 
 
 def taps():
@@ -206,9 +205,11 @@
     return jnp.where(pair == slot, pltpu.roll(value, (2 * slot - first_column) % 128, 1), into)
 
 
-def bulk_kernel(nz, pops, mask, post, solidp, right_cols, left_cols):
+def bulk_kernel(nz, pops, mask, post, solidp, ya, yb):
     height = pops.shape[2]
     kz = lax.axis_index("gz")
+    ky = lax.axis_index("gy") * lax.axis_size("col") + lax.axis_index("col")
+    y_even = lax.rem(ky, 2) == 0
     pair = lax.broadcasted_iota(jnp.int32, (8, 128), 1) // 2
 
     def body(t, carry):
@@ -232,17 +233,19 @@
                 post[j, x, out, :] = pltpu.roll(p[j], 127, 1)
                 right = put_pair(pair, slot, p[i], 126, right)
                 left = put_pair(pair, slot, p[j], 0, left)
-        right_cols[out, :] = jnp.where(pair < LANE_PLUS // 2, flat, right)
-        left_cols[out, :] = jnp.where(pair < LANE_PLUS // 2, flat, left)
+        right = jnp.where(pair < LANE_PLUS // 2, flat, right)
+        left = jnp.where(pair < LANE_PLUS // 2, flat, left)
+        ya[pl.ds(row, 8), :] = jnp.where(y_even, right, left)
+        yb[pl.ds(row, 8), :] = jnp.where(y_even, left, right)
         return carry
 
     lax.fori_loop(0, height // 8, body, 0)
 
 
 def column_kernel(
-    nz, post_in, solid_in, right_in, left_in, sent, za, zb, z2c, z2d, bandz,
+    nz, post_in, solid_in, sent, za, zb, z2c, z2d, bandz, pick,
     post, solidp, ya, yb, linear, meanrow,
-    wide, filt, moved, ends,
+    wide, filt, moved,
 ):
     height = post.shape[2] - 2 * PAD
     rows = height + 2 * PAD
@@ -304,31 +307,31 @@
     linear[3] = jnp.broadcast_to(cols[:, 0:1], (rows, 128))
 
     pair = lane // 2
-    for row in range(0, rows, 8):
+    for row in (0, rows - 8):
         out = slice(row, row + 8)
-        if row == 0 or row == rows - 8:
-            flat = right = left = jnp.zeros((8, 128), jnp.float32)
-            for x in range(4):
-                flat = put_pair(pair, FLAG_PLANE + x, solidp[x, out, :], 127, flat)
-                for q, i in enumerate(Y_FLAT):
-                    flat = put_pair(pair, 4 * q + x, post[i, x, out, :], 127, flat)
-                for n, i in enumerate(Y_PLUS):
-                    slot = LANE_PLUS // 2 + 4 * n + x
-                    right = put_pair(pair, slot, post[i, x, out, :], 127, right)
-                    left = put_pair(pair, slot, post[MIRROR_Y[i], x, out, :], 127, left)
-            right = jnp.where(pair < LANE_PLUS // 2, flat, right)
-            left = jnp.where(pair < LANE_PLUS // 2, flat, left)
-        else:
-            right, left = right_in[out, :], left_in[out, :]
-        for c in range(3):
-            v = linear[c, out, :]
-            far = LANE_FAR + c
-            right = jnp.where(lane == far, pltpu.roll(v, (far - 63) % 128, 1), right)
-            left = jnp.where(lane == far, pltpu.roll(v, (far - 64) % 128, 1), left)
-        ends[0, out, :] = jnp.where(y_even, right, left)
-        ends[1, out, :] = jnp.where(y_even, left, right)
-    ya[0:Y_ROWS, :] = ends[0, FIRST : FIRST + Y_ROWS, :]
-    yb[0:Y_ROWS, :] = ends[1, FIRST : FIRST + Y_ROWS, :]
+        flat = right = left = jnp.zeros((8, 128), jnp.float32)
+        for x in range(4):
+            flat = put_pair(pair, FLAG_PLANE + x, solidp[x, out, :], 127, flat)
+            for q, i in enumerate(Y_FLAT):
+                flat = put_pair(pair, 4 * q + x, post[i, x, out, :], 127, flat)
+            for n, i in enumerate(Y_PLUS):
+                slot = LANE_PLUS // 2 + 4 * n + x
+                right = put_pair(pair, slot, post[i, x, out, :], 127, right)
+                left = put_pair(pair, slot, post[MIRROR_Y[i], x, out, :], 127, left)
+        right = jnp.where(pair < LANE_PLUS // 2, flat, right)
+        left = jnp.where(pair < LANE_PLUS // 2, flat, left)
+        at = slice(0, 2) if row else slice(6, 8)
+        ya[at, :] = jnp.where(y_even, right, left)[at, :]
+        yb[at, :] = jnp.where(y_even, left, right)[at, :]
+    spare = jnp.zeros((1, 128), jnp.float32)
+    for c in range(3):
+        far = dot3(pick[...], linear[c], NT)
+        far = jnp.concatenate([far, jnp.zeros((8, 128 - rows), jnp.float32)], axis=1)
+        ya[Y_FAR + c : Y_FAR + c + 1, :] = jnp.where(y_even, far[0:1, :], far[1:2, :])
+        yb[Y_FAR + c : Y_FAR + c + 1, :] = jnp.where(y_even, far[1:2, :], far[0:1, :])
+    for ref in (ya, yb):
+        ref[5:6, :] = spare
+        ref[Y_FILTER + 3 * Y_HALF : Y_MESSAGE, :] = jnp.zeros((2, 128), jnp.float32)
     middle = FIRST + Y_HALF
     lane_h = lax.broadcasted_iota(jnp.int32, (Y_HALF, 128), 1)
     for c in range(3):
@@ -345,8 +348,19 @@
     return None if source < 0 else min(source, 3)
 
 
+def assemble(tall, sa, sb, ya, yb, a_first):
+    end = PAD + sa.shape[0]
+    for out, source, a, b in (
+        (slice(PAD, end), slice(0, sa.shape[0]), sa, sb),
+        (slice(PAD - 2, PAD), slice(6, 8), ya, yb),
+        (slice(end, end + 2), slice(0, 2), ya, yb),
+    ):
+        tall[0, out, :] = jnp.where(a_first, a[source, :], b[source, :])
+        tall[1, out, :] = jnp.where(a_first, b[source, :], a[source, :])
+
+
 def interior_kernel(
-    nz, post, solidp, linear, ya, yb, wy, wg, post2, flow_own, ghost_own, own_right, own_left, tall
+    nz, post, solidp, linear, sa, sb, ya, yb, wy, wg, post2, flow_own, ghost_own, own_right, own_left, tall
 ):
     rows = post.shape[2]
     top = rows - PAD
@@ -380,15 +394,13 @@
     for c in range(3):
         ghost_own[8 * c : 8 * c + 8, 0:rows] = dot3(wg[:, 0:128], linear[c], NT)
         ghost_own[8 * c : 8 * c + 8, rows:128] = jnp.zeros((8, 128 - rows), jnp.float32)
-    a, b = ya[0:Y_ROWS, :], yb[0:Y_ROWS, :]
-    tall[0, FIRST : FIRST + Y_ROWS, :] = jnp.where(y_even, a, b)
-    tall[1, FIRST : FIRST + Y_ROWS, :] = jnp.where(y_even, b, a)
+    assemble(tall, sa, sb, ya, yb, y_even)
     own_right[0:128, :] = jnp.transpose(tall[0])
     own_left[0:128, :] = jnp.transpose(tall[1])
 
 
 def final_kernel(
-    nz, post, solidp, post2, flow_own, ghost_own, own_right, own_left, meanrow, ya, yb, wy, wg,
+    nz, post, solidp, post2, flow_own, ghost_own, own_right, own_left, meanrow, sa, sb, ya, yb, wy, wg,
     inflow, state_out,
     lhs, flow, inlet2, strip_left, strip_right, moving, still, ghost_moving, ghost_still,
     state, flow_out, tall, sems,
@@ -402,9 +414,7 @@
     lane = lax.broadcasted_iota(jnp.int32, (8, 128), 1)
     sub = lax.broadcasted_iota(jnp.int32, (8, 128), 0)
 
-    a, b = ya[0:Y_ROWS, :], yb[0:Y_ROWS, :]
-    tall[0, FIRST : FIRST + Y_ROWS, :] = jnp.where(y_even, b, a)
-    tall[1, FIRST : FIRST + Y_ROWS, :] = jnp.where(y_even, a, b)
+    assemble(tall, sa, sb, ya, yb, jnp.logical_not(y_even))
     strip_left[0:128, :] = jnp.transpose(tall[0])
     strip_right[0:128, :] = jnp.transpose(tall[1])
 
@@ -430,10 +440,10 @@
         g = dot3(wg[:, 128:384], lhs[rows * c : rows * (c + 1), :], NT)
         g = jnp.concatenate([g, jnp.zeros((8, 128 - rows), jnp.float32)], axis=1)
         g = g + ghost_own[8 * c : 8 * c + 8, :]
-        far = slice(LANE_FAR + c, LANE_FAR + c + 1)
+        far = slice(Y_FAR + c, Y_FAR + c + 1)
         at = [g[n : n + 1, :] for n in range(4)]
-        at[0] = at[0] + b_end * strip_left[far, :]
-        at[3] = at[3] + b_end * strip_right[far, :]
+        at[0] = at[0] + b_end * jnp.where(y_even, yb[far, :], ya[far, :])
+        at[3] = at[3] + b_end * jnp.where(y_even, ya[far, :], yb[far, :])
         if c == 0:
             at = [v + meanrow[0:1, :] for v in at]
         column_flow.append(at)
@@ -640,15 +650,20 @@
     far = swap_pairs(nz, 1, 2)
     rd = lax.ppermute(z2, "gz", far) if far else jnp.zeros_like(z2)
 
-    post, solidp, right_cols, left_cols = pl.pallas_call(
+    post, solidp, sa, sb = pl.pallas_call(
         lambda *refs: bulk_kernel(nz, *refs),
-        out_shape=(f32(19, 4, rows, 128), f32(4, rows, 128), f32(rows, 128), f32(rows, 128)),
+        out_shape=(f32(19, 4, rows, 128), f32(4, rows, 128), f32(height, 128), f32(height, 128)),
         in_specs=vm(2),
         out_specs=vm(4),
         compiler_params=params(4),
         cost_estimate=cost(4_000_000_000, 8_000_000),
         name="bulk",
     )(populations, mask)
+
+    pa = lax.ppermute(sa, ("gy", "col"), ring_pairs(ny, 0))
+    pb = lax.ppermute(sb, ("gy", "col"), ring_pairs(ny, 1))
+    pick = np.zeros((8, 128), np.float32)
+    pick[0, span - HW - 1] = pick[1, HW] = 1.0
 
     line = np.arange(rows) - PAD
     used = (line >= -1) & (line <= height)
@@ -659,16 +674,15 @@
             f32(19, 4, rows, 128), f32(4, rows, 128), f32(Y_MESSAGE, 128), f32(Y_MESSAGE, 128),
             f32(4, rows, 128), f32(8, 128),
         ),
-        in_specs=vm(10),
+        in_specs=vm(9),
         out_specs=vm(6),
         scratch_shapes=[
             scratch(3 * height, 384), scratch(rows, 384), scratch(3, 2, ROW_PARAM, 128),
-            scratch(2, rows, 128),
         ],
         input_output_aliases={0: 0, 1: 1},
         compiler_params=params(4),
         name="columns",
-    )(post, solidp, right_cols, left_cols, za, ra, rb, rc, rd, jnp.asarray(bandz, jnp.float32))
+    )(post, solidp, za, ra, rb, rc, rd, jnp.asarray(bandz, jnp.float32), jnp.asarray(pick))
 
     qa = lax.ppermute(ya, ("gy", "col"), ring_pairs(ny, 0))
     qb = lax.ppermute(yb, ("gy", "col"), ring_pairs(ny, 1))
@@ -686,17 +700,17 @@
         out_shape=(
             f32(19, 3, rows, 128), f32(3 * rows, 128), f32(24, 128), f32(144, 128), f32(144, 128),
         ),
-        in_specs=vm(7),
+        in_specs=vm(9),
         out_specs=vm(5),
         scratch_shapes=[scratch(2, 128, 128)],
         compiler_params=params(4),
         cost_estimate=cost(4_000_000_000, 8_000_000),
         name="interior",
-    )(post, solidp, linear, ya, yb, wy, wg)
+    )(post, solidp, linear, sa, sb, ya, yb, wy, wg)
     inflow, state = pl.pallas_call(
         lambda *refs: final_kernel(nz, *refs),
         out_shape=(f32(3, height, span), f32(19, 4, height, span)),
-        in_specs=vm(12),
+        in_specs=vm(14),
         out_specs=hbm(2),
         scratch_shapes=[
             scratch(3 * rows, 256), scratch(3 * rows, 128), scratch(19, rows, 128),
@@ -706,7 +720,7 @@
         ],
         compiler_params=params(8),
         name="stream",
-    )(post, solidp, post2, flow_own, ghost_own, own_right, own_left, meanrow, qa, qb, wy, wg)
+    )(post, solidp, post2, flow_own, ghost_own, own_right, own_left, meanrow, pa, pb, qa, qb, wy, wg)
     return inflow, state
 
 

time: 21.9 us -> 21.6 us (0.986)
  the two profiles are of different devices: /device:TPU:11 before, /device:TPU:0 now
where the time goes in v4:
time: 21.6 us; the launch traced here: 21.4 us
  starting transfers between devices  9.79 us (45%)
  Pallas kernels  8.55 us (40%)
  waiting for transfers between devices  2.25 us (10%)
  between operations  0.79 us (4%)
    ppermute x1, starting transfers between devices, shards(): ra = lax.ppermute(za, 'gz', swap_pairs(nz, 0))  3.09 us
    ppermute x1, starting transfers between devices, shards(): rc = lax.ppermute(z2, 'gz', swap_pairs(nz, 0, 2))  2.59 us
    ppermute x1, starting transfers between devices, shards(): pb = lax.ppermute(sb, ('gy', 'col'), ring_pairs(ny, 1))  2.55 us
    pallas_call x1, Pallas kernels, shards(): pl.pallas_call(lambda *refs: final_kernel(nz, *refs), out_shape=(f32(3, h...  2.46 us
    ppermute x1, waiting for transfers between devices, shards(): qb = lax.ppermute(yb, ('gy', 'col'), ring_pairs(ny, 1))  2.23 us
    pallas_call x1, Pallas kernels, shards(): pl.pallas_call(lambda *refs: interior_kernel(nz, *refs), out_shape=(f32(1...  1.92 us
    pallas_call x1, Pallas kernels, shards(): pl.pallas_call(lambda *refs: bulk_kernel(nz, *refs), out_shape=(f32(19, 4...  1.88 us
    pallas_call x1, Pallas kernels, shards(): pl.pallas_call(lambda *refs: edge_kernel(nz, *refs), out_shape=(f32(messa...  1.63 us
  transfers between devices with their start and end apart: 7, of which 1 were waited for; matrix products, arithmetic and copies ran while one was open for 0% of the time, Pallas kernels for 21%

profile of v4, /device:TPU:0, one launch (start us, length us, event | category | flops | bytes accessed | tf_op | source)
XLA Modules:
  0.0 21.4 jit_solution(3838371121980558102)
XLA Ops:
  0.6 0.0 copy-start.2
  0.6 0.0 copy-start
  0.7 1.6 %edge_rows.1 = (f32[280,128]{1,0:T(8,128)S(1)}, f32[280,128]{1,0:T(8,128)S(1)}) custom-call(f32[19,4,64,128]{3,2,1,0:T(8,128)} %refs_0_.3, s32[4,64,128]{2,1,0:T(8,128)} %refs_1_.3, f32[3,64,128]{2,1,0:T(8,128)} %refs_2_.1, f32[1,64]{1,0:T(1,128)} %bitcast.1, f32[3,64]{1,0:T(4,128)} %refs_4_.1, f32[3,64]{1,0:T(4,128)} %refs_5_.1), custom_call_target="tpu_custom_call" | custom-call | tf_op jit(solution)/shard_map/edge_rows/pallas_call | solution.py:625
  2.3 3.1 %collective-permute-start = (f32[280,128]{1,0:T(8,128)S(1)}, f32[280,128]{1,0:T(8,128)S(1)}, u32[]{:S(2)}, u32[]{:S(2)}) collective-permute-start(f32[280,128]{1,0:T(8,128)S(1)} %get-tuple-element.21.refs_0_.refs_2_), channel_id=1, source_target_pairs={{0,2},{2,0},{4,6},{6,4},{1,3},{3,1},{5,7},{7,5},{8,10},{10,8},{12,... | collective-permute-start | bytes 430088 | tf_op jit(solution)/shard_map/ppermute | solution.py:647
  5.4 2.6 %collective-permute-start.2 = (f32[16,128]{1,0:T(8,128)S(1)}, f32[16,128]{1,0:T(8,128)S(1)}, u32[]{:S(2)}, u32[]{:S(2)}) collective-permute-start(f32[16,128]{1,0:T(8,128)S(1)} %far_rows.1), channel_id=1, source_target_pairs={{0,4},{2,6},{4,0},{6,2},{1,5},{3,7},{5,1},{7,3},{8,12},{10,14},{12... | collective-permute-start | bytes 24584 | tf_op jit(solution)/shard_map/ppermute | solution.py:649
  8.0 0.0 copy-start.3
  8.0 0.0 copy-start.5
  8.0 0.8 %collective-permute-start.1 = (f32[280,128]{1,0:T(8,128)S(1)}, f32[280,128]{1,0:T(8,128)S(1)}, u32[]{:S(2)}, u32[]{:S(2)}) collective-permute-start(f32[280,128]{1,0:T(8,128)S(1)} %get-tuple-element.22), channel_id=1, source_target_pairs={{2,4},{4,2},{3,5},{5,3},{10,12},{12,10},{11,13},{13,11},{18,20},{2... | collective-permute-start | bytes 430088 | tf_op jit(solution)/shard_map/ppermute | solution.py:648
  8.8 0.0 copy-done.2
  8.8 0.0 copy-done
  8.8 1.9 %bulk.1 = (f32[19,4,80,128]{3,2,1,0:T(8,128)S(1)}, f32[4,80,128]{2,1,0:T(8,128)S(1)}, f32[64,128]{1,0:T(8,128)S(1)}, f32[64,128]{1,0:T(8,128)S(1)}) custom-call(f32[19,4,64,128]{3,2,1,0:T(8,128)S(1)} %copy-done, s32[4,64,128]{2,1,0:T(8,128)S(1)} %copy-done.2), custom_call_target="tpu_custom_call" | custom-call | flops 4000000000 | bytes 8000000 | tf_op jit(solution)/shard_map/bulk/pallas_call | solution.py:653
  10.7 0.0 copy-start.1
  10.7 0.0 copy-start.4
  10.7 0.1 collective-permute-start.3
  10.8 2.5 %collective-permute-start.4 = (f32[64,128]{1,0:T(8,128)S(1)}, f32[64,128]{1,0:T(8,128)S(1)}, u32[]{:S(2)}, u32[]{:S(2)}) collective-permute-start(f32[64,128]{1,0:T(8,128)S(1)} %get-tuple-element.27.refs_4_), channel_id=1, source_target_pairs={{0,25},{1,8},{8,1},{9,16},{16,9},{17,24},{24,17},{25,0},{2,27},{3,... | collective-permute-start | bytes 98312 | tf_op jit(solution)/shard_map/ppermute | solution.py:664
  13.3 0.0 collective-permute-done.2.refs_5_
  13.3 0.0 collective-permute-done.1.refs_4_
  13.3 0.0 collective-permute-done.refs_3_
  13.4 0.0 copy-done.3
  13.4 0.0 copy-done.5
  13.4 0.7 %columns.1 = (f32[19,4,80,128]{3,2,1,0:T(8,128)S(1)}, f32[4,80,128]{2,1,0:T(8,128)S(1)}, f32[112,128]{1,0:T(8,128)S(1)}, f32[112,128]{1,0:T(8,128)S(1)}, f32[4,8...) custom-call(f32[19,4,80,128]{3,2,1,0:T(8,128)S(1)} %get-tuple-element.19.refs_0_, ...), custom_call_target="tpu_custom_call", output_to_operand_aliasing={{0}: (0, {}), {1}: (1, {})} | custom-call | tf_op jit(solution)/shard_map/columns/pallas_call | solution.py:671
  14.0 0.1 collective-permute-start.5
  14.1 0.6 %collective-permute-start.6 = (f32[112,128]{1,0:T(8,128)S(1)}, f32[112,128]{1,0:T(8,128)S(1)}, u32[]{:S(2)}, u32[]{:S(2)}) collective-permute-start(f32[112,128]{1,0:T(8,128)S(1)} %get-tuple-element.29.refs_6_), channel_id=1, source_target_pairs={{0,25},{1,8},{8,1},{9,16},{16,9},{17,24},{24,17},{25,0},{2,27},{3,... | collective-permute-start | bytes 172040 | tf_op jit(solution)/shard_map/ppermute | solution.py:688
  14.8 0.0 copy-done.1
  14.8 0.0 copy-done.4
  14.8 1.9 %interior.1 = (f32[19,3,80,128]{3,2,1,0:T(8,128)S(1)}, f32[240,128]{1,0:T(8,128)S(1)}, f32[24,128]{1,0:T(8,128)S(1)}, f32[144,128]{1,0:T(8,128)S(1)}, f32[144,128]{1,0:T(8,128)S(1)}) custom-call(f32[19,4,80,128]{3,2,1,0:T(8,128)S(1)} %get-tuple-element.23.refs_0_, f32[4,80,128]{2,1,0:T(8,128)S(1)} %get-tuple-element.24.refs_1_, ...), custom_call_target="tpu_custom_call" | custom-call | flops 4000000000 | bytes 8000000 | tf_op jit(solution)/shard_map/interior/pallas_call | solution.py:698
  16.7 0.0 collective-permute-done.3.refs_8_
  16.7 0.0 collective-permute-done.4.refs_9_
  16.7 0.0 collective-permute-done.5.refs_10_
  16.7 2.2 %collective-permute-done.6.refs_11_ = f32[112,128]{1,0:T(8,128)S(1)} collective-permute-done((f32[112,128]{1,0:T(8,128)S(1)}, f32[112,128]{1,0:T(8,128)S(1)}, u32[]{:S(2)}, u32[]{:S(2)}) %collective-permute-start.6) | collective-permute-done | bytes 57376 | tf_op jit(solution)/shard_map/ppermute | solution.py:688
  19.0 2.5 %stream.1 = (f32[3,64,128]{2,1,0:T(8,128)}, f32[19,4,64,128]{3,2,1,0:T(8,128)}) custom-call(f32[19,4,80,128]{3,2,1,0:T(8,128)S(1)} %get-tuple-element.23.refs_0_, f32[4,80,128]{2,1,0:T(8,128)S(1)} %get-tuple-element.24.refs_1_, f32[19,3,80,128]{3,2,1,0:T(8,128)S(1)} %get-tuple-element.30.refs_2_, f32[240,128]{1,0:T(8,128)S(1)} %get-tuple-element.31.refs_3_, ...), custom_call_target="tpu_custom_call" | custom-call | tf_op jit(solution)/shard_map/stream/pallas_call | solution.py:710
  (2 shorter events, 0.0 us)
Async XLA Ops:
  0.6 8.1 %copy-start.2 = (s32[4,64,128]{2,1,0:T(8,128)S(1)}, s32[4,64,128]{2,1,0:T(8,128)}, u32[]{:S(2)}) copy-start(s32[4,64,128]{2,1,0:T(8,128)} %refs_1_.3) | copy-start | bytes 393220
  0.6 8.1 %copy-start = (f32[19,4,64,128]{3,2,1,0:T(8,128)S(1)}, f32[19,4,64,128]{3,2,1,0:T(8,128)}, u32[]{:S(2)}) copy-start(f32[19,4,64,128]{3,2,1,0:T(8,128)} %refs_0_.3) | copy-start | bytes 7471108
  2.3 11.1 %collective-permute-start = (f32[280,128]{1,0:T(8,128)S(1)}, f32[280,128]{1,0:T(8,128)S(1)}, u32[]{:S(2)}, u32[]{:S(2)}) collective-permute-start(f32[280,128]{1,0:T(8,128)S(1)} %get-tuple-element.21.refs_0_.refs_2_), channel_id=1, source_target_pairs={{0,2},{2,0},{4,6},{6,4},{1,3},{3,1},{5,7},{7,5},{8,10},{10,8},{12,... | collective-permute-start | bytes 430088 | tf_op jit(solution)/shard_map/ppermute | solution.py:647
  5.4 8.0 %collective-permute-start.2 = (f32[16,128]{1,0:T(8,128)S(1)}, f32[16,128]{1,0:T(8,128)S(1)}, u32[]{:S(2)}, u32[]{:S(2)}) collective-permute-start(f32[16,128]{1,0:T(8,128)S(1)} %far_rows.1), channel_id=1, source_target_pairs={{0,4},{2,6},{4,0},{6,2},{1,5},{3,7},{5,1},{7,3},{8,12},{10,14},{12... | collective-permute-start | bytes 24584 | tf_op jit(solution)/shard_map/ppermute | solution.py:649
  8.0 5.4 %copy-start.3 = (f32[80,192]{1,0:T(8,128)S(1)}, f32[80,192]{1,0:T(8,128)}, u32[]{:S(2)}) copy-start(f32[80,192]{1,0:T(8,128)} %constant.10.clone.refs_7_) | copy-start | bytes 184324
  8.0 5.4 %copy-start.5 = (f32[8,128]{1,0:T(8,128)S(1)}, f32[8,128]{1,0:T(8,128)}, u32[]{:S(2)}) copy-start(f32[8,128]{1,0:T(8,128)} %constant.11.clone.refs_8_) | copy-start | bytes 12292
  8.0 5.4 %collective-permute-start.1 = (f32[280,128]{1,0:T(8,128)S(1)}, f32[280,128]{1,0:T(8,128)S(1)}, u32[]{:S(2)}, u32[]{:S(2)}) collective-permute-start(f32[280,128]{1,0:T(8,128)S(1)} %get-tuple-element.22), channel_id=1, source_target_pairs={{2,4},{4,2},{3,5},{5,3},{10,12},{12,10},{11,13},{13,11},{18,20},{2... | collective-permute-start | bytes 430088 | tf_op jit(solution)/shard_map/ppermute | solution.py:648
  10.7 4.1 %copy-start.1 = (f32[384,128]{1,0:T(8,128)S(1)}, f32[384,128]{1,0:T(8,128)}, u32[]{:S(2)}) copy-start(f32[384,128]{1,0:T(8,128)} %constant.12.clone.refs_7_.refs_12_) | copy-start | bytes 589828
  10.7 4.1 %copy-start.4 = (f32[8,384]{1,0:T(8,128)S(1)}, f32[8,384]{1,0:T(8,128)}, u32[]{:S(2)}) copy-start(f32[8,384]{1,0:T(8,128)} %constant.13.clone.refs_8_.refs_13_) | copy-start | bytes 36868
  10.7 6.0 %collective-permute-start.3 = (f32[64,128]{1,0:T(8,128)S(1)}, f32[64,128]{1,0:T(8,128)S(1)}, u32[]{:S(2)}, u32[]{:S(2)}) collective-permute-start(f32[64,128]{1,0:T(8,128)S(1)} %get-tuple-element.26.refs_3_), channel_id=1, source_target_pairs={{0,1},{1,0},{8,9},{9,8},{16,17},{17,16},{24,25},{25,24},{2,3},{3,2... | collective-permute-start | bytes 98312 | tf_op jit(solution)/shard_map/ppermute | solution.py:663
  10.8 5.9 %collective-permute-start.4 = (f32[64,128]{1,0:T(8,128)S(1)}, f32[64,128]{1,0:T(8,128)S(1)}, u32[]{:S(2)}, u32[]{:S(2)}) collective-permute-start(f32[64,128]{1,0:T(8,128)S(1)} %get-tuple-element.27.refs_4_), channel_id=1, source_target_pairs={{0,25},{1,8},{8,1},{9,16},{16,9},{17,24},{24,17},{25,0},{2,27},{3,... | collective-permute-start | bytes 98312 | tf_op jit(solution)/shard_map/ppermute | solution.py:664
  14.0 2.7 %collective-permute-start.5 = (f32[112,128]{1,0:T(8,128)S(1)}, f32[112,128]{1,0:T(8,128)S(1)}, u32[]{:S(2)}, u32[]{:S(2)}) collective-permute-start(f32[112,128]{1,0:T(8,128)S(1)} %get-tuple-element.28.refs_5_), channel_id=1, source_target_pairs={{0,1},{1,0},{8,9},{9,8},{16,17},{17,16},{24,25},{25,24},{2,3},{3,2... | collective-permute-start | bytes 172040 | tf_op jit(solution)/shard_map/ppermute | solution.py:687
  14.1 4.8 %collective-permute-start.6 = (f32[112,128]{1,0:T(8,128)S(1)}, f32[112,128]{1,0:T(8,128)S(1)}, u32[]{:S(2)}, u32[]{:S(2)}) collective-permute-start(f32[112,128]{1,0:T(8,128)S(1)} %get-tuple-element.29.refs_6_), channel_id=1, source_target_pairs={{0,25},{1,8},{8,1},{9,16},{16,9},{17,24},{24,17},{25,0},{2,27},{3,... | collective-permute-start | bytes 172040 | tf_op jit(solution)/shard_map/ppermute | solution.py:688

commit v5 on v4

--- a/solution.py
+++ b/solution.py
@@ -139,33 +139,26 @@
     copies = [pltpu.make_async_copy(src, dst, sems.at[n]) for n, (src, dst) in enumerate(copies)]
     for copy in copies:
         copy.start()
-    for copy in copies[:4]:
-        copy.wait()
     for part, row in ((0, 0), (1, height - 8)):
+        copies[part].wait()
+        copies[2 + part].wait()
         wall = wall_rows(row, height, kz, nz)
         at = slice(8 * part, 8 * part + 8)
         for x in range(4):
             solid = (flags[x, at, :] == 1) | wall
             post = collide([raw[i, x, at, :] for i in range(19)], solid)
-            for i in range(19):
-                edge[i, x, at, :] = post[i]
-            edge[19, x, at, :] = solid.astype(jnp.float32)
-
-    def put(row, up, down):
-        za[row : row + 1, :] = jnp.where(upward, up, down)
-        zb[row : row + 1, :] = jnp.where(upward, down, up)
-
-    q = 0
-    for i in Z_EDGE:
-        for x in range(4):
-            put(4 * q + x, edge[i, x, 15:16, :], edge[MIRROR_Z[i], x, 0:1, :])
-        q += 1
-    for i in Z_SECOND:
-        for x in range(4):
-            put(4 * q + x, edge[i, x, 14:15, :], edge[MIRROR_Z[i], x, 1:2, :])
-        q += 1
-    for x in range(4):
-        put(4 * q + x, edge[19, x, 15:16, :], edge[19, x, 0:1, :])
+            post.append(solid.astype(jnp.float32))
+            for i in range(20):
+                edge[64 * i + 16 * x + 8 * part : 64 * i + 16 * x + 8 * part + 8, :] = post[i]
+
+    def put(q, i, depth):
+        up = edge[pl.ds(64 * i + 15 - depth, 4, stride=16), :]
+        down = edge[pl.ds(64 * (i if i == 19 else MIRROR_Z[i]) + depth, 4, stride=16), :]
+        za[4 * q : 4 * q + 4, :] = jnp.where(upward, up, down)
+        zb[4 * q : 4 * q + 4, :] = jnp.where(upward, down, up)
+
+    for q, i in enumerate(Z_EDGE + Z_SECOND + [19]):
+        put(q, i, 1 if len(Z_EDGE) <= q < 19 else 0)
     for copy in copies[4:]:
         copy.wait()
     for ref in (za, zb):
@@ -348,6 +341,13 @@
     return None if source < 0 else min(source, 3)
 
 
+INWARD = [i for i in range(19) if DIRS[i][2]]
+
+
+def both_ghosts(sub, low, high):
+    return jnp.where(sub < 4, low, high)
+
+
 def assemble(tall, sa, sb, ya, yb, a_first):
     end = PAD + sa.shape[0]
     for out, source, a, b in (
@@ -369,22 +369,30 @@
     y_even = lax.rem(ky, 2) == 0
     sub = lax.broadcasted_iota(jnp.int32, (8, 128), 0)
 
-    def step(row, outside):
+    def moved(i, value):
+        return pltpu.roll(value, DIRS[i][1] % 128, 1) if DIRS[i][1] else value
+
+    outside = ((sub < 4) & (kz == 0)) | ((sub >= 4) & (kz == nz - 1))
+    for x in range(1, 4):
+        solid = both_ghosts(sub, solidp[x, PAD - 1 : PAD + 7, :], solidp[x, top - 7 : top + 1, :]) > 0.5
+        g = []
+        for i in range(19):
+            low, high, source = PAD - 1 - DIRS[i][2], top - 7 - DIRS[i][2], streamed(i, x)
+            g.append(both_ghosts(sub, post[i, source, low : low + 8, :], post[i, source, high : high + 8, :]))
+        p = collide(g, solid, INWARD)
+        for i in INWARD:
+            row, at = (PAD - 1, 0) if DIRS[i][2] == 1 else (top, 7)
+            value = moved(i, jnp.where(outside, 0.0, p[i]))
+            post2[i, x - 1, row : row + 1, :] = value[at : at + 1, :]
+
+    def body(t, carry):
+        row = pl.multiple_of(t * 8 + PAD, 8)
         for x in range(1, 4):
             solid = solidp[x, pl.ds(row, 8), :] > 0.5
             g = [post[i, streamed(i, x), pl.ds(row - DIRS[i][2], 8), :] for i in range(19)]
             p = collide(g, solid)
             for i in range(19):
-                value = p[i] if outside is None else jnp.where(outside, 0.0, p[i])
-                if DIRS[i][1]:
-                    value = pltpu.roll(value, DIRS[i][1] % 128, 1)
-                post2[i, x - 1, pl.ds(row, 8), :] = value
-
-    step(PAD - 1, (sub == 0) & (kz == 0))
-    step(top - 7, (sub == 7) & (kz == nz - 1))
-
-    def body(t, carry):
-        step(pl.multiple_of(t * 8 + PAD, 8), None)
+                post2[i, x - 1, pl.ds(row, 8), :] = moved(i, p[i])
         return carry
 
     lax.fori_loop(0, rows // 8 - 2, body, 0)
@@ -415,8 +423,8 @@
     sub = lax.broadcasted_iota(jnp.int32, (8, 128), 0)
 
     assemble(tall, sa, sb, ya, yb, jnp.logical_not(y_even))
-    strip_left[0:128, :] = jnp.transpose(tall[0])
-    strip_right[0:128, :] = jnp.transpose(tall[1])
+    strip_left[0:128, 0:rows] = jnp.transpose(tall[0, 0:rows, :])
+    strip_right[0:128, 0:rows] = jnp.transpose(tall[1, 0:rows, :])
 
     lane_h = lax.broadcasted_iota(jnp.int32, (Y_HALF, 128), 1)
     for c in range(3):
@@ -488,25 +496,42 @@
                 moving[pl.ds(16 * n + (column + 2) % 4, 4, stride=4), :] = value
             else:
                 still[pl.ds(8 * Y_FLAT.index(i) + 2 - column, 4, stride=2), :] = value
-    ghost_moving[...] = jnp.transpose(moving[...])
-    ghost_still[...] = jnp.transpose(still[...])
-
-    def inlet(row, outside_rows):
-        us = [INLET * flow[pl.ds(rows * c + row, 8), :] for c in range(3)]
-        eq = inlet_state(*us)
-        solid = solidp[0, pl.ds(row, 8), :] > 0.5
-        for i in range(19):
+    ghost_moving[:, 0:80] = jnp.transpose(moving[0:80, :])
+    ghost_still[:, 0:72] = jnp.transpose(still[0:72, :])
+
+    def inlet_values(us, solid, planes, load):
+        eq = inlet_state(*[INLET * u for u in us])
+        for i in planes:
             j = OPP[i]
             source = streamed(j, 0)
-            if source is None:
-                value = jnp.where(solid, 0.0, eq[i])
-            else:
-                value = jnp.where(solid, post[j, source, pl.ds(row - DIRS[j][2], 8), :], eq[i])
-            if outside_rows is not None:
-                value = jnp.where(outside_rows, 0.0, value)
-            if DIRS[i][1]:
-                value = pltpu.roll(value, DIRS[i][1] % 128, 1)
-            inlet2[i, pl.ds(row, 8), :] = value
+            bounced = 0.0 if source is None else load(j, source)
+            yield i, jnp.where(solid, bounced, eq[i])
+
+    def moved(i, value):
+        return pltpu.roll(value, DIRS[i][1] % 128, 1) if DIRS[i][1] else value
+
+    def inlet(row):
+        us = [flow[pl.ds(rows * c + row, 8), :] for c in range(3)]
+        solid = solidp[0, pl.ds(row, 8), :] > 0.5
+        load = lambda j, source: post[j, source, pl.ds(row - DIRS[j][2], 8), :]
+        for i, value in inlet_values(us, solid, range(19), load):
+            inlet2[i, pl.ds(row, 8), :] = moved(i, value)
+
+    def inlet_ghosts():
+        low, high = PAD - 1, top - 7
+
+        def both(ref, shift, *lead):
+            low_at, high_at = slice(low + shift, low + shift + 8), slice(high + shift, high + shift + 8)
+            return both_ghosts(sub, ref[(*lead, low_at)], ref[(*lead, high_at)])
+
+        us = [both(flow, rows * c) for c in range(3)]
+        solid = both(solidp, 0, 0) > 0.5
+        load = lambda j, source: both(post, -DIRS[j][2], j, source)
+        beyond = ((sub < 4) & (kz == 0)) | ((sub >= 4) & (kz == nz - 1))
+        for i, value in inlet_values(us, solid, INWARD, load):
+            row, at = (PAD - 1, 0) if DIRS[i][2] == 1 else (top, 7)
+            value = moved(i, jnp.where(beyond, 0.0, value))
+            inlet2[i, row : row + 1, :] = value[at : at + 1, :]
 
     def out_copy(t):
         at = pl.ds(pl.multiple_of(t * 8, 8), 8)
@@ -552,12 +577,11 @@
                     write(j, 0, jnp.zeros((8, 128), jnp.float32))
         out_copy(t).start()
 
-    inlet(PAD - 1, (sub == 0) & (kz == 0))
-    inlet(top - 7, (sub == 7) & (kz == nz - 1))
-    inlet(PAD, None)
+    inlet_ghosts()
+    inlet(PAD)
 
     def main(t, carry):
-        inlet(pl.multiple_of(t * 8 + PAD, 8), None)
+        inlet(pl.multiple_of(t * 8 + PAD, 8))
         last(t - 1)
         return carry
 
@@ -629,7 +653,7 @@
         out_specs=vm(2),
         scratch_shapes=[
             scratch(19, 4, 16, 128), flags(4, 16, 128), scratch(1, height), scratch(3, height),
-            scratch(3, height), scratch(20, 4, 16, 128), dma((13,)),
+            scratch(3, height), scratch(20 * 4 * 16, 128), dma((13,)),
         ],
         compiler_params=params(8),
         name="edge_rows",

time: 21.6 us -> 21.5 us (level)
  Pallas kernels: 8.55 us -> 8.32 us
  transfers between devices with their start and end apart: 7 -> 7, of which waited for: 1 -> 1; matrix products, arithmetic and copies ran while one was open for 0% -> 0% of each run, Pallas kernels for 21% -> 20%
where the time goes in v5:
time: 21.5 us; the launch traced here: 21.3 us
  starting transfers between devices  9.79 us (46%)
  Pallas kernels  8.32 us (39%)
  waiting for transfers between devices  2.36 us (11%)
  between operations  0.79 us (4%)
    ppermute x1, starting transfers between devices, shards(): ra = lax.ppermute(za, 'gz', swap_pairs(nz, 0))  3.09 us
    ppermute x1, starting transfers between devices, shards(): rc = lax.ppermute(z2, 'gz', swap_pairs(nz, 0, 2))  2.59 us
    ppermute x1, starting transfers between devices, shards(): pb = lax.ppermute(sb, ('gy', 'col'), ring_pairs(ny, 1))  2.55 us
    pallas_call x1, Pallas kernels, shards(): pl.pallas_call(lambda *refs: final_kernel(nz, *refs), out_shape=(f32(3, h...  2.45 us
    ppermute x1, waiting for transfers between devices, shards(): qb = lax.ppermute(yb, ('gy', 'col'), ring_pairs(ny, 1))  2.35 us
    pallas_call x1, Pallas kernels, shards(): pl.pallas_call(lambda *refs: bulk_kernel(nz, *refs), out_shape=(f32(19, 4...  1.88 us
    pallas_call x1, Pallas kernels, shards(): pl.pallas_call(lambda *refs: interior_kernel(nz, *refs), out_shape=(f32(1...  1.81 us
    pallas_call x1, Pallas kernels, shards(): pl.pallas_call(lambda *refs: edge_kernel(nz, *refs), out_shape=(f32(messa...  1.52 us
  transfers between devices with their start and end apart: 7, of which 1 were waited for; matrix products, arithmetic and copies ran while one was open for 0% of the time, Pallas kernels for 20%

profile of v5, /device:TPU:0, one launch (start us, length us, event | category | flops | bytes accessed | tf_op | source)
XLA Modules:
  0.0 21.3 jit_solution(250812158202078172)
XLA Ops:
  0.6 0.0 copy-start.2
  0.6 0.0 copy-start
  0.7 1.5 %edge_rows.1 = (f32[280,128]{1,0:T(8,128)S(1)}, f32[280,128]{1,0:T(8,128)S(1)}) custom-call(f32[19,4,64,128]{3,2,1,0:T(8,128)} %refs_0_.3, s32[4,64,128]{2,1,0:T(8,128)} %refs_1_.3, f32[3,64,128]{2,1,0:T(8,128)} %refs_2_.1, f32[1,64]{1,0:T(1,128)} %bitcast.1, f32[3,64]{1,0:T(4,128)} %refs_4_.1, f32[3,64]{1,0:T(4,128)} %refs_5_.1), custom_call_target="tpu_custom_call" | custom-call | tf_op jit(solution)/shard_map/edge_rows/pallas_call | solution.py:649
  2.2 3.1 %collective-permute-start = (f32[280,128]{1,0:T(8,128)S(1)}, f32[280,128]{1,0:T(8,128)S(1)}, u32[]{:S(2)}, u32[]{:S(2)}) collective-permute-start(f32[280,128]{1,0:T(8,128)S(1)} %get-tuple-element.21.refs_0_.refs_2_), channel_id=1, source_target_pairs={{0,2},{2,0},{4,6},{6,4},{1,3},{3,1},{5,7},{7,5},{8,10},{10,8},{12,... | collective-permute-start | bytes 430088 | tf_op jit(solution)/shard_map/ppermute | solution.py:671
  5.3 2.6 %collective-permute-start.2 = (f32[16,128]{1,0:T(8,128)S(1)}, f32[16,128]{1,0:T(8,128)S(1)}, u32[]{:S(2)}, u32[]{:S(2)}) collective-permute-start(f32[16,128]{1,0:T(8,128)S(1)} %far_rows.1), channel_id=1, source_target_pairs={{0,4},{2,6},{4,0},{6,2},{1,5},{3,7},{5,1},{7,3},{8,12},{10,14},{12... | collective-permute-start | bytes 24584 | tf_op jit(solution)/shard_map/ppermute | solution.py:673
  7.9 0.0 copy-start.3
  7.9 0.0 copy-start.5
  7.9 0.8 %collective-permute-start.1 = (f32[280,128]{1,0:T(8,128)S(1)}, f32[280,128]{1,0:T(8,128)S(1)}, u32[]{:S(2)}, u32[]{:S(2)}) collective-permute-start(f32[280,128]{1,0:T(8,128)S(1)} %get-tuple-element.22), channel_id=1, source_target_pairs={{2,4},{4,2},{3,5},{5,3},{10,12},{12,10},{11,13},{13,11},{18,20},{2... | collective-permute-start | bytes 430088 | tf_op jit(solution)/shard_map/ppermute | solution.py:672
  8.7 0.0 copy-done.2
  8.7 0.0 copy-done
  8.7 1.9 %bulk.1 = (f32[19,4,80,128]{3,2,1,0:T(8,128)S(1)}, f32[4,80,128]{2,1,0:T(8,128)S(1)}, f32[64,128]{1,0:T(8,128)S(1)}, f32[64,128]{1,0:T(8,128)S(1)}) custom-call(f32[19,4,64,128]{3,2,1,0:T(8,128)S(1)} %copy-done, s32[4,64,128]{2,1,0:T(8,128)S(1)} %copy-done.2), custom_call_target="tpu_custom_call" | custom-call | flops 4000000000 | bytes 8000000 | tf_op jit(solution)/shard_map/bulk/pallas_call | solution.py:677
  10.6 0.0 copy-start.1
  10.6 0.0 copy-start.4
  10.6 0.1 collective-permute-start.3
  10.7 2.5 %collective-permute-start.4 = (f32[64,128]{1,0:T(8,128)S(1)}, f32[64,128]{1,0:T(8,128)S(1)}, u32[]{:S(2)}, u32[]{:S(2)}) collective-permute-start(f32[64,128]{1,0:T(8,128)S(1)} %get-tuple-element.27.refs_4_), channel_id=1, source_target_pairs={{0,25},{1,8},{8,1},{9,16},{16,9},{17,24},{24,17},{25,0},{2,27},{3,... | collective-permute-start | bytes 98312 | tf_op jit(solution)/shard_map/ppermute | solution.py:688
  13.2 0.0 collective-permute-done.2.refs_5_
  13.2 0.0 collective-permute-done.1.refs_4_
  13.2 0.0 collective-permute-done.refs_3_
  13.2 0.0 copy-done.3
  13.3 0.0 copy-done.5
  13.3 0.7 %columns.1 = (f32[19,4,80,128]{3,2,1,0:T(8,128)S(1)}, f32[4,80,128]{2,1,0:T(8,128)S(1)}, f32[112,128]{1,0:T(8,128)S(1)}, f32[112,128]{1,0:T(8,128)S(1)}, f32[4,8...) custom-call(f32[19,4,80,128]{3,2,1,0:T(8,128)S(1)} %get-tuple-element.19.refs_0_, ...), custom_call_target="tpu_custom_call", output_to_operand_aliasing={{0}: (0, {}), {1}: (1, {})} | custom-call | tf_op jit(solution)/shard_map/columns/pallas_call | solution.py:695
  13.9 0.1 collective-permute-start.5
  14.0 0.6 %collective-permute-start.6 = (f32[112,128]{1,0:T(8,128)S(1)}, f32[112,128]{1,0:T(8,128)S(1)}, u32[]{:S(2)}, u32[]{:S(2)}) collective-permute-start(f32[112,128]{1,0:T(8,128)S(1)} %get-tuple-element.29.refs_6_), channel_id=1, source_target_pairs={{0,25},{1,8},{8,1},{9,16},{16,9},{17,24},{24,17},{25,0},{2,27},{3,... | collective-permute-start | bytes 172040 | tf_op jit(solution)/shard_map/ppermute | solution.py:712
  14.6 0.0 copy-done.1
  14.6 0.0 copy-done.4
  14.6 1.8 %interior.1 = (f32[19,3,80,128]{3,2,1,0:T(8,128)S(1)}, f32[240,128]{1,0:T(8,128)S(1)}, f32[24,128]{1,0:T(8,128)S(1)}, f32[144,128]{1,0:T(8,128)S(1)}, f32[144,128]{1,0:T(8,128)S(1)}) custom-call(f32[19,4,80,128]{3,2,1,0:T(8,128)S(1)} %get-tuple-element.23.refs_0_, f32[4,80,128]{2,1,0:T(8,128)S(1)} %get-tuple-element.24.refs_1_, ...), custom_call_target="tpu_custom_call" | custom-call | flops 4000000000 | bytes 8000000 | tf_op jit(solution)/shard_map/interior/pallas_call | solution.py:722
  16.5 0.0 collective-permute-done.3.refs_8_
  16.5 0.0 collective-permute-done.4.refs_9_
  16.5 0.0 collective-permute-done.5.refs_10_
  16.5 2.3 %collective-permute-done.6.refs_11_ = f32[112,128]{1,0:T(8,128)S(1)} collective-permute-done((f32[112,128]{1,0:T(8,128)S(1)}, f32[112,128]{1,0:T(8,128)S(1)}, u32[]{:S(2)}, u32[]{:S(2)}) %collective-permute-start.6) | collective-permute-done | bytes 57376 | tf_op jit(solution)/shard_map/ppermute | solution.py:712
  18.8 2.5 %stream.1 = (f32[3,64,128]{2,1,0:T(8,128)}, f32[19,4,64,128]{3,2,1,0:T(8,128)}) custom-call(f32[19,4,80,128]{3,2,1,0:T(8,128)S(1)} %get-tuple-element.23.refs_0_, f32[4,80,128]{2,1,0:T(8,128)S(1)} %get-tuple-element.24.refs_1_, f32[19,3,80,128]{3,2,1,0:T(8,128)S(1)} %get-tuple-element.30.refs_2_, f32[240,128]{1,0:T(8,128)S(1)} %get-tuple-element.31.refs_3_, ...), custom_call_target="tpu_custom_call" | custom-call | tf_op jit(solution)/shard_map/stream/pallas_call | solution.py:734
  (2 shorter events, 0.0 us)
Async XLA Ops:
  0.6 8.0 %copy-start.2 = (s32[4,64,128]{2,1,0:T(8,128)S(1)}, s32[4,64,128]{2,1,0:T(8,128)}, u32[]{:S(2)}) copy-start(s32[4,64,128]{2,1,0:T(8,128)} %refs_1_.3) | copy-start | bytes 393220
  0.6 8.0 %copy-start = (f32[19,4,64,128]{3,2,1,0:T(8,128)S(1)}, f32[19,4,64,128]{3,2,1,0:T(8,128)}, u32[]{:S(2)}) copy-start(f32[19,4,64,128]{3,2,1,0:T(8,128)} %refs_0_.3) | copy-start | bytes 7471108
  2.2 11.1 %collective-permute-start = (f32[280,128]{1,0:T(8,128)S(1)}, f32[280,128]{1,0:T(8,128)S(1)}, u32[]{:S(2)}, u32[]{:S(2)}) collective-permute-start(f32[280,128]{1,0:T(8,128)S(1)} %get-tuple-element.21.refs_0_.refs_2_), channel_id=1, source_target_pairs={{0,2},{2,0},{4,6},{6,4},{1,3},{3,1},{5,7},{7,5},{8,10},{10,8},{12,... | collective-permute-start | bytes 430088 | tf_op jit(solution)/shard_map/ppermute | solution.py:671
  5.3 8.0 %collective-permute-start.2 = (f32[16,128]{1,0:T(8,128)S(1)}, f32[16,128]{1,0:T(8,128)S(1)}, u32[]{:S(2)}, u32[]{:S(2)}) collective-permute-start(f32[16,128]{1,0:T(8,128)S(1)} %far_rows.1), channel_id=1, source_target_pairs={{0,4},{2,6},{4,0},{6,2},{1,5},{3,7},{5,1},{7,3},{8,12},{10,14},{12... | collective-permute-start | bytes 24584 | tf_op jit(solution)/shard_map/ppermute | solution.py:673
  7.9 5.4 %copy-start.3 = (f32[80,192]{1,0:T(8,128)S(1)}, f32[80,192]{1,0:T(8,128)}, u32[]{:S(2)}) copy-start(f32[80,192]{1,0:T(8,128)} %constant.10.clone.refs_7_) | copy-start | bytes 184324
  7.9 5.4 %copy-start.5 = (f32[8,128]{1,0:T(8,128)S(1)}, f32[8,128]{1,0:T(8,128)}, u32[]{:S(2)}) copy-start(f32[8,128]{1,0:T(8,128)} %constant.11.clone.refs_8_) | copy-start | bytes 12292
  7.9 5.4 %collective-permute-start.1 = (f32[280,128]{1,0:T(8,128)S(1)}, f32[280,128]{1,0:T(8,128)S(1)}, u32[]{:S(2)}, u32[]{:S(2)}) collective-permute-start(f32[280,128]{1,0:T(8,128)S(1)} %get-tuple-element.22), channel_id=1, source_target_pairs={{2,4},{4,2},{3,5},{5,3},{10,12},{12,10},{11,13},{13,11},{18,20},{2... | collective-permute-start | bytes 430088 | tf_op jit(solution)/shard_map/ppermute | solution.py:672
  10.6 4.1 %copy-start.1 = (f32[384,128]{1,0:T(8,128)S(1)}, f32[384,128]{1,0:T(8,128)}, u32[]{:S(2)}) copy-start(f32[384,128]{1,0:T(8,128)} %constant.12.clone.refs_7_.refs_12_) | copy-start | bytes 589828
  10.6 4.1 %copy-start.4 = (f32[8,384]{1,0:T(8,128)S(1)}, f32[8,384]{1,0:T(8,128)}, u32[]{:S(2)}) copy-start(f32[8,384]{1,0:T(8,128)} %constant.13.clone.refs_8_.refs_13_) | copy-start | bytes 36868
  10.6 5.9 %collective-permute-start.3 = (f32[64,128]{1,0:T(8,128)S(1)}, f32[64,128]{1,0:T(8,128)S(1)}, u32[]{:S(2)}, u32[]{:S(2)}) collective-permute-start(f32[64,128]{1,0:T(8,128)S(1)} %get-tuple-element.26.refs_3_), channel_id=1, source_target_pairs={{0,1},{1,0},{8,9},{9,8},{16,17},{17,16},{24,25},{25,24},{2,3},{3,2... | collective-permute-start | bytes 98312 | tf_op jit(solution)/shard_map/ppermute | solution.py:687
  10.7 5.8 %collective-permute-start.4 = (f32[64,128]{1,0:T(8,128)S(1)}, f32[64,128]{1,0:T(8,128)S(1)}, u32[]{:S(2)}, u32[]{:S(2)}) collective-permute-start(f32[64,128]{1,0:T(8,128)S(1)} %get-tuple-element.27.refs_4_), channel_id=1, source_target_pairs={{0,25},{1,8},{8,1},{9,16},{16,9},{17,24},{24,17},{25,0},{2,27},{3,... | collective-permute-start | bytes 98312 | tf_op jit(solution)/shard_map/ppermute | solution.py:688
  13.9 2.6 %collective-permute-start.5 = (f32[112,128]{1,0:T(8,128)S(1)}, f32[112,128]{1,0:T(8,128)S(1)}, u32[]{:S(2)}, u32[]{:S(2)}) collective-permute-start(f32[112,128]{1,0:T(8,128)S(1)} %get-tuple-element.28.refs_5_), channel_id=1, source_target_pairs={{0,1},{1,0},{8,9},{9,8},{16,17},{17,16},{24,25},{25,24},{2,3},{3,2... | collective-permute-start | bytes 172040 | tf_op jit(solution)/shard_map/ppermute | solution.py:711
  14.0 4.8 %collective-permute-start.6 = (f32[112,128]{1,0:T(8,128)S(1)}, f32[112,128]{1,0:T(8,128)S(1)}, u32[]{:S(2)}, u32[]{:S(2)}) collective-permute-start(f32[112,128]{1,0:T(8,128)S(1)} %get-tuple-element.29.refs_6_), channel_id=1, source_target_pairs={{0,25},{1,8},{8,1},{9,16},{16,9},{17,24},{24,17},{25,0},{2,27},{3,... | collective-permute-start | bytes 172040 | tf_op jit(solution)/shard_map/ppermute | solution.py:712

commit v6 on v5

--- a/solution.py
+++ b/solution.py
@@ -222,8 +222,7 @@
             for n, i in enumerate(Y_PLUS):
                 j = MIRROR_Y[i]
                 slot = LANE_PLUS // 2 + 4 * n + x
-                post[i, x, out, :] = pltpu.roll(p[i], 1, 1)
-                post[j, x, out, :] = pltpu.roll(p[j], 127, 1)
+                post[i, x, out, :], post[j, x, out, :] = p[i], p[j]
                 right = put_pair(pair, slot, p[i], 126, right)
                 left = put_pair(pair, slot, p[j], 0, left)
         right = jnp.where(pair < LANE_PLUS // 2, flat, right)
@@ -238,7 +237,7 @@
 def column_kernel(
     nz, post_in, solid_in, sent, za, zb, z2c, z2d, bandz, pick,
     post, solidp, ya, yb, linear, meanrow,
-    wide, filt, moved,
+    wide, filt, edges,
 ):
     height = post.shape[2] - 2 * PAD
     rows = height + 2 * PAD
@@ -255,20 +254,16 @@
         return jnp.where(z_even, za[row : row + n, :], zb[row : row + n, :])
 
     top = PAD + height
-    low, high = below(0, ROW_PARAM), above(0, ROW_PARAM)
-    for n, shift in enumerate((0, 1, 127)):
-        moved[n, 0] = low if shift == 0 else pltpu.roll(low, shift, 1)
-        moved[n, 1] = high if shift == 0 else pltpu.roll(high, shift, 1)
+    edges[0], edges[1] = below(0, ROW_PARAM), above(0, ROW_PARAM)
     for items, first, depth in ((Z_EDGE, 0, 0), (Z_SECOND, len(Z_EDGE), 1)):
         for q, i in enumerate(items):
-            n = DIRS[i][1] % 3
             for x in range(4):
                 at = slice(4 * (first + q) + x, 4 * (first + q) + x + 1)
-                post[i, x, PAD - 1 - depth : PAD - depth, :] = moved[n, 0, at, :]
-                post[MIRROR_Z[i], x, top + depth : top + depth + 1, :] = moved[n, 1, at, :]
+                post[i, x, PAD - 1 - depth : PAD - depth, :] = edges[0, at, :]
+                post[MIRROR_Z[i], x, top + depth : top + depth + 1, :] = edges[1, at, :]
     for x in range(4):
-        solidp[x, PAD - 1 : PAD, :] = moved[0, 0, ROW_SOLID + x : ROW_SOLID + x + 1, :]
-        solidp[x, top : top + 1, :] = moved[0, 1, ROW_SOLID + x : ROW_SOLID + x + 1, :]
+        solidp[x, PAD - 1 : PAD, :] = edges[0, ROW_SOLID + x : ROW_SOLID + x + 1, :]
+        solidp[x, top : top + 1, :] = edges[1, ROW_SOLID + x : ROW_SOLID + x + 1, :]
 
     lane = lax.broadcasted_iota(jnp.int32, (8, 128), 1)
     own_par = pltpu.roll(sent[ROW_PARAM : ROW_PARAM + 8, :], PAD, 1)
@@ -309,8 +304,8 @@
                 flat = put_pair(pair, 4 * q + x, post[i, x, out, :], 127, flat)
             for n, i in enumerate(Y_PLUS):
                 slot = LANE_PLUS // 2 + 4 * n + x
-                right = put_pair(pair, slot, post[i, x, out, :], 127, right)
-                left = put_pair(pair, slot, post[MIRROR_Y[i], x, out, :], 127, left)
+                right = put_pair(pair, slot, post[i, x, out, :], 126, right)
+                left = put_pair(pair, slot, post[MIRROR_Y[i], x, out, :], 0, left)
         right = jnp.where(pair < LANE_PLUS // 2, flat, right)
         left = jnp.where(pair < LANE_PLUS // 2, flat, left)
         at = slice(0, 2) if row else slice(6, 8)
@@ -378,7 +373,8 @@
         g = []
         for i in range(19):
             low, high, source = PAD - 1 - DIRS[i][2], top - 7 - DIRS[i][2], streamed(i, x)
-            g.append(both_ghosts(sub, post[i, source, low : low + 8, :], post[i, source, high : high + 8, :]))
+            value = both_ghosts(sub, post[i, source, low : low + 8, :], post[i, source, high : high + 8, :])
+            g.append(moved(i, value))
         p = collide(g, solid, INWARD)
         for i in INWARD:
             row, at = (PAD - 1, 0) if DIRS[i][2] == 1 else (top, 7)
@@ -389,7 +385,7 @@
         row = pl.multiple_of(t * 8 + PAD, 8)
         for x in range(1, 4):
             solid = solidp[x, pl.ds(row, 8), :] > 0.5
-            g = [post[i, streamed(i, x), pl.ds(row - DIRS[i][2], 8), :] for i in range(19)]
+            g = [moved(i, post[i, streamed(i, x), pl.ds(row - DIRS[i][2], 8), :]) for i in range(19)]
             p = collide(g, solid)
             for i in range(19):
                 post2[i, x - 1, pl.ds(row, 8), :] = moved(i, p[i])
@@ -504,7 +500,7 @@
         for i in planes:
             j = OPP[i]
             source = streamed(j, 0)
-            bounced = 0.0 if source is None else load(j, source)
+            bounced = 0.0 if source is None else moved(j, load(j, source))
             yield i, jnp.where(solid, bounced, eq[i])
 
     def moved(i, value):
@@ -701,7 +697,7 @@
         in_specs=vm(9),
         out_specs=vm(6),
         scratch_shapes=[
-            scratch(3 * height, 384), scratch(rows, 384), scratch(3, 2, ROW_PARAM, 128),
+            scratch(3 * height, 384), scratch(rows, 384), scratch(2, ROW_PARAM, 128),
         ],
         input_output_aliases={0: 0, 1: 1},
         compiler_params=params(4),

time: 21.5 us -> 21.4 us (level)
  waiting for transfers between devices: 2.36 us -> 1.8 us
  Pallas kernels: 8.32 us -> 8.78 us
    pallas_call x1, Pallas kernels: 1.81 us -> 2.38 us  [shards(): pl.pallas_call(lambda *refs: interior_kernel(nz, *refs), out_shape=(f32(1...]
    ppermute x1, waiting for transfers between devices: 2.35 us -> 1.78 us  [shards(): qb = lax.ppermute(yb, ('gy', 'col'), ring_pairs(ny, 1))]
  transfers between devices with their start and end apart: 7 -> 7, of which waited for: 1 -> 1; matrix products, arithmetic and copies ran while one was open for 0% -> 0% of each run, Pallas kernels for 20% -> 22%
where the time goes in v6:
time: 21.4 us; the launch traced here: 21.2 us
  starting transfers between devices  9.79 us (46%)
  Pallas kernels  8.78 us (41%)
  waiting for transfers between devices  1.8 us (8%)
  between operations  0.79 us (4%)
    ppermute x1, starting transfers between devices, shards(): ra = lax.ppermute(za, 'gz', swap_pairs(nz, 0))  3.09 us
    pallas_call x1, Pallas kernels, shards(): pl.pallas_call(lambda *refs: final_kernel(nz, *refs), out_shape=(f32(3, h...  2.59 us
    ppermute x1, starting transfers between devices, shards(): rc = lax.ppermute(z2, 'gz', swap_pairs(nz, 0, 2))  2.59 us
    ppermute x1, starting transfers between devices, shards(): pb = lax.ppermute(sb, ('gy', 'col'), ring_pairs(ny, 1))  2.55 us
    pallas_call x1, Pallas kernels, shards(): pl.pallas_call(lambda *refs: interior_kernel(nz, *refs), out_shape=(f32(1...  2.38 us
    ppermute x1, waiting for transfers between devices, shards(): qb = lax.ppermute(yb, ('gy', 'col'), ring_pairs(ny, 1))  1.78 us
    pallas_call x1, Pallas kernels, shards(): pl.pallas_call(lambda *refs: bulk_kernel(nz, *refs), out_shape=(f32(19, 4...  1.69 us
    pallas_call x1, Pallas kernels, shards(): pl.pallas_call(lambda *refs: edge_kernel(nz, *refs), out_shape=(f32(messa...  1.52 us
  transfers between devices with their start and end apart: 7, of which 1 were waited for; matrix products, arithmetic and copies ran while one was open for 0% of the time, Pallas kernels for 22%

profile of v6, /device:TPU:0, one launch (start us, length us, event | category | flops | bytes accessed | tf_op | source)
XLA Modules:
  0.0 21.2 jit_solution(4152859311668354797)
XLA Ops:
  0.6 0.0 copy-start.2
  0.6 0.0 copy-start
  0.7 1.5 %edge_rows.1 = (f32[280,128]{1,0:T(8,128)S(1)}, f32[280,128]{1,0:T(8,128)S(1)}) custom-call(f32[19,4,64,128]{3,2,1,0:T(8,128)} %refs_0_.3, s32[4,64,128]{2,1,0:T(8,128)} %refs_1_.3, f32[3,64,128]{2,1,0:T(8,128)} %refs_2_.1, f32[1,64]{1,0:T(1,128)} %bitcast.1, f32[3,64]{1,0:T(4,128)} %refs_4_.1, f32[3,64]{1,0:T(4,128)} %refs_5_.1), custom_call_target="tpu_custom_call" | custom-call | tf_op jit(solution)/shard_map/edge_rows/pallas_call | solution.py:645
  2.2 3.1 %collective-permute-start = (f32[280,128]{1,0:T(8,128)S(1)}, f32[280,128]{1,0:T(8,128)S(1)}, u32[]{:S(2)}, u32[]{:S(2)}) collective-permute-start(f32[280,128]{1,0:T(8,128)S(1)} %get-tuple-element.21.refs_0_.refs_2_), channel_id=1, source_target_pairs={{0,2},{2,0},{4,6},{6,4},{1,3},{3,1},{5,7},{7,5},{8,10},{10,8},{12,... | collective-permute-start | bytes 430088 | tf_op jit(solution)/shard_map/ppermute | solution.py:667
  5.3 2.6 %collective-permute-start.2 = (f32[16,128]{1,0:T(8,128)S(1)}, f32[16,128]{1,0:T(8,128)S(1)}, u32[]{:S(2)}, u32[]{:S(2)}) collective-permute-start(f32[16,128]{1,0:T(8,128)S(1)} %far_rows.1), channel_id=1, source_target_pairs={{0,4},{2,6},{4,0},{6,2},{1,5},{3,7},{5,1},{7,3},{8,12},{10,14},{12... | collective-permute-start | bytes 24584 | tf_op jit(solution)/shard_map/ppermute | solution.py:669
  7.9 0.0 copy-start.3
  7.9 0.0 copy-start.5
  7.9 0.8 %collective-permute-start.1 = (f32[280,128]{1,0:T(8,128)S(1)}, f32[280,128]{1,0:T(8,128)S(1)}, u32[]{:S(2)}, u32[]{:S(2)}) collective-permute-start(f32[280,128]{1,0:T(8,128)S(1)} %get-tuple-element.22), channel_id=1, source_target_pairs={{2,4},{4,2},{3,5},{5,3},{10,12},{12,10},{11,13},{13,11},{18,20},{2... | collective-permute-start | bytes 430088 | tf_op jit(solution)/shard_map/ppermute | solution.py:668
  8.7 0.0 copy-done.2
  8.7 0.0 copy-done
  8.7 1.7 %bulk.1 = (f32[19,4,80,128]{3,2,1,0:T(8,128)S(1)}, f32[4,80,128]{2,1,0:T(8,128)S(1)}, f32[64,128]{1,0:T(8,128)S(1)}, f32[64,128]{1,0:T(8,128)S(1)}) custom-call(f32[19,4,64,128]{3,2,1,0:T(8,128)S(1)} %copy-done, s32[4,64,128]{2,1,0:T(8,128)S(1)} %copy-done.2), custom_call_target="tpu_custom_call" | custom-call | flops 4000000000 | bytes 8000000 | tf_op jit(solution)/shard_map/bulk/pallas_call | solution.py:673
  10.4 0.0 copy-start.1
  10.4 0.0 copy-start.4
  10.4 0.1 collective-permute-start.3
  10.5 2.5 %collective-permute-start.4 = (f32[64,128]{1,0:T(8,128)S(1)}, f32[64,128]{1,0:T(8,128)S(1)}, u32[]{:S(2)}, u32[]{:S(2)}) collective-permute-start(f32[64,128]{1,0:T(8,128)S(1)} %get-tuple-element.27.refs_4_), channel_id=1, source_target_pairs={{0,25},{1,8},{8,1},{9,16},{16,9},{17,24},{24,17},{25,0},{2,27},{3,... | collective-permute-start | bytes 98312 | tf_op jit(solution)/shard_map/ppermute | solution.py:684
  13.0 0.0 collective-permute-done.2.refs_5_
  13.0 0.0 collective-permute-done.1.refs_4_
  13.0 0.0 collective-permute-done.refs_3_
  13.1 0.0 copy-done.3
  13.1 0.0 copy-done.5
  13.1 0.6 %columns.1 = (f32[19,4,80,128]{3,2,1,0:T(8,128)S(1)}, f32[4,80,128]{2,1,0:T(8,128)S(1)}, f32[112,128]{1,0:T(8,128)S(1)}, f32[112,128]{1,0:T(8,128)S(1)}, f32[4,8...) custom-call(f32[19,4,80,128]{3,2,1,0:T(8,128)S(1)} %get-tuple-element.19.refs_0_, ...), custom_call_target="tpu_custom_call", output_to_operand_aliasing={{0}: (0, {}), {1}: (1, {})} | custom-call | tf_op jit(solution)/shard_map/columns/pallas_call | solution.py:691
  13.7 0.1 collective-permute-start.5
  13.8 0.6 %collective-permute-start.6 = (f32[112,128]{1,0:T(8,128)S(1)}, f32[112,128]{1,0:T(8,128)S(1)}, u32[]{:S(2)}, u32[]{:S(2)}) collective-permute-start(f32[112,128]{1,0:T(8,128)S(1)} %get-tuple-element.29.refs_6_), channel_id=1, source_target_pairs={{0,25},{1,8},{8,1},{9,16},{16,9},{17,24},{24,17},{25,0},{2,27},{3,... | collective-permute-start | bytes 172040 | tf_op jit(solution)/shard_map/ppermute | solution.py:708
  14.4 0.0 copy-done.1
  14.4 0.0 copy-done.4
  14.4 2.4 %interior.1 = (f32[19,3,80,128]{3,2,1,0:T(8,128)S(1)}, f32[240,128]{1,0:T(8,128)S(1)}, f32[24,128]{1,0:T(8,128)S(1)}, f32[144,128]{1,0:T(8,128)S(1)}, f32[144,128]{1,0:T(8,128)S(1)}) custom-call(f32[19,4,80,128]{3,2,1,0:T(8,128)S(1)} %get-tuple-element.23.refs_0_, f32[4,80,128]{2,1,0:T(8,128)S(1)} %get-tuple-element.24.refs_1_, ...), custom_call_target="tpu_custom_call" | custom-call | flops 4000000000 | bytes 8000000 | tf_op jit(solution)/shard_map/interior/pallas_call | solution.py:718
  16.8 0.0 collective-permute-done.3.refs_8_
  16.8 0.0 collective-permute-done.4.refs_9_
  16.8 0.0 collective-permute-done.5.refs_10_
  16.8 1.8 %collective-permute-done.6.refs_11_ = f32[112,128]{1,0:T(8,128)S(1)} collective-permute-done((f32[112,128]{1,0:T(8,128)S(1)}, f32[112,128]{1,0:T(8,128)S(1)}, u32[]{:S(2)}, u32[]{:S(2)}) %collective-permute-start.6) | collective-permute-done | bytes 57376 | tf_op jit(solution)/shard_map/ppermute | solution.py:708
  18.6 2.6 %stream.1 = (f32[3,64,128]{2,1,0:T(8,128)}, f32[19,4,64,128]{3,2,1,0:T(8,128)}) custom-call(f32[19,4,80,128]{3,2,1,0:T(8,128)S(1)} %get-tuple-element.23.refs_0_, f32[4,80,128]{2,1,0:T(8,128)S(1)} %get-tuple-element.24.refs_1_, f32[19,3,80,128]{3,2,1,0:T(8,128)S(1)} %get-tuple-element.30.refs_2_, f32[240,128]{1,0:T(8,128)S(1)} %get-tuple-element.31.refs_3_, ...), custom_call_target="tpu_custom_call" | custom-call | tf_op jit(solution)/shard_map/stream/pallas_call | solution.py:730
  (2 shorter events, 0.0 us)
Async XLA Ops:
  0.6 8.0 %copy-start.2 = (s32[4,64,128]{2,1,0:T(8,128)S(1)}, s32[4,64,128]{2,1,0:T(8,128)}, u32[]{:S(2)}) copy-start(s32[4,64,128]{2,1,0:T(8,128)} %refs_1_.3) | copy-start | bytes 393220
  0.6 8.0 %copy-start = (f32[19,4,64,128]{3,2,1,0:T(8,128)S(1)}, f32[19,4,64,128]{3,2,1,0:T(8,128)}, u32[]{:S(2)}) copy-start(f32[19,4,64,128]{3,2,1,0:T(8,128)} %refs_0_.3) | copy-start | bytes 7471108
  2.2 10.9 %collective-permute-start = (f32[280,128]{1,0:T(8,128)S(1)}, f32[280,128]{1,0:T(8,128)S(1)}, u32[]{:S(2)}, u32[]{:S(2)}) collective-permute-start(f32[280,128]{1,0:T(8,128)S(1)} %get-tuple-element.21.refs_0_.refs_2_), channel_id=1, source_target_pairs={{0,2},{2,0},{4,6},{6,4},{1,3},{3,1},{5,7},{7,5},{8,10},{10,8},{12,... | collective-permute-start | bytes 430088 | tf_op jit(solution)/shard_map/ppermute | solution.py:667
  5.3 7.8 %collective-permute-start.2 = (f32[16,128]{1,0:T(8,128)S(1)}, f32[16,128]{1,0:T(8,128)S(1)}, u32[]{:S(2)}, u32[]{:S(2)}) collective-permute-start(f32[16,128]{1,0:T(8,128)S(1)} %far_rows.1), channel_id=1, source_target_pairs={{0,4},{2,6},{4,0},{6,2},{1,5},{3,7},{5,1},{7,3},{8,12},{10,14},{12... | collective-permute-start | bytes 24584 | tf_op jit(solution)/shard_map/ppermute | solution.py:669
  7.9 5.2 %copy-start.3 = (f32[80,192]{1,0:T(8,128)S(1)}, f32[80,192]{1,0:T(8,128)}, u32[]{:S(2)}) copy-start(f32[80,192]{1,0:T(8,128)} %constant.10.clone.refs_7_) | copy-start | bytes 184324
  7.9 5.2 %copy-start.5 = (f32[8,128]{1,0:T(8,128)S(1)}, f32[8,128]{1,0:T(8,128)}, u32[]{:S(2)}) copy-start(f32[8,128]{1,0:T(8,128)} %constant.11.clone.refs_8_) | copy-start | bytes 12292
  7.9 5.2 %collective-permute-start.1 = (f32[280,128]{1,0:T(8,128)S(1)}, f32[280,128]{1,0:T(8,128)S(1)}, u32[]{:S(2)}, u32[]{:S(2)}) collective-permute-start(f32[280,128]{1,0:T(8,128)S(1)} %get-tuple-element.22), channel_id=1, source_target_pairs={{2,4},{4,2},{3,5},{5,3},{10,12},{12,10},{11,13},{13,11},{18,20},{2... | collective-permute-start | bytes 430088 | tf_op jit(solution)/shard_map/ppermute | solution.py:668
  10.4 4.0 %copy-start.1 = (f32[384,128]{1,0:T(8,128)S(1)}, f32[384,128]{1,0:T(8,128)}, u32[]{:S(2)}) copy-start(f32[384,128]{1,0:T(8,128)} %constant.12.clone.refs_7_.refs_12_) | copy-start | bytes 589828
  10.4 4.0 %copy-start.4 = (f32[8,384]{1,0:T(8,128)S(1)}, f32[8,384]{1,0:T(8,128)}, u32[]{:S(2)}) copy-start(f32[8,384]{1,0:T(8,128)} %constant.13.clone.refs_8_.refs_13_) | copy-start | bytes 36868
  10.4 6.4 %collective-permute-start.3 = (f32[64,128]{1,0:T(8,128)S(1)}, f32[64,128]{1,0:T(8,128)S(1)}, u32[]{:S(2)}, u32[]{:S(2)}) collective-permute-start(f32[64,128]{1,0:T(8,128)S(1)} %get-tuple-element.26.refs_3_), channel_id=1, source_target_pairs={{0,1},{1,0},{8,9},{9,8},{16,17},{17,16},{24,25},{25,24},{2,3},{3,2... | collective-permute-start | bytes 98312 | tf_op jit(solution)/shard_map/ppermute | solution.py:683
  10.5 6.3 %collective-permute-start.4 = (f32[64,128]{1,0:T(8,128)S(1)}, f32[64,128]{1,0:T(8,128)S(1)}, u32[]{:S(2)}, u32[]{:S(2)}) collective-permute-start(f32[64,128]{1,0:T(8,128)S(1)} %get-tuple-element.27.refs_4_), channel_id=1, source_target_pairs={{0,25},{1,8},{8,1},{9,16},{16,9},{17,24},{24,17},{25,0},{2,27},{3,... | collective-permute-start | bytes 98312 | tf_op jit(solution)/shard_map/ppermute | solution.py:684
  13.7 3.1 %collective-permute-start.5 = (f32[112,128]{1,0:T(8,128)S(1)}, f32[112,128]{1,0:T(8,128)S(1)}, u32[]{:S(2)}, u32[]{:S(2)}) collective-permute-start(f32[112,128]{1,0:T(8,128)S(1)} %get-tuple-element.28.refs_5_), channel_id=1, source_target_pairs={{0,1},{1,0},{8,9},{9,8},{16,17},{17,16},{24,25},{25,24},{2,3},{3,2... | collective-permute-start | bytes 172040 | tf_op jit(solution)/shard_map/ppermute | solution.py:707
  13.8 4.8 %collective-permute-start.6 = (f32[112,128]{1,0:T(8,128)S(1)}, f32[112,128]{1,0:T(8,128)S(1)}, u32[]{:S(2)}, u32[]{:S(2)}) collective-permute-start(f32[112,128]{1,0:T(8,128)S(1)} %get-tuple-element.29.refs_6_), channel_id=1, source_target_pairs={{0,25},{1,8},{8,1},{9,16},{16,9},{17,24},{24,17},{25,0},{2,27},{3,... | collective-permute-start | bytes 172040 | tf_op jit(solution)/shard_map/ppermute | solution.py:708

commit v7 on v6

--- a/solution.py
+++ b/solution.py
@@ -231,7 +231,7 @@
         yb[pl.ds(row, 8), :] = jnp.where(y_even, left, right)
         return carry
 
-    lax.fori_loop(0, height // 8, body, 0)
+    lax.fori_loop(0, height // 8, body, 0, unroll=2)
 
 
 def column_kernel(
@@ -391,7 +391,7 @@
                 post2[i, x - 1, pl.ds(row, 8), :] = moved(i, p[i])
         return carry
 
-    lax.fori_loop(0, rows // 8 - 2, body, 0)
+    lax.fori_loop(0, rows // 8 - 2, body, 0, unroll=2)
 
     flow_own[...] = dot3(linear[0:3].reshape(3 * rows, 128), wy[0:128, :])
     flow_own[0:rows, :] += linear[3]

time: 21.4 us -> 21.1 us (0.986)
  Pallas kernels: 8.78 us -> 7.86 us
  waiting for transfers between devices: 1.8 us -> 2.43 us
    ppermute x1, waiting for transfers between devices: 1.78 us -> 2.42 us  [shards(): qb = lax.ppermute(yb, ('gy', 'col'), ring_pairs(ny, 1))]
    pallas_call x1, Pallas kernels: 2.38 us -> 1.74 us  [shards(): pl.pallas_call(lambda *refs: interior_kernel(nz, *refs), out_shape=(f32(1...]
    pallas_call x1, Pallas kernels: 1.69 us -> 1.41 us  [shards(): pl.pallas_call(lambda *refs: bulk_kernel(nz, *refs), out_shape=(f32(19, 4...]
  transfers between devices with their start and end apart: 7 -> 7, of which waited for: 1 -> 1; matrix products, arithmetic and copies ran while one was open for 0% -> 0% of each run, Pallas kernels for 22% -> 18%
where the time goes in v7:
time: 21.1 us; the launch traced here: 20.9 us
  starting transfers between devices  9.79 us (46%)
  Pallas kernels  7.86 us (37%)
  waiting for transfers between devices  2.43 us (12%)
  between operations  0.79 us (4%)
    ppermute x1, starting transfers between devices, shards(): ra = lax.ppermute(za, 'gz', swap_pairs(nz, 0))  3.09 us
    pallas_call x1, Pallas kernels, shards(): pl.pallas_call(lambda *refs: final_kernel(nz, *refs), out_shape=(f32(3, h...  2.59 us
    ppermute x1, starting transfers between devices, shards(): rc = lax.ppermute(z2, 'gz', swap_pairs(nz, 0, 2))  2.59 us
    ppermute x1, starting transfers between devices, shards(): pb = lax.ppermute(sb, ('gy', 'col'), ring_pairs(ny, 1))  2.55 us
    ppermute x1, waiting for transfers between devices, shards(): qb = lax.ppermute(yb, ('gy', 'col'), ring_pairs(ny, 1))  2.42 us
    pallas_call x1, Pallas kernels, shards(): pl.pallas_call(lambda *refs: interior_kernel(nz, *refs), out_shape=(f32(1...  1.74 us
    pallas_call x1, Pallas kernels, shards(): pl.pallas_call(lambda *refs: edge_kernel(nz, *refs), out_shape=(f32(messa...  1.52 us
    pallas_call x1, Pallas kernels, shards(): pl.pallas_call(lambda *refs: bulk_kernel(nz, *refs), out_shape=(f32(19, 4...  1.41 us
  transfers between devices with their start and end apart: 7, of which 1 were waited for; matrix products, arithmetic and copies ran while one was open for 0% of the time, Pallas kernels for 18%

profile of v7, /device:TPU:0, one launch (start us, length us, event | category | flops | bytes accessed | tf_op | source)
XLA Modules:
  0.0 20.9 jit_solution(17873263115854949985)
XLA Ops:
  0.6 0.0 copy-start.2
  0.6 0.0 copy-start
  0.7 1.5 %edge_rows.1 = (f32[280,128]{1,0:T(8,128)S(1)}, f32[280,128]{1,0:T(8,128)S(1)}) custom-call(f32[19,4,64,128]{3,2,1,0:T(8,128)} %refs_0_.3, s32[4,64,128]{2,1,0:T(8,128)} %refs_1_.3, f32[3,64,128]{2,1,0:T(8,128)} %refs_2_.1, f32[1,64]{1,0:T(1,128)} %bitcast.1, f32[3,64]{1,0:T(4,128)} %refs_4_.1, f32[3,64]{1,0:T(4,128)} %refs_5_.1), custom_call_target="tpu_custom_call" | custom-call | tf_op jit(solution)/shard_map/edge_rows/pallas_call | solution.py:645
  2.2 3.1 %collective-permute-start = (f32[280,128]{1,0:T(8,128)S(1)}, f32[280,128]{1,0:T(8,128)S(1)}, u32[]{:S(2)}, u32[]{:S(2)}) collective-permute-start(f32[280,128]{1,0:T(8,128)S(1)} %get-tuple-element.21.refs_0_.refs_2_), channel_id=1, source_target_pairs={{0,2},{2,0},{4,6},{6,4},{1,3},{3,1},{5,7},{7,5},{8,10},{10,8},{12,... | collective-permute-start | bytes 430088 | tf_op jit(solution)/shard_map/ppermute | solution.py:667
  5.3 2.6 %collective-permute-start.2 = (f32[16,128]{1,0:T(8,128)S(1)}, f32[16,128]{1,0:T(8,128)S(1)}, u32[]{:S(2)}, u32[]{:S(2)}) collective-permute-start(f32[16,128]{1,0:T(8,128)S(1)} %far_rows.1), channel_id=1, source_target_pairs={{0,4},{2,6},{4,0},{6,2},{1,5},{3,7},{5,1},{7,3},{8,12},{10,14},{12... | collective-permute-start | bytes 24584 | tf_op jit(solution)/shard_map/ppermute | solution.py:669
  7.9 0.0 copy-start.3
  7.9 0.0 copy-start.5
  7.9 0.8 %collective-permute-start.1 = (f32[280,128]{1,0:T(8,128)S(1)}, f32[280,128]{1,0:T(8,128)S(1)}, u32[]{:S(2)}, u32[]{:S(2)}) collective-permute-start(f32[280,128]{1,0:T(8,128)S(1)} %get-tuple-element.22), channel_id=1, source_target_pairs={{2,4},{4,2},{3,5},{5,3},{10,12},{12,10},{11,13},{13,11},{18,20},{2... | collective-permute-start | bytes 430088 | tf_op jit(solution)/shard_map/ppermute | solution.py:668
  8.7 0.0 copy-done.2
  8.7 0.0 copy-done
  8.7 1.4 %bulk.1 = (f32[19,4,80,128]{3,2,1,0:T(8,128)S(1)}, f32[4,80,128]{2,1,0:T(8,128)S(1)}, f32[64,128]{1,0:T(8,128)S(1)}, f32[64,128]{1,0:T(8,128)S(1)}) custom-call(f32[19,4,64,128]{3,2,1,0:T(8,128)S(1)} %copy-done, s32[4,64,128]{2,1,0:T(8,128)S(1)} %copy-done.2), custom_call_target="tpu_custom_call" | custom-call | flops 4000000000 | bytes 8000000 | tf_op jit(solution)/shard_map/bulk/pallas_call | solution.py:673
  10.1 0.0 copy-start.1
  10.1 0.0 copy-start.4
  10.1 0.1 collective-permute-start.3
  10.2 2.5 %collective-permute-start.4 = (f32[64,128]{1,0:T(8,128)S(1)}, f32[64,128]{1,0:T(8,128)S(1)}, u32[]{:S(2)}, u32[]{:S(2)}) collective-permute-start(f32[64,128]{1,0:T(8,128)S(1)} %get-tuple-element.27.refs_4_), channel_id=1, source_target_pairs={{0,25},{1,8},{8,1},{9,16},{16,9},{17,24},{24,17},{25,0},{2,27},{3,... | collective-permute-start | bytes 98312 | tf_op jit(solution)/shard_map/ppermute | solution.py:684
  12.8 0.0 collective-permute-done.2.refs_5_
  12.8 0.0 collective-permute-done.1.refs_4_
  12.8 0.0 collective-permute-done.refs_3_
  12.8 0.0 copy-done.3
  12.8 0.0 copy-done.5
  12.8 0.6 %columns.1 = (f32[19,4,80,128]{3,2,1,0:T(8,128)S(1)}, f32[4,80,128]{2,1,0:T(8,128)S(1)}, f32[112,128]{1,0:T(8,128)S(1)}, f32[112,128]{1,0:T(8,128)S(1)}, f32[4,8...) custom-call(f32[19,4,80,128]{3,2,1,0:T(8,128)S(1)} %get-tuple-element.19.refs_0_, ...), custom_call_target="tpu_custom_call", output_to_operand_aliasing={{0}: (0, {}), {1}: (1, {})} | custom-call | tf_op jit(solution)/shard_map/columns/pallas_call | solution.py:691
  13.4 0.1 collective-permute-start.5
  13.5 0.6 %collective-permute-start.6 = (f32[112,128]{1,0:T(8,128)S(1)}, f32[112,128]{1,0:T(8,128)S(1)}, u32[]{:S(2)}, u32[]{:S(2)}) collective-permute-start(f32[112,128]{1,0:T(8,128)S(1)} %get-tuple-element.29.refs_6_), channel_id=1, source_target_pairs={{0,25},{1,8},{8,1},{9,16},{16,9},{17,24},{24,17},{25,0},{2,27},{3,... | collective-permute-start | bytes 172040 | tf_op jit(solution)/shard_map/ppermute | solution.py:708
  14.1 0.0 copy-done.1
  14.1 0.0 copy-done.4
  14.1 1.7 %interior.1 = (f32[19,3,80,128]{3,2,1,0:T(8,128)S(1)}, f32[240,128]{1,0:T(8,128)S(1)}, f32[24,128]{1,0:T(8,128)S(1)}, f32[144,128]{1,0:T(8,128)S(1)}, f32[144,128]{1,0:T(8,128)S(1)}) custom-call(f32[19,4,80,128]{3,2,1,0:T(8,128)S(1)} %get-tuple-element.23.refs_0_, f32[4,80,128]{2,1,0:T(8,128)S(1)} %get-tuple-element.24.refs_1_, ...), custom_call_target="tpu_custom_call" | custom-call | flops 4000000000 | bytes 8000000 | tf_op jit(solution)/shard_map/interior/pallas_call | solution.py:718
  15.9 0.0 collective-permute-done.3.refs_8_
  15.9 0.0 collective-permute-done.4.refs_9_
  15.9 0.0 collective-permute-done.5.refs_10_
  15.9 2.4 %collective-permute-done.6.refs_11_ = f32[112,128]{1,0:T(8,128)S(1)} collective-permute-done((f32[112,128]{1,0:T(8,128)S(1)}, f32[112,128]{1,0:T(8,128)S(1)}, u32[]{:S(2)}, u32[]{:S(2)}) %collective-permute-start.6) | collective-permute-done | bytes 57376 | tf_op jit(solution)/shard_map/ppermute | solution.py:708
  18.3 2.6 %stream.1 = (f32[3,64,128]{2,1,0:T(8,128)}, f32[19,4,64,128]{3,2,1,0:T(8,128)}) custom-call(f32[19,4,80,128]{3,2,1,0:T(8,128)S(1)} %get-tuple-element.23.refs_0_, f32[4,80,128]{2,1,0:T(8,128)S(1)} %get-tuple-element.24.refs_1_, f32[19,3,80,128]{3,2,1,0:T(8,128)S(1)} %get-tuple-element.30.refs_2_, f32[240,128]{1,0:T(8,128)S(1)} %get-tuple-element.31.refs_3_, ...), custom_call_target="tpu_custom_call" | custom-call | tf_op jit(solution)/shard_map/stream/pallas_call | solution.py:730
  (2 shorter events, 0.0 us)
Async XLA Ops:
  0.6 8.0 %copy-start.2 = (s32[4,64,128]{2,1,0:T(8,128)S(1)}, s32[4,64,128]{2,1,0:T(8,128)}, u32[]{:S(2)}) copy-start(s32[4,64,128]{2,1,0:T(8,128)} %refs_1_.3) | copy-start | bytes 393220
  0.6 8.0 %copy-start = (f32[19,4,64,128]{3,2,1,0:T(8,128)S(1)}, f32[19,4,64,128]{3,2,1,0:T(8,128)}, u32[]{:S(2)}) copy-start(f32[19,4,64,128]{3,2,1,0:T(8,128)} %refs_0_.3) | copy-start | bytes 7471108
  2.2 10.6 %collective-permute-start = (f32[280,128]{1,0:T(8,128)S(1)}, f32[280,128]{1,0:T(8,128)S(1)}, u32[]{:S(2)}, u32[]{:S(2)}) collective-permute-start(f32[280,128]{1,0:T(8,128)S(1)} %get-tuple-element.21.refs_0_.refs_2_), channel_id=1, source_target_pairs={{0,2},{2,0},{4,6},{6,4},{1,3},{3,1},{5,7},{7,5},{8,10},{10,8},{12,... | collective-permute-start | bytes 430088 | tf_op jit(solution)/shard_map/ppermute | solution.py:667
  5.3 7.5 %collective-permute-start.2 = (f32[16,128]{1,0:T(8,128)S(1)}, f32[16,128]{1,0:T(8,128)S(1)}, u32[]{:S(2)}, u32[]{:S(2)}) collective-permute-start(f32[16,128]{1,0:T(8,128)S(1)} %far_rows.1), channel_id=1, source_target_pairs={{0,4},{2,6},{4,0},{6,2},{1,5},{3,7},{5,1},{7,3},{8,12},{10,14},{12... | collective-permute-start | bytes 24584 | tf_op jit(solution)/shard_map/ppermute | solution.py:669
  7.9 4.9 %copy-start.3 = (f32[80,192]{1,0:T(8,128)S(1)}, f32[80,192]{1,0:T(8,128)}, u32[]{:S(2)}) copy-start(f32[80,192]{1,0:T(8,128)} %constant.10.clone.refs_7_) | copy-start | bytes 184324
  7.9 4.9 %copy-start.5 = (f32[8,128]{1,0:T(8,128)S(1)}, f32[8,128]{1,0:T(8,128)}, u32[]{:S(2)}) copy-start(f32[8,128]{1,0:T(8,128)} %constant.11.clone.refs_8_) | copy-start | bytes 12292
  7.9 4.9 %collective-permute-start.1 = (f32[280,128]{1,0:T(8,128)S(1)}, f32[280,128]{1,0:T(8,128)S(1)}, u32[]{:S(2)}, u32[]{:S(2)}) collective-permute-start(f32[280,128]{1,0:T(8,128)S(1)} %get-tuple-element.22), channel_id=1, source_target_pairs={{2,4},{4,2},{3,5},{5,3},{10,12},{12,10},{11,13},{13,11},{18,20},{2... | collective-permute-start | bytes 430088 | tf_op jit(solution)/shard_map/ppermute | solution.py:668
  10.1 4.0 %copy-start.1 = (f32[384,128]{1,0:T(8,128)S(1)}, f32[384,128]{1,0:T(8,128)}, u32[]{:S(2)}) copy-start(f32[384,128]{1,0:T(8,128)} %constant.12.clone.refs_7_.refs_12_) | copy-start | bytes 589828
  10.1 4.0 %copy-start.4 = (f32[8,384]{1,0:T(8,128)S(1)}, f32[8,384]{1,0:T(8,128)}, u32[]{:S(2)}) copy-start(f32[8,384]{1,0:T(8,128)} %constant.13.clone.refs_8_.refs_13_) | copy-start | bytes 36868
  10.1 5.7 %collective-permute-start.3 = (f32[64,128]{1,0:T(8,128)S(1)}, f32[64,128]{1,0:T(8,128)S(1)}, u32[]{:S(2)}, u32[]{:S(2)}) collective-permute-start(f32[64,128]{1,0:T(8,128)S(1)} %get-tuple-element.26.refs_3_), channel_id=1, source_target_pairs={{0,1},{1,0},{8,9},{9,8},{16,17},{17,16},{24,25},{25,24},{2,3},{3,2... | collective-permute-start | bytes 98312 | tf_op jit(solution)/shard_map/ppermute | solution.py:683
  10.2 5.7 %collective-permute-start.4 = (f32[64,128]{1,0:T(8,128)S(1)}, f32[64,128]{1,0:T(8,128)S(1)}, u32[]{:S(2)}, u32[]{:S(2)}) collective-permute-start(f32[64,128]{1,0:T(8,128)S(1)} %get-tuple-element.27.refs_4_), channel_id=1, source_target_pairs={{0,25},{1,8},{8,1},{9,16},{16,9},{17,24},{24,17},{25,0},{2,27},{3,... | collective-permute-start | bytes 98312 | tf_op jit(solution)/shard_map/ppermute | solution.py:684
  13.4 2.5 %collective-permute-start.5 = (f32[112,128]{1,0:T(8,128)S(1)}, f32[112,128]{1,0:T(8,128)S(1)}, u32[]{:S(2)}, u32[]{:S(2)}) collective-permute-start(f32[112,128]{1,0:T(8,128)S(1)} %get-tuple-element.28.refs_5_), channel_id=1, source_target_pairs={{0,1},{1,0},{8,9},{9,8},{16,17},{17,16},{24,25},{25,24},{2,3},{3,2... | collective-permute-start | bytes 172040 | tf_op jit(solution)/shard_map/ppermute | solution.py:707
  13.5 4.8 %collective-permute-start.6 = (f32[112,128]{1,0:T(8,128)S(1)}, f32[112,128]{1,0:T(8,128)S(1)}, u32[]{:S(2)}, u32[]{:S(2)}) collective-permute-start(f32[112,128]{1,0:T(8,128)S(1)} %get-tuple-element.29.refs_6_), channel_id=1, source_target_pairs={{0,25},{1,8},{8,1},{9,16},{16,9},{17,24},{24,17},{25,0},{2,27},{3,... | collective-permute-start | bytes 172040 | tf_op jit(solution)/shard_map/ppermute | solution.py:708

commit v8 on v5

--- a/solution.py
+++ b/solution.py
@@ -232,7 +232,7 @@
         yb[pl.ds(row, 8), :] = jnp.where(y_even, left, right)
         return carry
 
-    lax.fori_loop(0, height // 8, body, 0)
+    lax.fori_loop(0, height // 8, body, 0, unroll=2)
 
 
 def column_kernel(
@@ -395,7 +395,7 @@
                 post2[i, x - 1, pl.ds(row, 8), :] = moved(i, p[i])
         return carry
 
-    lax.fori_loop(0, rows // 8 - 2, body, 0)
+    lax.fori_loop(0, rows // 8 - 2, body, 0, unroll=2)
 
     flow_own[...] = dot3(linear[0:3].reshape(3 * rows, 128), wy[0:128, :])
     flow_own[0:rows, :] += linear[3]

time: 21.5 us -> 21.1 us (0.981)
  Pallas kernels: 8.32 us -> 7.64 us
  waiting for transfers between devices: 2.36 us -> 2.68 us
    pallas_call x1, Pallas kernels: 1.88 us -> 1.51 us  [shards(): pl.pallas_call(lambda *refs: bulk_kernel(nz, *refs), out_shape=(f32(19, 4...]
    ppermute x1, waiting for transfers between devices: 2.35 us -> 2.66 us  [shards(): qb = lax.ppermute(yb, ('gy', 'col'), ring_pairs(ny, 1))]
    pallas_call x1, Pallas kernels: 1.81 us -> 1.49 us  [shards(): pl.pallas_call(lambda *refs: interior_kernel(nz, *refs), out_shape=(f32(1...]
  transfers between devices with their start and end apart: 7 -> 7, of which waited for: 1 -> 1; matrix products, arithmetic and copies ran while one was open for 0% -> 0% of each run, Pallas kernels for 20% -> 17%
where the time goes in v8:
time: 21.1 us; the launch traced here: 20.9 us
  starting transfers between devices  9.79 us (46%)
  Pallas kernels  7.64 us (36%)
  waiting for transfers between devices  2.68 us (13%)
  between operations  0.79 us (4%)
    ppermute x1, starting transfers between devices, shards(): ra = lax.ppermute(za, 'gz', swap_pairs(nz, 0))  3.09 us
    ppermute x1, waiting for transfers between devices, shards(): qb = lax.ppermute(yb, ('gy', 'col'), ring_pairs(ny, 1))  2.66 us
    ppermute x1, starting transfers between devices, shards(): rc = lax.ppermute(z2, 'gz', swap_pairs(nz, 0, 2))  2.59 us
    ppermute x1, starting transfers between devices, shards(): pb = lax.ppermute(sb, ('gy', 'col'), ring_pairs(ny, 1))  2.55 us
    pallas_call x1, Pallas kernels, shards(): pl.pallas_call(lambda *refs: final_kernel(nz, *refs), out_shape=(f32(3, h...  2.46 us
    pallas_call x1, Pallas kernels, shards(): pl.pallas_call(lambda *refs: edge_kernel(nz, *refs), out_shape=(f32(messa...  1.52 us
    pallas_call x1, Pallas kernels, shards(): pl.pallas_call(lambda *refs: bulk_kernel(nz, *refs), out_shape=(f32(19, 4...  1.51 us
    pallas_call x1, Pallas kernels, shards(): pl.pallas_call(lambda *refs: interior_kernel(nz, *refs), out_shape=(f32(1...  1.49 us
  transfers between devices with their start and end apart: 7, of which 1 were waited for; matrix products, arithmetic and copies ran while one was open for 0% of the time, Pallas kernels for 17%

profile of v8, /device:TPU:0, one launch (start us, length us, event | category | flops | bytes accessed | tf_op | source)
XLA Modules:
  0.0 20.9 jit_solution(10384443488691485291)
XLA Ops:
  0.6 0.0 copy-start.2
  0.6 0.0 copy-start
  0.7 1.5 %edge_rows.1 = (f32[280,128]{1,0:T(8,128)S(1)}, f32[280,128]{1,0:T(8,128)S(1)}) custom-call(f32[19,4,64,128]{3,2,1,0:T(8,128)} %refs_0_.3, s32[4,64,128]{2,1,0:T(8,128)} %refs_1_.3, f32[3,64,128]{2,1,0:T(8,128)} %refs_2_.1, f32[1,64]{1,0:T(1,128)} %bitcast.1, f32[3,64]{1,0:T(4,128)} %refs_4_.1, f32[3,64]{1,0:T(4,128)} %refs_5_.1), custom_call_target="tpu_custom_call" | custom-call | tf_op jit(solution)/shard_map/edge_rows/pallas_call | solution.py:649
  2.2 3.1 %collective-permute-start = (f32[280,128]{1,0:T(8,128)S(1)}, f32[280,128]{1,0:T(8,128)S(1)}, u32[]{:S(2)}, u32[]{:S(2)}) collective-permute-start(f32[280,128]{1,0:T(8,128)S(1)} %get-tuple-element.21.refs_0_.refs_2_), channel_id=1, source_target_pairs={{0,2},{2,0},{4,6},{6,4},{1,3},{3,1},{5,7},{7,5},{8,10},{10,8},{12,... | collective-permute-start | bytes 430088 | tf_op jit(solution)/shard_map/ppermute | solution.py:671
  5.3 2.6 %collective-permute-start.2 = (f32[16,128]{1,0:T(8,128)S(1)}, f32[16,128]{1,0:T(8,128)S(1)}, u32[]{:S(2)}, u32[]{:S(2)}) collective-permute-start(f32[16,128]{1,0:T(8,128)S(1)} %far_rows.1), channel_id=1, source_target_pairs={{0,4},{2,6},{4,0},{6,2},{1,5},{3,7},{5,1},{7,3},{8,12},{10,14},{12... | collective-permute-start | bytes 24584 | tf_op jit(solution)/shard_map/ppermute | solution.py:673
  7.9 0.0 copy-start.3
  7.9 0.0 copy-start.5
  7.9 0.8 %collective-permute-start.1 = (f32[280,128]{1,0:T(8,128)S(1)}, f32[280,128]{1,0:T(8,128)S(1)}, u32[]{:S(2)}, u32[]{:S(2)}) collective-permute-start(f32[280,128]{1,0:T(8,128)S(1)} %get-tuple-element.22), channel_id=1, source_target_pairs={{2,4},{4,2},{3,5},{5,3},{10,12},{12,10},{11,13},{13,11},{18,20},{2... | collective-permute-start | bytes 430088 | tf_op jit(solution)/shard_map/ppermute | solution.py:672
  8.7 0.0 copy-done.2
  8.7 0.0 copy-done
  8.7 1.5 %bulk.1 = (f32[19,4,80,128]{3,2,1,0:T(8,128)S(1)}, f32[4,80,128]{2,1,0:T(8,128)S(1)}, f32[64,128]{1,0:T(8,128)S(1)}, f32[64,128]{1,0:T(8,128)S(1)}) custom-call(f32[19,4,64,128]{3,2,1,0:T(8,128)S(1)} %copy-done, s32[4,64,128]{2,1,0:T(8,128)S(1)} %copy-done.2), custom_call_target="tpu_custom_call" | custom-call | flops 4000000000 | bytes 8000000 | tf_op jit(solution)/shard_map/bulk/pallas_call | solution.py:677
  10.2 0.0 copy-start.1
  10.2 0.0 copy-start.4
  10.2 0.1 collective-permute-start.3
  10.3 2.5 %collective-permute-start.4 = (f32[64,128]{1,0:T(8,128)S(1)}, f32[64,128]{1,0:T(8,128)S(1)}, u32[]{:S(2)}, u32[]{:S(2)}) collective-permute-start(f32[64,128]{1,0:T(8,128)S(1)} %get-tuple-element.27.refs_4_), channel_id=1, source_target_pairs={{0,25},{1,8},{8,1},{9,16},{16,9},{17,24},{24,17},{25,0},{2,27},{3,... | collective-permute-start | bytes 98312 | tf_op jit(solution)/shard_map/ppermute | solution.py:688
  12.9 0.0 collective-permute-done.2.refs_5_
  12.9 0.0 collective-permute-done.1.refs_4_
  12.9 0.0 collective-permute-done.refs_3_
  12.9 0.0 copy-done.3
  12.9 0.0 copy-done.5
  12.9 0.7 %columns.1 = (f32[19,4,80,128]{3,2,1,0:T(8,128)S(1)}, f32[4,80,128]{2,1,0:T(8,128)S(1)}, f32[112,128]{1,0:T(8,128)S(1)}, f32[112,128]{1,0:T(8,128)S(1)}, f32[4,8...) custom-call(f32[19,4,80,128]{3,2,1,0:T(8,128)S(1)} %get-tuple-element.19.refs_0_, ...), custom_call_target="tpu_custom_call", output_to_operand_aliasing={{0}: (0, {}), {1}: (1, {})} | custom-call | tf_op jit(solution)/shard_map/columns/pallas_call | solution.py:695
  13.6 0.1 collective-permute-start.5
  13.6 0.6 %collective-permute-start.6 = (f32[112,128]{1,0:T(8,128)S(1)}, f32[112,128]{1,0:T(8,128)S(1)}, u32[]{:S(2)}, u32[]{:S(2)}) collective-permute-start(f32[112,128]{1,0:T(8,128)S(1)} %get-tuple-element.29.refs_6_), channel_id=1, source_target_pairs={{0,25},{1,8},{8,1},{9,16},{16,9},{17,24},{24,17},{25,0},{2,27},{3,... | collective-permute-start | bytes 172040 | tf_op jit(solution)/shard_map/ppermute | solution.py:712
  14.3 0.0 copy-done.1
  14.3 0.0 copy-done.4
  14.3 1.5 %interior.1 = (f32[19,3,80,128]{3,2,1,0:T(8,128)S(1)}, f32[240,128]{1,0:T(8,128)S(1)}, f32[24,128]{1,0:T(8,128)S(1)}, f32[144,128]{1,0:T(8,128)S(1)}, f32[144,128]{1,0:T(8,128)S(1)}) custom-call(f32[19,4,80,128]{3,2,1,0:T(8,128)S(1)} %get-tuple-element.23.refs_0_, f32[4,80,128]{2,1,0:T(8,128)S(1)} %get-tuple-element.24.refs_1_, ...), custom_call_target="tpu_custom_call" | custom-call | flops 4000000000 | bytes 8000000 | tf_op jit(solution)/shard_map/interior/pallas_call | solution.py:722
  15.8 0.0 collective-permute-done.3.refs_8_
  15.8 0.0 collective-permute-done.4.refs_9_
  15.8 0.0 collective-permute-done.5.refs_10_
  15.8 2.7 %collective-permute-done.6.refs_11_ = f32[112,128]{1,0:T(8,128)S(1)} collective-permute-done((f32[112,128]{1,0:T(8,128)S(1)}, f32[112,128]{1,0:T(8,128)S(1)}, u32[]{:S(2)}, u32[]{:S(2)}) %collective-permute-start.6) | collective-permute-done | bytes 57376 | tf_op jit(solution)/shard_map/ppermute | solution.py:712
  18.5 2.5 %stream.1 = (f32[3,64,128]{2,1,0:T(8,128)}, f32[19,4,64,128]{3,2,1,0:T(8,128)}) custom-call(f32[19,4,80,128]{3,2,1,0:T(8,128)S(1)} %get-tuple-element.23.refs_0_, f32[4,80,128]{2,1,0:T(8,128)S(1)} %get-tuple-element.24.refs_1_, f32[19,3,80,128]{3,2,1,0:T(8,128)S(1)} %get-tuple-element.30.refs_2_, f32[240,128]{1,0:T(8,128)S(1)} %get-tuple-element.31.refs_3_, ...), custom_call_target="tpu_custom_call" | custom-call | tf_op jit(solution)/shard_map/stream/pallas_call | solution.py:734
  (2 shorter events, 0.0 us)
Async XLA Ops:
  0.6 8.0 %copy-start.2 = (s32[4,64,128]{2,1,0:T(8,128)S(1)}, s32[4,64,128]{2,1,0:T(8,128)}, u32[]{:S(2)}) copy-start(s32[4,64,128]{2,1,0:T(8,128)} %refs_1_.3) | copy-start | bytes 393220
  0.6 8.0 %copy-start = (f32[19,4,64,128]{3,2,1,0:T(8,128)S(1)}, f32[19,4,64,128]{3,2,1,0:T(8,128)}, u32[]{:S(2)}) copy-start(f32[19,4,64,128]{3,2,1,0:T(8,128)} %refs_0_.3) | copy-start | bytes 7471108
  2.2 10.7 %collective-permute-start = (f32[280,128]{1,0:T(8,128)S(1)}, f32[280,128]{1,0:T(8,128)S(1)}, u32[]{:S(2)}, u32[]{:S(2)}) collective-permute-start(f32[280,128]{1,0:T(8,128)S(1)} %get-tuple-element.21.refs_0_.refs_2_), channel_id=1, source_target_pairs={{0,2},{2,0},{4,6},{6,4},{1,3},{3,1},{5,7},{7,5},{8,10},{10,8},{12,... | collective-permute-start | bytes 430088 | tf_op jit(solution)/shard_map/ppermute | solution.py:671
  5.3 7.6 %collective-permute-start.2 = (f32[16,128]{1,0:T(8,128)S(1)}, f32[16,128]{1,0:T(8,128)S(1)}, u32[]{:S(2)}, u32[]{:S(2)}) collective-permute-start(f32[16,128]{1,0:T(8,128)S(1)} %far_rows.1), channel_id=1, source_target_pairs={{0,4},{2,6},{4,0},{6,2},{1,5},{3,7},{5,1},{7,3},{8,12},{10,14},{12... | collective-permute-start | bytes 24584 | tf_op jit(solution)/shard_map/ppermute | solution.py:673
  7.9 5.0 %copy-start.3 = (f32[80,192]{1,0:T(8,128)S(1)}, f32[80,192]{1,0:T(8,128)}, u32[]{:S(2)}) copy-start(f32[80,192]{1,0:T(8,128)} %constant.10.clone.refs_7_) | copy-start | bytes 184324
  7.9 5.0 %copy-start.5 = (f32[8,128]{1,0:T(8,128)S(1)}, f32[8,128]{1,0:T(8,128)}, u32[]{:S(2)}) copy-start(f32[8,128]{1,0:T(8,128)} %constant.11.clone.refs_8_) | copy-start | bytes 12292
  7.9 5.0 %collective-permute-start.1 = (f32[280,128]{1,0:T(8,128)S(1)}, f32[280,128]{1,0:T(8,128)S(1)}, u32[]{:S(2)}, u32[]{:S(2)}) collective-permute-start(f32[280,128]{1,0:T(8,128)S(1)} %get-tuple-element.22), channel_id=1, source_target_pairs={{2,4},{4,2},{3,5},{5,3},{10,12},{12,10},{11,13},{13,11},{18,20},{2... | collective-permute-start | bytes 430088 | tf_op jit(solution)/shard_map/ppermute | solution.py:672
  10.2 4.1 %copy-start.1 = (f32[384,128]{1,0:T(8,128)S(1)}, f32[384,128]{1,0:T(8,128)}, u32[]{:S(2)}) copy-start(f32[384,128]{1,0:T(8,128)} %constant.12.clone.refs_7_.refs_12_) | copy-start | bytes 589828
  10.2 4.1 %copy-start.4 = (f32[8,384]{1,0:T(8,128)S(1)}, f32[8,384]{1,0:T(8,128)}, u32[]{:S(2)}) copy-start(f32[8,384]{1,0:T(8,128)} %constant.13.clone.refs_8_.refs_13_) | copy-start | bytes 36868
  10.2 5.6 %collective-permute-start.3 = (f32[64,128]{1,0:T(8,128)S(1)}, f32[64,128]{1,0:T(8,128)S(1)}, u32[]{:S(2)}, u32[]{:S(2)}) collective-permute-start(f32[64,128]{1,0:T(8,128)S(1)} %get-tuple-element.26.refs_3_), channel_id=1, source_target_pairs={{0,1},{1,0},{8,9},{9,8},{16,17},{17,16},{24,25},{25,24},{2,3},{3,2... | collective-permute-start | bytes 98312 | tf_op jit(solution)/shard_map/ppermute | solution.py:687
  10.3 5.5 %collective-permute-start.4 = (f32[64,128]{1,0:T(8,128)S(1)}, f32[64,128]{1,0:T(8,128)S(1)}, u32[]{:S(2)}, u32[]{:S(2)}) collective-permute-start(f32[64,128]{1,0:T(8,128)S(1)} %get-tuple-element.27.refs_4_), channel_id=1, source_target_pairs={{0,25},{1,8},{8,1},{9,16},{16,9},{17,24},{24,17},{25,0},{2,27},{3,... | collective-permute-start | bytes 98312 | tf_op jit(solution)/shard_map/ppermute | solution.py:688
  13.6 2.2 %collective-permute-start.5 = (f32[112,128]{1,0:T(8,128)S(1)}, f32[112,128]{1,0:T(8,128)S(1)}, u32[]{:S(2)}, u32[]{:S(2)}) collective-permute-start(f32[112,128]{1,0:T(8,128)S(1)} %get-tuple-element.28.refs_5_), channel_id=1, source_target_pairs={{0,1},{1,0},{8,9},{9,8},{16,17},{17,16},{24,25},{25,24},{2,3},{3,2... | collective-permute-start | bytes 172040 | tf_op jit(solution)/shard_map/ppermute | solution.py:711
  13.6 4.8 %collective-permute-start.6 = (f32[112,128]{1,0:T(8,128)S(1)}, f32[112,128]{1,0:T(8,128)S(1)}, u32[]{:S(2)}, u32[]{:S(2)}) collective-permute-start(f32[112,128]{1,0:T(8,128)S(1)} %get-tuple-element.29.refs_6_), channel_id=1, source_target_pairs={{0,25},{1,8},{8,1},{9,16},{16,9},{17,24},{24,17},{25,0},{2,27},{3,... | collective-permute-start | bytes 172040 | tf_op jit(solution)/shard_map/ppermute | solution.py:712

commit v9 on v8

--- a/solution.py
+++ b/solution.py
@@ -586,7 +586,7 @@
         return carry
 
     tiles = height // 8
-    lax.fori_loop(1, tiles, main, 0)
+    lax.fori_loop(1, tiles, main, 0, unroll=True)
     last(tiles - 1)
     for t in range(tiles):
         out_copy(t).wait()

time: 21.1 us -> 20.9 us (level)
    pallas_call x1, Pallas kernels: 2.46 us -> 2.25 us  [shards(): pl.pallas_call(lambda *refs: final_kernel(nz, *refs), out_shape=(f32(3, h...]
  transfers between devices with their start and end apart: 7 -> 7, of which waited for: 1 -> 1; matrix products, arithmetic and copies ran while one was open for 0% -> 0% of each run, Pallas kernels for 17% -> 18%
where the time goes in v9:
time: 20.9 us; the launch traced here: 20.7 us
  starting transfers between devices  9.79 us (47%)
  Pallas kernels  7.43 us (36%)
  waiting for transfers between devices  2.68 us (13%)
  between operations  0.79 us (4%)
    ppermute x1, starting transfers between devices, shards(): ra = lax.ppermute(za, 'gz', swap_pairs(nz, 0))  3.09 us
    ppermute x1, waiting for transfers between devices, shards(): qb = lax.ppermute(yb, ('gy', 'col'), ring_pairs(ny, 1))  2.66 us
    ppermute x1, starting transfers between devices, shards(): rc = lax.ppermute(z2, 'gz', swap_pairs(nz, 0, 2))  2.59 us
    ppermute x1, starting transfers between devices, shards(): pb = lax.ppermute(sb, ('gy', 'col'), ring_pairs(ny, 1))  2.55 us
    pallas_call x1, Pallas kernels, shards(): pl.pallas_call(lambda *refs: final_kernel(nz, *refs), out_shape=(f32(3, h...  2.25 us
    pallas_call x1, Pallas kernels, shards(): pl.pallas_call(lambda *refs: edge_kernel(nz, *refs), out_shape=(f32(messa...  1.52 us
    pallas_call x1, Pallas kernels, shards(): pl.pallas_call(lambda *refs: bulk_kernel(nz, *refs), out_shape=(f32(19, 4...  1.51 us
    pallas_call x1, Pallas kernels, shards(): pl.pallas_call(lambda *refs: interior_kernel(nz, *refs), out_shape=(f32(1...  1.49 us
  transfers between devices with their start and end apart: 7, of which 1 were waited for; matrix products, arithmetic and copies ran while one was open for 0% of the time, Pallas kernels for 18%

profile of v9, /device:TPU:0, one launch (start us, length us, event | category | flops | bytes accessed | tf_op | source)
XLA Modules:
  0.0 20.7 jit_solution(12006511739907742090)
XLA Ops:
  0.6 0.0 copy-start.2
  0.6 0.0 copy-start
  0.7 1.5 %edge_rows.1 = (f32[280,128]{1,0:T(8,128)S(1)}, f32[280,128]{1,0:T(8,128)S(1)}) custom-call(f32[19,4,64,128]{3,2,1,0:T(8,128)} %refs_0_.3, s32[4,64,128]{2,1,0:T(8,128)} %refs_1_.3, f32[3,64,128]{2,1,0:T(8,128)} %refs_2_.1, f32[1,64]{1,0:T(1,128)} %bitcast.1, f32[3,64]{1,0:T(4,128)} %refs_4_.1, f32[3,64]{1,0:T(4,128)} %refs_5_.1), custom_call_target="tpu_custom_call" | custom-call | tf_op jit(solution)/shard_map/edge_rows/pallas_call | solution.py:649
  2.2 3.1 %collective-permute-start = (f32[280,128]{1,0:T(8,128)S(1)}, f32[280,128]{1,0:T(8,128)S(1)}, u32[]{:S(2)}, u32[]{:S(2)}) collective-permute-start(f32[280,128]{1,0:T(8,128)S(1)} %get-tuple-element.21.refs_0_.refs_2_), channel_id=1, source_target_pairs={{0,2},{2,0},{4,6},{6,4},{1,3},{3,1},{5,7},{7,5},{8,10},{10,8},{12,... | collective-permute-start | bytes 430088 | tf_op jit(solution)/shard_map/ppermute | solution.py:671
  5.3 2.6 %collective-permute-start.2 = (f32[16,128]{1,0:T(8,128)S(1)}, f32[16,128]{1,0:T(8,128)S(1)}, u32[]{:S(2)}, u32[]{:S(2)}) collective-permute-start(f32[16,128]{1,0:T(8,128)S(1)} %far_rows.1), channel_id=1, source_target_pairs={{0,4},{2,6},{4,0},{6,2},{1,5},{3,7},{5,1},{7,3},{8,12},{10,14},{12... | collective-permute-start | bytes 24584 | tf_op jit(solution)/shard_map/ppermute | solution.py:673
  7.9 0.0 copy-start.3
  7.9 0.0 copy-start.5
  7.9 0.8 %collective-permute-start.1 = (f32[280,128]{1,0:T(8,128)S(1)}, f32[280,128]{1,0:T(8,128)S(1)}, u32[]{:S(2)}, u32[]{:S(2)}) collective-permute-start(f32[280,128]{1,0:T(8,128)S(1)} %get-tuple-element.22), channel_id=1, source_target_pairs={{2,4},{4,2},{3,5},{5,3},{10,12},{12,10},{11,13},{13,11},{18,20},{2... | collective-permute-start | bytes 430088 | tf_op jit(solution)/shard_map/ppermute | solution.py:672
  8.7 0.0 copy-done.2
  8.7 0.0 copy-done
  8.7 1.5 %bulk.1 = (f32[19,4,80,128]{3,2,1,0:T(8,128)S(1)}, f32[4,80,128]{2,1,0:T(8,128)S(1)}, f32[64,128]{1,0:T(8,128)S(1)}, f32[64,128]{1,0:T(8,128)S(1)}) custom-call(f32[19,4,64,128]{3,2,1,0:T(8,128)S(1)} %copy-done, s32[4,64,128]{2,1,0:T(8,128)S(1)} %copy-done.2), custom_call_target="tpu_custom_call" | custom-call | flops 4000000000 | bytes 8000000 | tf_op jit(solution)/shard_map/bulk/pallas_call | solution.py:677
  10.2 0.0 copy-start.1
  10.2 0.0 copy-start.4
  10.2 0.1 collective-permute-start.3
  10.3 2.5 %collective-permute-start.4 = (f32[64,128]{1,0:T(8,128)S(1)}, f32[64,128]{1,0:T(8,128)S(1)}, u32[]{:S(2)}, u32[]{:S(2)}) collective-permute-start(f32[64,128]{1,0:T(8,128)S(1)} %get-tuple-element.27.refs_4_), channel_id=1, source_target_pairs={{0,25},{1,8},{8,1},{9,16},{16,9},{17,24},{24,17},{25,0},{2,27},{3,... | collective-permute-start | bytes 98312 | tf_op jit(solution)/shard_map/ppermute | solution.py:688
  12.9 0.0 collective-permute-done.2.refs_5_
  12.9 0.0 collective-permute-done.1.refs_4_
  12.9 0.0 collective-permute-done.refs_3_
  12.9 0.0 copy-done.3
  12.9 0.0 copy-done.5
  12.9 0.7 %columns.1 = (f32[19,4,80,128]{3,2,1,0:T(8,128)S(1)}, f32[4,80,128]{2,1,0:T(8,128)S(1)}, f32[112,128]{1,0:T(8,128)S(1)}, f32[112,128]{1,0:T(8,128)S(1)}, f32[4,8...) custom-call(f32[19,4,80,128]{3,2,1,0:T(8,128)S(1)} %get-tuple-element.19.refs_0_, ...), custom_call_target="tpu_custom_call", output_to_operand_aliasing={{0}: (0, {}), {1}: (1, {})} | custom-call | tf_op jit(solution)/shard_map/columns/pallas_call | solution.py:695
  13.6 0.1 collective-permute-start.5
  13.6 0.6 %collective-permute-start.6 = (f32[112,128]{1,0:T(8,128)S(1)}, f32[112,128]{1,0:T(8,128)S(1)}, u32[]{:S(2)}, u32[]{:S(2)}) collective-permute-start(f32[112,128]{1,0:T(8,128)S(1)} %get-tuple-element.29.refs_6_), channel_id=1, source_target_pairs={{0,25},{1,8},{8,1},{9,16},{16,9},{17,24},{24,17},{25,0},{2,27},{3,... | collective-permute-start | bytes 172040 | tf_op jit(solution)/shard_map/ppermute | solution.py:712
  14.3 0.0 copy-done.1
  14.3 0.0 copy-done.4
  14.3 1.5 %interior.1 = (f32[19,3,80,128]{3,2,1,0:T(8,128)S(1)}, f32[240,128]{1,0:T(8,128)S(1)}, f32[24,128]{1,0:T(8,128)S(1)}, f32[144,128]{1,0:T(8,128)S(1)}, f32[144,128]{1,0:T(8,128)S(1)}) custom-call(f32[19,4,80,128]{3,2,1,0:T(8,128)S(1)} %get-tuple-element.23.refs_0_, f32[4,80,128]{2,1,0:T(8,128)S(1)} %get-tuple-element.24.refs_1_, ...), custom_call_target="tpu_custom_call" | custom-call | flops 4000000000 | bytes 8000000 | tf_op jit(solution)/shard_map/interior/pallas_call | solution.py:722
  15.8 0.0 collective-permute-done.3.refs_8_
  15.8 0.0 collective-permute-done.4.refs_9_
  15.8 0.0 collective-permute-done.5.refs_10_
  15.8 2.7 %collective-permute-done.6.refs_11_ = f32[112,128]{1,0:T(8,128)S(1)} collective-permute-done((f32[112,128]{1,0:T(8,128)S(1)}, f32[112,128]{1,0:T(8,128)S(1)}, u32[]{:S(2)}, u32[]{:S(2)}) %collective-permute-start.6) | collective-permute-done | bytes 57376 | tf_op jit(solution)/shard_map/ppermute | solution.py:712
  18.5 2.2 %stream.1 = (f32[3,64,128]{2,1,0:T(8,128)}, f32[19,4,64,128]{3,2,1,0:T(8,128)}) custom-call(f32[19,4,80,128]{3,2,1,0:T(8,128)S(1)} %get-tuple-element.23.refs_0_, f32[4,80,128]{2,1,0:T(8,128)S(1)} %get-tuple-element.24.refs_1_, f32[19,3,80,128]{3,2,1,0:T(8,128)S(1)} %get-tuple-element.30.refs_2_, f32[240,128]{1,0:T(8,128)S(1)} %get-tuple-element.31.refs_3_, ...), custom_call_target="tpu_custom_call" | custom-call | tf_op jit(solution)/shard_map/stream/pallas_call | solution.py:734
  (2 shorter events, 0.0 us)
Async XLA Ops:
  0.6 8.0 %copy-start.2 = (s32[4,64,128]{2,1,0:T(8,128)S(1)}, s32[4,64,128]{2,1,0:T(8,128)}, u32[]{:S(2)}) copy-start(s32[4,64,128]{2,1,0:T(8,128)} %refs_1_.3) | copy-start | bytes 393220
  0.6 8.0 %copy-start = (f32[19,4,64,128]{3,2,1,0:T(8,128)S(1)}, f32[19,4,64,128]{3,2,1,0:T(8,128)}, u32[]{:S(2)}) copy-start(f32[19,4,64,128]{3,2,1,0:T(8,128)} %refs_0_.3) | copy-start | bytes 7471108
  2.2 10.7 %collective-permute-start = (f32[280,128]{1,0:T(8,128)S(1)}, f32[280,128]{1,0:T(8,128)S(1)}, u32[]{:S(2)}, u32[]{:S(2)}) collective-permute-start(f32[280,128]{1,0:T(8,128)S(1)} %get-tuple-element.21.refs_0_.refs_2_), channel_id=1, source_target_pairs={{0,2},{2,0},{4,6},{6,4},{1,3},{3,1},{5,7},{7,5},{8,10},{10,8},{12,... | collective-permute-start | bytes 430088 | tf_op jit(solution)/shard_map/ppermute | solution.py:671
  5.3 7.6 %collective-permute-start.2 = (f32[16,128]{1,0:T(8,128)S(1)}, f32[16,128]{1,0:T(8,128)S(1)}, u32[]{:S(2)}, u32[]{:S(2)}) collective-permute-start(f32[16,128]{1,0:T(8,128)S(1)} %far_rows.1), channel_id=1, source_target_pairs={{0,4},{2,6},{4,0},{6,2},{1,5},{3,7},{5,1},{7,3},{8,12},{10,14},{12... | collective-permute-start | bytes 24584 | tf_op jit(solution)/shard_map/ppermute | solution.py:673
  7.9 5.0 %copy-start.3 = (f32[80,192]{1,0:T(8,128)S(1)}, f32[80,192]{1,0:T(8,128)}, u32[]{:S(2)}) copy-start(f32[80,192]{1,0:T(8,128)} %constant.10.clone.refs_7_) | copy-start | bytes 184324
  7.9 5.0 %copy-start.5 = (f32[8,128]{1,0:T(8,128)S(1)}, f32[8,128]{1,0:T(8,128)}, u32[]{:S(2)}) copy-start(f32[8,128]{1,0:T(8,128)} %constant.11.clone.refs_8_) | copy-start | bytes 12292
  7.9 5.0 %collective-permute-start.1 = (f32[280,128]{1,0:T(8,128)S(1)}, f32[280,128]{1,0:T(8,128)S(1)}, u32[]{:S(2)}, u32[]{:S(2)}) collective-permute-start(f32[280,128]{1,0:T(8,128)S(1)} %get-tuple-element.22), channel_id=1, source_target_pairs={{2,4},{4,2},{3,5},{5,3},{10,12},{12,10},{11,13},{13,11},{18,20},{2... | collective-permute-start | bytes 430088 | tf_op jit(solution)/shard_map/ppermute | solution.py:672
  10.2 4.1 %copy-start.1 = (f32[384,128]{1,0:T(8,128)S(1)}, f32[384,128]{1,0:T(8,128)}, u32[]{:S(2)}) copy-start(f32[384,128]{1,0:T(8,128)} %constant.12.clone.refs_7_.refs_12_) | copy-start | bytes 589828
  10.2 4.1 %copy-start.4 = (f32[8,384]{1,0:T(8,128)S(1)}, f32[8,384]{1,0:T(8,128)}, u32[]{:S(2)}) copy-start(f32[8,384]{1,0:T(8,128)} %constant.13.clone.refs_8_.refs_13_) | copy-start | bytes 36868
  10.2 5.6 %collective-permute-start.3 = (f32[64,128]{1,0:T(8,128)S(1)}, f32[64,128]{1,0:T(8,128)S(1)}, u32[]{:S(2)}, u32[]{:S(2)}) collective-permute-start(f32[64,128]{1,0:T(8,128)S(1)} %get-tuple-element.26.refs_3_), channel_id=1, source_target_pairs={{0,1},{1,0},{8,9},{9,8},{16,17},{17,16},{24,25},{25,24},{2,3},{3,2... | collective-permute-start | bytes 98312 | tf_op jit(solution)/shard_map/ppermute | solution.py:687
  10.3 5.5 %collective-permute-start.4 = (f32[64,128]{1,0:T(8,128)S(1)}, f32[64,128]{1,0:T(8,128)S(1)}, u32[]{:S(2)}, u32[]{:S(2)}) collective-permute-start(f32[64,128]{1,0:T(8,128)S(1)} %get-tuple-element.27.refs_4_), channel_id=1, source_target_pairs={{0,25},{1,8},{8,1},{9,16},{16,9},{17,24},{24,17},{25,0},{2,27},{3,... | collective-permute-start | bytes 98312 | tf_op jit(solution)/shard_map/ppermute | solution.py:688
  13.6 2.2 %collective-permute-start.5 = (f32[112,128]{1,0:T(8,128)S(1)}, f32[112,128]{1,0:T(8,128)S(1)}, u32[]{:S(2)}, u32[]{:S(2)}) collective-permute-start(f32[112,128]{1,0:T(8,128)S(1)} %get-tuple-element.28.refs_5_), channel_id=1, source_target_pairs={{0,1},{1,0},{8,9},{9,8},{16,17},{17,16},{24,25},{25,24},{2,3},{3,2... | collective-permute-start | bytes 172040 | tf_op jit(solution)/shard_map/ppermute | solution.py:711
  13.6 4.8 %collective-permute-start.6 = (f32[112,128]{1,0:T(8,128)S(1)}, f32[112,128]{1,0:T(8,128)S(1)}, u32[]{:S(2)}, u32[]{:S(2)}) collective-permute-start(f32[112,128]{1,0:T(8,128)S(1)} %get-tuple-element.29.refs_6_), channel_id=1, source_target_pairs={{0,25},{1,8},{8,1},{9,16},{16,9},{17,24},{24,17},{25,0},{2,27},{3,... | collective-permute-start | bytes 172040 | tf_op jit(solution)/shard_map/ppermute | solution.py:712
